TPU v7x, 32 devices: a whole 2x2x4 slice. The times are simulated.
32 devices in a mesh: req: 4 (over z), exp: 8 (over y, x, core).
Axes of the slice: x: 2, y: 2, z: 4, core: 2. Of those that a mesh axis runs over, the one named last changes fastest.
Arguments:
- queries: bfloat16 [512, 9216], P('req', 'exp'), may hold values from -8 to 8
- new_latent: bfloat16 [512, 576], P('req'), may hold values from -6 to 6
- pool: bfloat16 [128, 36864], P('req'), may hold values from -5 to 5
- page_list: int32 [8, 16], replicated, may hold values from 0 to 127, as said below
- prefix_len: int32 [8], replicated, may hold values from 1 to 1024, as said below
- hidden_in: bfloat16 [512, 7168], P(('req', 'exp')), may hold values from -6 to 6
- norm_gain: bfloat16 [7168], replicated, may hold values from 0.5 to 1.5
- uv_weight: bfloat16 [16, 512, 128], P('exp'), may hold values from -0.25 to 0.25
- out_weight: bfloat16 [2048, 7168], P('exp', 'req'), may hold values from -1 to 1
- route_ids: int32 [512, 8], P('req'), may hold values from 0 to 7, all different within a row; in each aligned block of 128 rows (0 to 127, 128 to 255, ...) at most 128 rows name the same one
- route_weight: float32 [512, 8], P('req'), may hold values from 0.05 to 0.6
- gate_weight: bfloat16 [8, 7168, 2048], P('exp', None, 'req'), may hold values from -0.0625 to 0.0625
- up_weight: bfloat16 [8, 7168, 2048], P('exp', None, 'req'), may hold values from -0.0625 to 0.0625
- down_weight: bfloat16 [8, 2048, 7168], P('exp', 'req'), may hold values from -0.125 to 0.125
Outputs:
- mixed: bfloat16 [512, 7168], P(('req', 'exp'))
Inputs may be any that keep to these rules, and one draw needn't show every extreme that they name: `page_list`: pool row p is held by req index p // 32. The page at position j of a list lies at depth j of a radix tree with ids j * 8 to j * 8 + 7 at that depth; two lists that share the page at position j share all earlier positions. Counting only positions j < ceil(prefix_len / 64), the 2 requests of one req index (rows r * 2 onward) need at most 8 distinct pages held by one req index, and some req index needs exactly 8 from some holder. `prefix_len`: every request has at least one cached token; some req index has all its requests at the full 16 * 64 cached tokens. `route_ids`: in each block of 128 rows (the tokens of one req index) no expert is named by more than 128 rows, a bound that some block reaches.
All inputs are finite; a program needn't handle non-finite values.
Results may differ from a plain program's by a relative error of at most 0.023.
Values may be sent and summed in bfloat16 or wider, within the bound.
No kernel may reach another device: no remote copies, remote signals or barrier semaphores. Data moves between devices by JAX's collectives and lax.ppermute only.
A program may use at most 64 MiB of HBM per device.

v0:
```python
import functools

import jax
import jax.numpy as jnp
import numpy as np
from jax import lax
from jax.experimental import pallas as pl
from jax.experimental.pallas import tpu as pltpu
from jax.sharding import PartitionSpec as P

score_scale = 192.0 ** (-0.5)
norm_eps = 1e-06
chunk_count = 2


def swap(x, axis, distance):
    size = lax.axis_size(axis)
    return lax.ppermute(x, axis, [(i, i ^ distance) for i in range(size)])


def pick_kernel(plan, place, lists, pool, *outs):
    req_count, per_index, depth_here, pool_rows, width, far_width, far_split, near_split = plan
    slots = per_index * depth_here
    req_index, exp_index = place[0], place[1]
    row = lax.broadcasted_iota(jnp.int32, (16, pool_rows), 0)
    column = lax.broadcasted_iota(jnp.int32, (16, pool_rows), 1)

    def wanted(target):
        hot = row < 0
        for slot in range(slots):
            request, depth = slot // depth_here, slot % depth_here
            page = lists[target * per_index + request, req_index * depth_here + depth]
            hot = hot | ((row == slot) & (column == page - req_index * pool_rows))
        return hot.astype(jnp.float32)

    def lay(hot, start, split, piece):
        total = jnp.zeros((16, piece), jnp.float32)
        for part in range(split):
            shifted = hot if part == 0 else pltpu.roll(hot, part * slots, 0)
            cols = pl.ds(pl.multiple_of(start + part * piece, 128), piece)
            total = total + jnp.dot(
                shifted.astype(jnp.bfloat16), pool[:, cols], preferred_element_type=jnp.float32
            )
        return total.astype(jnp.bfloat16)

    for out, j in zip(outs, range(1, req_count)):
        out[...] = lay(
            wanted(req_index ^ j), exp_index * far_width, far_split, far_width // far_split
        )


def near_kernel(plan, place, lists, pool, out):
    req_count, per_index, depth_here, pool_rows, width, far_width, far_split, near_split = plan
    slots = per_index * depth_here
    req_index = place[0]
    row = lax.broadcasted_iota(jnp.int32, (16, pool_rows), 0)
    column = lax.broadcasted_iota(jnp.int32, (16, pool_rows), 1)
    hots = [row < 0] * near_split
    for slot in range(slots):
        request, depth = slot // depth_here, slot % depth_here
        page = lists[req_index * per_index + request, req_index * depth_here + depth]
        here = column == page - req_index * pool_rows
        for part in range(near_split):
            hots[part] = hots[part] | ((row == part * slots + slot) & here)
    hots = [hot.astype(jnp.float32).astype(jnp.bfloat16) for hot in hots]
    piece = width // near_split
    step = 1152
    for start in range(0, piece, step):
        total = jnp.zeros((16, step), jnp.float32)
        for part in range(near_split):
            cols = slice(part * piece + start, part * piece + start + step)
            total = total + jnp.dot(hots[part], pool[:, cols], preferred_element_type=jnp.float32)
        out[:, start : start + step] = total.astype(jnp.bfloat16)


def attention_kernel(
    plan, place, near, far, new, q_even, q_odd, bias_even, bias_odd, bias_new, uv, out,
    k_even, k_odd, s_even, s_odd, heads,
):
    per_index, latent, kv_rank, head_here, tok_rows, order, sub_rows, chunks = plan
    pair = 2 * latent
    window = latent + 64
    lead = pair - window
    units, far_rows, far_width = far.shape
    near_rows = near.shape[0]
    base = 0

    def place_keys(rows, value_of, pairs, base):
        for p in range(pairs):
            k_even[base : base + rows, :] = value_of(p * pair, p * pair + window)
            k_odd[base : base + rows, :] = value_of(p * pair + lead, (p + 1) * pair)
            base += rows
        return base

    base = place_keys(near_rows, lambda a, b: near[:, a:b], near.shape[1] // pair, base)
    for m in range(units):
        base = place_keys(far_rows, lambda a, b: far[m, :, a:b], far_width // pair, base)
    rows_k = (((1,), (1,)), ((), ()))

    def times(a, b):
        return lax.dot_general(a, b, rows_k, preferred_element_type=jnp.float32) * score_scale

    s_even[...] = times(q_even[...], k_even[...])
    s_odd[...] = times(q_odd[...], k_odd[...])
    s_new = times(q_even[...], new[...])
    new_count = tok_rows // per_index
    p_even, p_odd, p_new = [], [], []
    for h in range(head_here):
        for i in range(per_index):
            at = h * tok_rows + i * new_count
            rows = slice(at, at + new_count)
            even = s_even[rows, :] + bias_even[i : i + 1, :]
            odd = s_odd[rows, :] + bias_odd[i : i + 1, :]
            fresh = s_new[rows, :] + bias_new[i * new_count : (i + 1) * new_count, :]
            top = jnp.maximum(
                jnp.max(jnp.maximum(even, odd), axis=-1, keepdims=True),
                jnp.max(fresh, axis=-1, keepdims=True),
            )
            even, odd, fresh = jnp.exp(even - top), jnp.exp(odd - top), jnp.exp(fresh - top)
            share = 1.0 / (
                jnp.sum(even + odd, axis=-1, keepdims=True)
                + jnp.sum(fresh, axis=-1, keepdims=True)
            )
            p_even.append((even * share).astype(jnp.bfloat16))
            p_odd.append((odd * share).astype(jnp.bfloat16))
            p_new.append((fresh * share).astype(jnp.bfloat16))
    p_even, p_odd, p_new = (jnp.concatenate(p, axis=0) for p in (p_even, p_odd, p_new))
    first = jnp.dot(p_even, k_even[:, :kv_rank], preferred_element_type=jnp.float32)
    second = jnp.dot(p_odd, k_odd[...], preferred_element_type=jnp.float32)
    third = jnp.dot(p_new, new[:, :kv_rank], preferred_element_type=jnp.float32)
    latent_out = (first + third + second[:, 64 : 64 + kv_rank]).astype(jnp.bfloat16)
    value_width = uv.shape[2]
    for h in range(head_here):
        heads[:, h * value_width : (h + 1) * value_width] = jnp.dot(
            latent_out[h * tok_rows : (h + 1) * tok_rows],
            uv[h],
            preferred_element_type=jnp.float32,
        )
    if sub_rows % 8:
        out[...] = heads[...].astype(jnp.bfloat16)
        return
    exp_index = place[1]
    blocks = []
    for m in order:
        for c in range(chunks):
            at = ((exp_index ^ m) * chunks + c) * sub_rows
            blocks.append(heads[pl.ds(pl.multiple_of(at, 8), sub_rows), :])
    out[...] = jnp.concatenate(blocks, axis=0).astype(jnp.bfloat16)


def local(
    queries,
    new_latent,
    pool,
    page_list,
    prefix_len,
    hidden_in,
    norm_gain,
    uv_weight,
    out_weight,
    route_ids,
    route_weight,
    gate_weight,
    up_weight,
    down_weight,
):
    req_count = lax.axis_size("req")
    exp_count = lax.axis_size("exp")
    req_index = lax.axis_index("req")
    exp_index = lax.axis_index("exp")
    tok_rows = queries.shape[0]
    latent = new_latent.shape[1]
    kv_rank = uv_weight.shape[1]
    value_width = uv_weight.shape[2]
    head_here = uv_weight.shape[0]
    pool_rows = pool.shape[0]
    page_size = pool.shape[1] // latent
    list_depth = page_list.shape[1]
    per_index = page_list.shape[0] // req_count
    depth_here = list_depth // req_count
    width = hidden_in.shape[1]
    col_width = width // req_count
    half_width = width // 2
    own_rows = tok_rows // exp_count
    sub_rows = own_rows // chunk_count
    outer = exp_count // 2
    req_rel = req_index ^ jnp.arange(req_count, dtype=jnp.int32)
    rel_order = [2 * k for k in range(outer)] + [2 * k + 1 for k in range(outer)]
    exp_rel = exp_index ^ jnp.array(rel_order, dtype=jnp.int32)

    slots = per_index * depth_here
    pair = 2 * latent
    pool_width = pool.shape[1]
    far_width = pool_width // exp_count
    far_split = min(16 // slots, far_width // pair)
    near_split = 16 // slots
    lengths = prefix_len.reshape(req_count, per_index)
    place = jnp.stack([req_index, exp_index]).astype(jnp.int32)
    plan = (
        req_count, per_index, depth_here, pool_rows, pool_width, far_width, far_split, near_split,
    )
    scalars = pl.BlockSpec(memory_space=pltpu.SMEM)
    whole = pl.BlockSpec(memory_space=pltpu.VMEM)
    far_shape = jax.ShapeDtypeStruct((16, far_width // far_split), jnp.bfloat16)
    sent = pl.pallas_call(
        functools.partial(pick_kernel, plan),
        out_shape=[far_shape] * (req_count - 1),
        in_specs=[scalars, scalars, whole],
        out_specs=[whole] * (req_count - 1),
        name="pick_far",
    )(place, page_list, pool)
    near = pl.pallas_call(
        functools.partial(near_kernel, plan),
        out_shape=jax.ShapeDtypeStruct((16, pool_width // near_split), jnp.bfloat16),
        in_specs=[scalars, scalars, whole],
        out_specs=whole,
        name="pick_near",
    )(place, page_list, pool)
    far = jnp.concatenate([swap(sent[j - 1], "req", j) for j in range(1, req_count)], axis=0)
    far_out = jnp.stack([far] + [swap(far, "exp", 2 * k) for k in range(1, outer)])
    far_all = jnp.concatenate([far_out, swap(far_out, "exp", 1)], axis=0)

    def positions(tokens, holder_ids, split, slot_row):
        depth = holder_ids * depth_here + slot_row % slots % depth_here
        return jnp.where(slot_row < slots * split, depth * page_size + tokens, list_depth * page_size)

    near_piece = page_size // near_split
    pairs = np.arange(near_piece // 2)[:, None]
    slot_row = np.arange(16)[None, :]
    near_pos = positions(slot_row // slots * near_piece + 2 * pairs, req_index, near_split, slot_row)
    near_req = np.broadcast_to(slot_row % slots // depth_here, near_pos.shape)
    far_tokens = page_size // exp_count
    far_piece = far_tokens // far_split
    pairs = np.arange(far_piece // 2).reshape(1, -1, 1, 1)
    slot_row = np.arange(16).reshape(1, 1, 1, -1)
    far_pos = positions(
        exp_rel.reshape(-1, 1, 1, 1) * far_tokens + slot_row // slots * far_piece + 2 * pairs,
        req_rel[1:].reshape(1, 1, -1, 1),
        far_split,
        slot_row,
    )
    far_req = np.broadcast_to(slot_row % slots // depth_here, far_pos.shape)
    key_pos = jnp.concatenate([near_pos.reshape(1, -1), far_pos.reshape(1, -1)], axis=1)
    key_req = np.concatenate([near_req.reshape(1, -1), far_req.reshape(1, -1)], axis=1)
    my_lengths = lax.dynamic_index_in_dim(lengths, req_index, 0, keepdims=False)[:, None]
    same = key_req == np.arange(per_index)[:, None]
    bias_even = jnp.where(same & (key_pos < my_lengths), 0.0, -1e30)
    bias_odd = jnp.where(same & (key_pos + 1 < my_lengths), 0.0, -1e30)
    new_count = tok_rows // per_index
    tok = np.arange(tok_rows)
    seen = (tok[:, None] // new_count == tok // new_count) & (tok <= tok[:, None])
    bias_new = jnp.asarray(np.where(seen, 0.0, -1e30), jnp.float32)
    by_head = queries.reshape(tok_rows, head_here, latent).transpose(1, 0, 2)
    by_head = by_head.reshape(head_here * tok_rows, latent)
    q_even = jnp.pad(by_head, ((0, 0), (0, 64)))
    q_odd = jnp.pad(by_head, ((0, 0), (64, 0)))
    new_keys = jnp.pad(new_latent, ((0, 0), (0, 64)))
    key_count = key_req.shape[1]
    q_rows = head_here * tok_rows
    head_cols = head_here * value_width
    head_out = pl.pallas_call(
        functools.partial(
            attention_kernel,
            (
                per_index, latent, kv_rank, head_here, tok_rows, tuple(rel_order), sub_rows,
                chunk_count,
            ),
        ),
        out_shape=jax.ShapeDtypeStruct((tok_rows, head_cols), jnp.bfloat16),
        in_specs=[scalars] + [whole] * 9,
        out_specs=whole,
        scratch_shapes=[
            pltpu.VMEM((key_count, latent + 64), jnp.bfloat16),
            pltpu.VMEM((key_count, latent + 64), jnp.bfloat16),
            pltpu.VMEM((q_rows, key_count), jnp.float32),
            pltpu.VMEM((q_rows, key_count), jnp.float32),
            pltpu.VMEM((tok_rows, head_cols), jnp.float32),
        ],
        compiler_params=pltpu.CompilerParams(vmem_limit_bytes=40 * 1024 * 1024),
        name="attention",
    )(place, near, far_all, new_keys, q_even, q_odd, bias_even, bias_odd, bias_new, uv_weight)
    head_out = head_out.reshape(exp_count, chunk_count, sub_rows, head_cols)
    if sub_rows % 8:
        head_out = head_out[exp_rel]

    chosen = route_ids == exp_index
    token_weight = jnp.sum(jnp.where(chosen, route_weight, 0.0), axis=1)
    token_weight = token_weight.reshape(exp_count, chunk_count, sub_rows)[exp_rel]
    weight_all = jnp.stack(
        [token_weight] + [swap(token_weight, "req", j) for j in range(1, req_count)]
    ).transpose(2, 1, 0, 3)

    hidden_cols = []
    for j in range(req_count):
        piece = lax.dynamic_slice_in_dim(hidden_in, req_rel[j] * col_width, col_width, 1)
        hidden_cols.append(piece if j == 0 else swap(piece, "req", j))
    hidden_cols = jnp.stack(hidden_cols).reshape(req_count, chunk_count, sub_rows, col_width)
    hidden_cols = hidden_cols.transpose(1, 0, 2, 3)

    heads_all = jnp.stack(
        [head_out] + [swap(head_out, "req", j) for j in range(1, req_count)], axis=2
    )
    block = req_count * sub_rows
    own_block = chunk_count * block
    partial = jnp.dot(
        heads_all.reshape(exp_count * own_block, head_cols),
        out_weight,
        preferred_element_type=jnp.float32,
    )
    cut = outer * own_block
    other = swap(partial[cut:].astype(jnp.bfloat16), "exp", 1)
    pair_sum = (partial[:cut] + other.astype(jnp.float32)).reshape(outer, own_block, col_width)
    attn = pair_sum[0]
    for k in range(1, outer):
        attn = attn + swap(pair_sum[k].astype(jnp.bfloat16), "exp", 2 * k).astype(jnp.float32)
    attn = attn.reshape(chunk_count, req_count, sub_rows, col_width)
    resid_cols = (hidden_cols.astype(jnp.float32) + attn).astype(jnp.bfloat16)

    def gather_columns(resid):
        slices = [resid]
        for j in range(1, req_count):
            got = swap(resid, "req", j)
            slices.append(jnp.stack([got[i ^ j] for i in range(req_count)]))
        ordered = jnp.stack(slices)[req_rel]
        return ordered.transpose(1, 2, 0, 3).reshape(block, width)

    def normalise(full):
        widened = full.astype(jnp.float32)
        inv_scale = lax.rsqrt(jnp.mean(widened * widened, axis=-1, keepdims=True) + norm_eps)
        return (widened * inv_scale * norm_gain.astype(jnp.float32)).astype(jnp.bfloat16)

    outer_bits = []
    bit = 1
    while bit < outer:
        outer_bits.append(bit)
        bit *= 2
    sides = (outer_bits, outer_bits[::-1])

    def gather_plane(piece, bits):
        held = piece[None]
        ids = [0]
        for bit in bits:
            held = jnp.concatenate([held, swap(held, "exp", 2 * bit)], axis=0)
            ids = ids + [k ^ bit for k in ids]
        back = [ids.index(k) for k in range(outer)]
        other = swap(held, "exp", 1)
        picks = [held[k] for k in back] + [other[k] for k in back]
        return jnp.concatenate(picks, axis=0)

    def scatter_plane(partial, bits):
        cut = outer * block
        other = swap(partial[cut:].astype(jnp.bfloat16), "exp", 1)
        held = (partial[:cut] + other.astype(jnp.float32)).reshape(outer, block, half_width)
        ids = list(range(outer))
        for bit in bits:
            keep = [n for n, k in enumerate(ids) if not k & bit]
            give = [ids.index(ids[n] ^ bit) for n in keep]
            sent = jnp.stack([held[n] for n in give]).astype(jnp.bfloat16)
            held = jnp.stack([held[n] for n in keep]) + swap(sent, "exp", 2 * bit).astype(
                jnp.float32
            )
            ids = [ids[n] for n in keep]
        return held[0].astype(jnp.bfloat16)

    gate_here = gate_weight[0]
    up_here = up_weight[0]
    down_here = down_weight[0]

    def experts(left, right, weights):
        def project(matrix):
            return jnp.dot(
                left, matrix[:half_width], preferred_element_type=jnp.float32
            ) + jnp.dot(right, matrix[half_width:], preferred_element_type=jnp.float32)

        active = (jax.nn.silu(project(gate_here)) * project(up_here)).astype(jnp.bfloat16)
        outs = []
        for matrix in (down_here[:, :half_width], down_here[:, half_width:]):
            out = jnp.dot(active, matrix, preferred_element_type=jnp.float32)
            outs.append(out * weights[:, None])
        return outs

    results = []
    for c in range(chunk_count):
        full = gather_columns(resid_cols[c])
        normed = normalise(full)
        rows = [
            gather_plane(normed[:, n * half_width : (n + 1) * half_width], sides[n])
            for n in range(2)
        ]
        outs = experts(rows[0], rows[1], weight_all[c].reshape(-1))
        sums = jnp.concatenate([scatter_plane(outs[n], sides[n]) for n in range(2)], axis=1)
        sums = sums.reshape(req_count, sub_rows, width)
        total = full[:sub_rows].astype(jnp.float32) + sums[0].astype(jnp.float32)
        for j in range(1, req_count):
            total = total + swap(sums[j], "req", j).astype(jnp.float32)
        results.append(total.astype(jnp.bfloat16))
    return jnp.concatenate(results, axis=0)


def solution(mesh):
    return jax.shard_map(
        local,
        mesh=mesh,
        in_specs=(
            P("req", "exp"),
            P("req", None),
            P("req", None),
            P(),
            P(),
            P(("req", "exp"), None),
            P(),
            P("exp", None, None),
            P("exp", "req"),
            P("req", None),
            P("req", None),
            P("exp", None, "req"),
            P("exp", None, "req"),
            P("exp", "req", None),
        ),
        out_specs=P(("req", "exp"), None),
        check_vma=False,
    )
```

profile of v0, /device:TPU:0, one launch (start us, length us, event | category | flops | bytes accessed | tf_op | source)
XLA Modules:
  0.0 198.1 jit_solution(17513316361771067369)
XLA Ops:
  0.7 2.6 %pick_far.1 = (bf16[16,2304]{1,0:T(8,128)(2,1)}, bf16[16,2304]{1,0:T(8,128)(2,1)}, bf16[16,2304]{1,0:T(8,128)(2,1)}) custom-call(s32[2]{0:T(128)} %pad_add_fusion.1.place, s32[8,16]{1,0:T(8,128)} %lists.3, bf16[32,36864]{1,0:T(8,128)(2,1)} %pool.3), custom_call_target="tpu_custom_call" | custom-call | tf_op jit(solution)/shard_map/pick_far/pallas_call | solution.py:205
  3.3 3.1 %collective-permute-start.3 = (bf16[16,2304]{1,0:T(8,128)(2,1)}, bf16[16,2304]{1,0:T(8,128)(2,1)S(1)}, u32[]{:S(2)}, u32[]{:S(2)}) collective-permute-start(bf16[16,2304]{1,0:T(8,128)(2,1)} %get-tuple-element.8), channel_id=1, source_target_pairs={{0,8},{8,0},{16,24},{24,16},{1,9},{9,1},{17,25},{25,17},{2,10},{10... | collective-permute-start | bytes 221192 | tf_op jit(solution)/shard_map/ppermute | solution.py:18
  6.4 2.6 %collective-permute-start.4 = (bf16[16,2304]{1,0:T(8,128)(2,1)}, bf16[16,2304]{1,0:T(8,128)(2,1)S(1)}, u32[]{:S(2)}, u32[]{:S(2)}) collective-permute-start(bf16[16,2304]{1,0:T(8,128)(2,1)} %get-tuple-element.9), channel_id=1, source_target_pairs={{0,16},{8,24},{16,0},{24,8},{1,17},{9,25},{17,1},{25,9},{2,18},{10... | collective-permute-start | bytes 221192 | tf_op jit(solution)/shard_map/ppermute | solution.py:18
  9.7 3.0 %pick_near.1.near = bf16[16,18432]{1,0:T(8,128)(2,1)} custom-call(s32[2]{0:T(128)} %pad_add_fusion.1.place, s32[8,16]{1,0:T(8,128)} %lists.3, bf16[32,36864]{1,0:T(8,128)(2,1)} %pool.3), custom_call_target="tpu_custom_call" | custom-call | tf_op jit(solution)/shard_map/pick_near/pallas_call | solution.py:212
  15.5 2.4 %collective-permute-start.8 = (bf16[48,2304]{1,0:T(8,128)(2,1)S(1)}, bf16[48,2304]{1,0:T(8,128)(2,1)S(1)}, u32[]{:S(2)}, u32[]{:S(2)}) collective-permute-start(bf16[48,2304]{1,0:T(8,128)(2,1)S(1)} %constant_dynamic-update-slice_fusion), channel_id=1, source_target_pairs={{0,6},{1,7},{2,4},{3,5},{4,2},{5,3},{6,0},{7,1},{8,14},{9,15},{10,... | collective-permute-start | bytes 663560 | tf_op jit(solution)/shard_map/ppermute | solution.py:18
  19.0 5.2 %collective-permute-done.8 = bf16[48,2304]{1,0:T(8,128)(2,1)S(1)} collective-permute-done((bf16[48,2304]{1,0:T(8,128)(2,1)S(1)}, bf16[48,2304]{1,0:T(8,128)(2,1)S(1)}, u32[]{:S(2)}, u32[]{:S(2)}) %collective-permute-start.8) | collective-permute-done | bytes 221216 | tf_op jit(solution)/shard_map/ppermute | solution.py:18
  24.2 2.2 %collective-permute-done.7 = bf16[48,2304]{1,0:T(8,128)(2,1)S(1)} collective-permute-done((bf16[48,2304]{1,0:T(8,128)(2,1)S(1)}, bf16[48,2304]{1,0:T(8,128)(2,1)S(1)}, u32[]{:S(2)}, u32[]{:S(2)}) %collective-permute-start.7) | collective-permute-done | bytes 221216 | tf_op jit(solution)/shard_map/ppermute | solution.py:18
  26.9 2.3 %collective-permute-done.9 = bf16[4,48,2304]{2,1,0:T(8,128)(2,1)S(1)} collective-permute-done((bf16[4,48,2304]{2,1,0:T(8,128)(2,1)S(1)}, bf16[4,48,2304]{2,1,0:T(8,128)(2,1)S(1)}, u32[]{:S(2)}, u32[]{:S(2)}) %collective-permute-start.9) | collective-permute-done | bytes 884768 | tf_op jit(solution)/shard_map/ppermute | solution.py:18
  29.3 3.2 %attention.1 = bf16[128,256]{1,0:T(8,128)(2,1)S(1)} custom-call(s32[2]{0:T(128)S(1)} %copy-done.5, bf16[16,18432]{1,0:T(8,128)(2,1)S(1)} %copy-done.2, bf16[8,48,2304]{2,1,0:T(8,128)(2,1)S(1)} %constant_dynamic-update-slice_fusion.3.far, bf16[128,640]{1,0:T(8,128)(2,1)S(1)} %pad.12.new, bf16[256,640]{1,0:T(8,128)(2,1)S(1)} %get-tuple-element.55.q_even, ...), custom_call_target="tpu_custom_call" | custom-call | tf_op jit(solution)/shard_map/attention/pallas_call | solution.py:261
  32.5 3.3 %collective-permute-start.12 = (bf16[8,2,8,256]{3,2,1,0:T(8,128)(2,1)S(1)}, bf16[8,2,8,256]{3,2,1,0:T(8,128)(2,1)S(1)}, u32[]{:S(2)}, u32[]{:S(2)}) collective-permute-start(bf16[8,2,8,256]{3,2,1,0:T(8,128)(2,1)S(1)} %bitcast.296), channel_id=1, source_target_pairs={{0,24},{8,16},{16,8},{24,0},{1,25},{9,17},{17,9},{25,1},{2,26},{10... | collective-permute-start | bytes 196616 | tf_op jit(solution)/shard_map/ppermute | solution.py:18
  38.7 3.2 %collective-permute-done.11 = bf16[8,2,8,256]{3,2,1,0:T(8,128)(2,1)S(1)} collective-permute-done((bf16[8,2,8,256]{3,2,1,0:T(8,128)(2,1)S(1)}, bf16[8,2,8,256]{3,2,1,0:T(8,128)(2,1)S(1)}, u32[]{:S(2)}, u32[]{:S(2)}) %collective-permute-start.11) | collective-permute-done | bytes 65568 | tf_op jit(solution)/shard_map/ppermute | solution.py:18
  42.6 1.8 copy-done.6
  47.1 2.2 %collective-permute-start.26 = (f32[8,2,8]{2,1,0:T(2,128)S(1)}, f32[8,2,8]{2,1,0:T(2,128)S(1)}, u32[]{:S(2)}, u32[]{:S(2)}) collective-permute-start(f32[8,2,8]{2,1,0:T(2,128)S(1)} %gather_fusion.1), channel_id=1, source_target_pairs={{0,8},{8,0},{16,24},{24,16},{1,9},{9,1},{17,25},{25,17},{2,10},{10... | collective-permute-start | bytes 1544 | tf_op jit(solution)/shard_map/ppermute | solution.py:18
  59.2 4.2 %collective-permute-done.28 = f32[8,2,8]{2,1,0:T(2,128)S(1)} collective-permute-done((f32[8,2,8]{2,1,0:T(2,128)S(1)}, f32[8,2,8]{2,1,0:T(2,128)S(1)}, u32[]{:S(2)}, u32[]{:S(2)}) %collective-permute-start.28) | collective-permute-done | bytes 544 | tf_op jit(solution)/shard_map/ppermute | solution.py:18
  64.7 2.5 %collective-permute-done.16 = bf16[64,1792]{1,0:T(8,128)(2,1)S(1)} collective-permute-done((bf16[64,1792]{1,0:T(8,128)(2,1)S(1)}, bf16[64,1792]{1,0:T(8,128)(2,1)S(1)}, u32[]{:S(2)}, u32[]{:S(2)}) %collective-permute-start.16) | collective-permute-done | bytes 229408 | tf_op jit(solution)/shard_map/ppermute | solution.py:18
  69.4 1.8 collective-permute-done.1
  71.3 1.9 collective-permute-start.40
  73.4 2.1 %collective-permute-start.19 = (bf16[4,8,1792]{2,1,0:T(8,128)(2,1)S(1)}, bf16[4,8,1792]{2,1,0:T(8,128)(2,1)S(1)}, u32[]{:S(2)}, u32[]{:S(2)}) collective-permute-start(bf16[4,8,1792]{2,1,0:T(8,128)(2,1)S(1)} %get-tuple-element.57), channel_id=1, source_target_pairs={{0,24},{8,16},{16,8},{24,0},{1,25},{9,17},{17,9},{25,1},{2,26},{10... | collective-permute-start | bytes 344072 | tf_op jit(solution)/shard_map/ppermute | solution.py:18
  75.5 2.4 %collective-permute-start.17 = (bf16[4,8,1792]{2,1,0:T(8,128)(2,1)S(1)}, bf16[4,8,1792]{2,1,0:T(8,128)(2,1)S(1)}, u32[]{:S(2)}, u32[]{:S(2)}) collective-permute-start(bf16[4,8,1792]{2,1,0:T(8,128)(2,1)S(1)} %get-tuple-element.57), channel_id=1, source_target_pairs={{0,8},{8,0},{16,24},{24,16},{1,9},{9,1},{17,25},{25,17},{2,10},{10... | collective-permute-start | bytes 344072 | tf_op jit(solution)/shard_map/ppermute | solution.py:18
  79.3 4.3 %collective-permute-start.38 = (bf16[4,8,1792]{2,1,0:T(8,128)(2,1)S(1)}, bf16[4,8,1792]{2,1,0:T(8,128)(2,1)S(1)}, u32[]{:S(2)}, u32[]{:S(2)}) collective-permute-start(bf16[4,8,1792]{2,1,0:T(8,128)(2,1)S(1)} %get-tuple-element.58), channel_id=1, source_target_pairs={{0,8},{8,0},{16,24},{24,16},{1,9},{9,1},{17,25},{25,17},{2,10},{10... | collective-permute-start | bytes 344072 | tf_op jit(solution)/shard_map/ppermute | solution.py:18
  83.7 6.7 %collective-permute-done.39 = bf16[4,8,1792]{2,1,0:T(8,128)(2,1)S(1)} collective-permute-done((bf16[4,8,1792]{2,1,0:T(8,128)(2,1)S(1)}, bf16[4,8,1792]{2,1,0:T(8,128)(2,1)S(1)}, u32[]{:S(2)}, u32[]{:S(2)}) %collective-permute-start.39) | collective-permute-done | bytes 114720 | tf_op jit(solution)/shard_map/ppermute | solution.py:18
  98.9 4.4 %collective-permute-done.20 = bf16[1,32,3584]{2,1,0:T(8,128)(2,1)S(1)} collective-permute-done((bf16[1,32,3584]{2,1,0:T(8,128)(2,1)S(1)}, bf16[1,32,3584]{2,1,0:T(8,128)(2,1)S(1)}, u32[]{:S(2)}, u32[]{:S(2)}) %collective-permute-start.20) | collective-permute-done | bytes 229408 | tf_op jit(solution)/shard_map/ppermute | solution.py:18
  105.7 2.5 %collective-permute-done.41 = bf16[1,32,3584]{2,1,0:T(8,128)(2,1)S(1)} collective-permute-done((bf16[1,32,3584]{2,1,0:T(8,128)(2,1)S(1)}, bf16[1,32,3584]{2,1,0:T(8,128)(2,1)S(1)}, u32[]{:S(2)}, u32[]{:S(2)}) %collective-permute-start.41) | collective-permute-done | bytes 229408 | tf_op jit(solution)/shard_map/ppermute | solution.py:18
  110.7 7.7 %collective-permute-done.24 = bf16[2,32,3584]{2,1,0:T(8,128)(2,1)S(1)} collective-permute-done((bf16[2,32,3584]{2,1,0:T(8,128)(2,1)S(1)}, bf16[2,32,3584]{2,1,0:T(8,128)(2,1)S(1)}, u32[]{:S(2)}, u32[]{:S(2)}) %collective-permute-start.24) | collective-permute-done | bytes 458784 | tf_op jit(solution)/shard_map/ppermute | solution.py:18
  119.7 5.7 %collective-permute-done.45 = bf16[2,32,3584]{2,1,0:T(8,128)(2,1)S(1)} collective-permute-done((bf16[2,32,3584]{2,1,0:T(8,128)(2,1)S(1)}, bf16[2,32,3584]{2,1,0:T(8,128)(2,1)S(1)}, u32[]{:S(2)}, u32[]{:S(2)}) %collective-permute-start.45) | collective-permute-done | bytes 458784 | tf_op jit(solution)/shard_map/ppermute | solution.py:18
  151.7 7.7 %collective-permute-done.33 = bf16[2,32,3584]{2,1,0:T(8,128)(2,1)S(1)} collective-permute-done((bf16[2,32,3584]{2,1,0:T(8,128)(2,1)S(1)}, bf16[2,32,3584]{2,1,0:T(8,128)(2,1)S(1)}, u32[]{:S(2)}, u32[]{:S(2)}) %collective-permute-start.33) | collective-permute-done | bytes 458784 | tf_op jit(solution)/shard_map/ppermute | solution.py:18
  162.2 7.1 %collective-permute-done.51 = bf16[2,32,3584]{2,1,0:T(8,128)(2,1)S(1)} collective-permute-done((bf16[2,32,3584]{2,1,0:T(8,128)(2,1)S(1)}, bf16[2,32,3584]{2,1,0:T(8,128)(2,1)S(1)}, u32[]{:S(2)}, u32[]{:S(2)}) %collective-permute-start.51) | collective-permute-done | bytes 458784 | tf_op jit(solution)/shard_map/ppermute | solution.py:18
  172.0 4.0 %collective-permute-done.34 = bf16[1,32,3584]{2,1,0:T(8,128)(2,1)S(1)} collective-permute-done((bf16[1,32,3584]{2,1,0:T(8,128)(2,1)S(1)}, bf16[1,32,3584]{2,1,0:T(8,128)(2,1)S(1)}, u32[]{:S(2)}, u32[]{:S(2)}) %collective-permute-start.34) | collective-permute-done | bytes 229408 | tf_op jit(solution)/shard_map/ppermute | solution.py:18
  177.2 2.5 %collective-permute-start.36 = (bf16[8,7168]{1,0:T(8,128)(2,1)S(1)}, bf16[8,7168]{1,0:T(8,128)(2,1)S(1)}, u32[]{:S(2)}, u32[]{:S(2)}) collective-permute-start(bf16[8,7168]{1,0:T(8,128)(2,1)S(1)} %get-tuple-element.42), channel_id=1, source_target_pairs={{0,16},{8,24},{16,0},{24,8},{1,17},{9,25},{17,1},{25,9},{2,18},{10... | collective-permute-start | bytes 344072 | tf_op jit(solution)/shard_map/ppermute | solution.py:18
  181.8 2.5 %collective-permute-done.35 = bf16[8,7168]{1,0:T(8,128)(2,1)S(1)} collective-permute-done((bf16[8,7168]{1,0:T(8,128)(2,1)S(1)}, bf16[8,7168]{1,0:T(8,128)(2,1)S(1)}, u32[]{:S(2)}, u32[]{:S(2)}) %collective-permute-start.35) | collective-permute-done | bytes 114720 | tf_op jit(solution)/shard_map/ppermute | solution.py:18
  184.3 10.0 %collective-permute-done.36 = bf16[8,7168]{1,0:T(8,128)(2,1)S(1)} collective-permute-done((bf16[8,7168]{1,0:T(8,128)(2,1)S(1)}, bf16[8,7168]{1,0:T(8,128)(2,1)S(1)}, u32[]{:S(2)}, u32[]{:S(2)}) %collective-permute-start.36) | collective-permute-done | bytes 114720 | tf_op jit(solution)/shard_map/ppermute | solution.py:18
  194.4 2.8 %collective-permute-done.54 = bf16[8,7168]{1,0:T(8,128)(2,1)S(1)} collective-permute-done((bf16[8,7168]{1,0:T(8,128)(2,1)S(1)}, bf16[8,7168]{1,0:T(8,128)(2,1)S(1)}, u32[]{:S(2)}, u32[]{:S(2)}) %collective-permute-start.54) | collective-permute-done | bytes 114720 | tf_op jit(solution)/shard_map/ppermute | solution.py:18
  (315 shorter events, 73.9 us)
Async XLA Ops:
  3.3 10.5 %collective-permute-start.3 = (bf16[16,2304]{1,0:T(8,128)(2,1)}, bf16[16,2304]{1,0:T(8,128)(2,1)S(1)}, u32[]{:S(2)}, u32[]{:S(2)}) collective-permute-start(bf16[16,2304]{1,0:T(8,128)(2,1)} %get-tuple-element.8), channel_id=1, source_target_pairs={{0,8},{8,0},{16,24},{24,16},{1,9},{9,1},{17,25},{25,17},{2,10},{10... | collective-permute-start | bytes 221192 | tf_op jit(solution)/shard_map/ppermute | solution.py:18
  45.9 12.0 %collective-permute-start.27 = (f32[8,2,8]{2,1,0:T(2,128)S(1)}, f32[8,2,8]{2,1,0:T(2,128)S(1)}, u32[]{:S(2)}, u32[]{:S(2)}) collective-permute-start(f32[8,2,8]{2,1,0:T(2,128)S(1)} %gather_fusion.1), channel_id=1, source_target_pairs={{0,16},{8,24},{16,0},{24,8},{1,17},{9,25},{17,1},{25,9},{2,18},{10... | collective-permute-start | bytes 1544 | tf_op jit(solution)/shard_map/ppermute | solution.py:18
  47.1 12.0 %collective-permute-start.26 = (f32[8,2,8]{2,1,0:T(2,128)S(1)}, f32[8,2,8]{2,1,0:T(2,128)S(1)}, u32[]{:S(2)}, u32[]{:S(2)}) collective-permute-start(f32[8,2,8]{2,1,0:T(2,128)S(1)} %gather_fusion.1), channel_id=1, source_target_pairs={{0,8},{8,0},{16,24},{24,16},{1,9},{9,1},{17,25},{25,17},{2,10},{10... | collective-permute-start | bytes 1544 | tf_op jit(solution)/shard_map/ppermute | solution.py:18
  54.3 10.3 %collective-permute-start.14 = (bf16[64,1792]{1,0:T(8,128)(2,1)S(1)}, bf16[64,1792]{1,0:T(8,128)(2,1)S(1)}, u32[]{:S(2)}, u32[]{:S(2)}) collective-permute-start(bf16[64,1792]{1,0:T(8,128)(2,1)S(1)} %get-tuple-element.37), channel_id=1, source_target_pairs={{0,2},{1,3},{2,0},{3,1},{4,6},{5,7},{6,4},{7,5},{8,10},{9,11},{10,... | collective-permute-start | bytes 688136 | tf_op jit(solution)/shard_map/ppermute | solution.py:18
  55.9 11.3 %collective-permute-start.16 = (bf16[64,1792]{1,0:T(8,128)(2,1)S(1)}, bf16[64,1792]{1,0:T(8,128)(2,1)S(1)}, u32[]{:S(2)}, u32[]{:S(2)}) collective-permute-start(bf16[64,1792]{1,0:T(8,128)(2,1)S(1)} %get-tuple-element.38), channel_id=1, source_target_pairs={{0,6},{1,7},{2,4},{3,5},{4,2},{5,3},{6,0},{7,1},{8,14},{9,15},{10,... | collective-permute-start | bytes 688136 | tf_op jit(solution)/shard_map/ppermute | solution.py:18
  57.3 11.3 %collective-permute-start.15 = (bf16[64,1792]{1,0:T(8,128)(2,1)S(1)}, bf16[64,1792]{1,0:T(8,128)(2,1)S(1)}, u32[]{:S(2)}, u32[]{:S(2)}) collective-permute-start(bf16[64,1792]{1,0:T(8,128)(2,1)S(1)} %get-tuple-element.39), channel_id=1, source_target_pairs={{0,4},{1,5},{2,6},{3,7},{4,0},{5,1},{6,2},{7,3},{8,12},{9,13},{10,... | collective-permute-start | bytes 688136 | tf_op jit(solution)/shard_map/ppermute | solution.py:18
  73.4 17.9 %collective-permute-start.19 = (bf16[4,8,1792]{2,1,0:T(8,128)(2,1)S(1)}, bf16[4,8,1792]{2,1,0:T(8,128)(2,1)S(1)}, u32[]{:S(2)}, u32[]{:S(2)}) collective-permute-start(bf16[4,8,1792]{2,1,0:T(8,128)(2,1)S(1)} %get-tuple-element.57), channel_id=1, source_target_pairs={{0,24},{8,16},{16,8},{24,0},{1,25},{9,17},{17,9},{25,1},{2,26},{10... | collective-permute-start | bytes 344072 | tf_op jit(solution)/shard_map/ppermute | solution.py:18
  75.5 15.9 %collective-permute-start.18 = (bf16[4,8,1792]{2,1,0:T(8,128)(2,1)S(1)}, bf16[4,8,1792]{2,1,0:T(8,128)(2,1)S(1)}, u32[]{:S(2)}, u32[]{:S(2)}) collective-permute-start(bf16[4,8,1792]{2,1,0:T(8,128)(2,1)S(1)} %get-tuple-element.57), channel_id=1, source_target_pairs={{0,16},{8,24},{16,0},{24,8},{1,17},{9,25},{17,1},{25,9},{2,18},{10... | collective-permute-start | bytes 344072 | tf_op jit(solution)/shard_map/ppermute | solution.py:18
  75.5 16.1 %collective-permute-start.17 = (bf16[4,8,1792]{2,1,0:T(8,128)(2,1)S(1)}, bf16[4,8,1792]{2,1,0:T(8,128)(2,1)S(1)}, u32[]{:S(2)}, u32[]{:S(2)}) collective-permute-start(bf16[4,8,1792]{2,1,0:T(8,128)(2,1)S(1)} %get-tuple-element.57), channel_id=1, source_target_pairs={{0,8},{8,0},{16,24},{24,16},{1,9},{9,1},{17,25},{25,17},{2,10},{10... | collective-permute-start | bytes 344072 | tf_op jit(solution)/shard_map/ppermute | solution.py:18
  77.9 12.5 %collective-permute-start.39 = (bf16[4,8,1792]{2,1,0:T(8,128)(2,1)S(1)}, bf16[4,8,1792]{2,1,0:T(8,128)(2,1)S(1)}, u32[]{:S(2)}, u32[]{:S(2)}) collective-permute-start(bf16[4,8,1792]{2,1,0:T(8,128)(2,1)S(1)} %get-tuple-element.58), channel_id=1, source_target_pairs={{0,16},{8,24},{16,0},{24,8},{1,17},{9,25},{17,1},{25,9},{2,18},{10... | collective-permute-start | bytes 344072 | tf_op jit(solution)/shard_map/ppermute | solution.py:18
  79.3 11.2 %collective-permute-start.38 = (bf16[4,8,1792]{2,1,0:T(8,128)(2,1)S(1)}, bf16[4,8,1792]{2,1,0:T(8,128)(2,1)S(1)}, u32[]{:S(2)}, u32[]{:S(2)}) collective-permute-start(bf16[4,8,1792]{2,1,0:T(8,128)(2,1)S(1)} %get-tuple-element.58), channel_id=1, source_target_pairs={{0,8},{8,0},{16,24},{24,16},{1,9},{9,1},{17,25},{25,17},{2,10},{10... | collective-permute-start | bytes 344072 | tf_op jit(solution)/shard_map/ppermute | solution.py:18
  97.0 11.2 %collective-permute-start.41 = (bf16[1,32,3584]{2,1,0:T(8,128)(2,1)S(1)}, bf16[1,32,3584]{2,1,0:T(8,128)(2,1)S(1)}, u32[]{:S(2)}, u32[]{:S(2)}) collective-permute-start(bf16[1,32,3584]{2,1,0:T(8,128)(2,1)S(1)} %get-tuple-element.50), channel_id=1, source_target_pairs={{0,2},{1,3},{2,0},{3,1},{4,6},{5,7},{6,4},{7,5},{8,10},{9,11},{10,... | collective-permute-start | bytes 688136 | tf_op jit(solution)/shard_map/ppermute | solution.py:18
  98.3 11.4 %collective-permute-start.44 = (bf16[1,32,3584]{2,1,0:T(8,128)(2,1)S(1)}, bf16[1,32,3584]{2,1,0:T(8,128)(2,1)S(1)}, u32[]{:S(2)}, u32[]{:S(2)}) collective-permute-start(bf16[1,32,3584]{2,1,0:T(8,128)(2,1)S(1)} %get-tuple-element.53), channel_id=1, source_target_pairs={{0,4},{1,5},{2,6},{3,7},{4,0},{5,1},{6,2},{7,3},{8,12},{9,13},{10,... | collective-permute-start | bytes 688136 | tf_op jit(solution)/shard_map/ppermute | solution.py:18
  103.3 16.2 %collective-permute-start.21 = (bf16[2,32,3584]{2,1,0:T(8,128)(2,1)S(1)}, bf16[2,32,3584]{2,1,0:T(8,128)(2,1)S(1)}, u32[]{:S(2)}, u32[]{:S(2)}) collective-permute-start(bf16[2,32,3584]{2,1,0:T(8,128)(2,1)S(1)} %pad_maximum_fusion.6), channel_id=1, source_target_pairs={{0,4},{1,5},{2,6},{3,7},{4,0},{5,1},{6,2},{7,3},{8,12},{9,13},{10,... | collective-permute-start | bytes 1376264 | tf_op jit(solution)/shard_map/ppermute | solution.py:18
  104.9 13.5 %collective-permute-start.24 = (bf16[2,32,3584]{2,1,0:T(8,128)(2,1)S(1)}, bf16[2,32,3584]{2,1,0:T(8,128)(2,1)S(1)}, u32[]{:S(2)}, u32[]{:S(2)}) collective-permute-start(bf16[2,32,3584]{2,1,0:T(8,128)(2,1)S(1)} %pad_maximum_fusion.7), channel_id=1, source_target_pairs={{0,2},{1,3},{2,0},{3,1},{4,6},{5,7},{6,4},{7,5},{8,10},{9,11},{10,... | collective-permute-start | bytes 1376264 | tf_op jit(solution)/shard_map/ppermute | solution.py:18
  108.2 18.4 %collective-permute-start.42 = (bf16[2,32,3584]{2,1,0:T(8,128)(2,1)S(1)}, bf16[2,32,3584]{2,1,0:T(8,128)(2,1)S(1)}, u32[]{:S(2)}, u32[]{:S(2)}) collective-permute-start(bf16[2,32,3584]{2,1,0:T(8,128)(2,1)S(1)} %pad_maximum_fusion.11), channel_id=1, source_target_pairs={{0,4},{1,5},{2,6},{3,7},{4,0},{5,1},{6,2},{7,3},{8,12},{9,13},{10,... | collective-permute-start | bytes 1376264 | tf_op jit(solution)/shard_map/ppermute | solution.py:18
  109.8 15.6 %collective-permute-start.45 = (bf16[2,32,3584]{2,1,0:T(8,128)(2,1)S(1)}, bf16[2,32,3584]{2,1,0:T(8,128)(2,1)S(1)}, u32[]{:S(2)}, u32[]{:S(2)}) collective-permute-start(bf16[2,32,3584]{2,1,0:T(8,128)(2,1)S(1)} %pad_maximum_fusion.12), channel_id=1, source_target_pairs={{0,2},{1,3},{2,0},{3,1},{4,6},{5,7},{6,4},{7,5},{8,10},{9,11},{10,... | collective-permute-start | bytes 1376264 | tf_op jit(solution)/shard_map/ppermute | solution.py:18
  119.6 11.5 %collective-permute-start.22 = (bf16[4,32,3584]{2,1,0:T(8,128)(2,1)S(1)}, bf16[4,32,3584]{2,1,0:T(8,128)(2,1)S(1)}, u32[]{:S(2)}, u32[]{:S(2)}) collective-permute-start(bf16[4,32,3584]{2,1,0:T(8,128)(2,1)S(1)} %pad_maximum_fusion), channel_id=1, source_target_pairs={{0,1},{1,0},{2,3},{3,2},{4,5},{5,4},{6,7},{7,6},{8,9},{9,8},{10,11... | collective-permute-start | bytes 2752520 | tf_op jit(solution)/shard_map/ppermute | solution.py:18
  125.7 12.2 %collective-permute-start.46 = (bf16[4,32,3584]{2,1,0:T(8,128)(2,1)S(1)}, bf16[4,32,3584]{2,1,0:T(8,128)(2,1)S(1)}, u32[]{:S(2)}, u32[]{:S(2)}) collective-permute-start(bf16[4,32,3584]{2,1,0:T(8,128)(2,1)S(1)} %pad_maximum_fusion.3), channel_id=1, source_target_pairs={{0,1},{1,0},{2,3},{3,2},{4,5},{5,4},{6,7},{7,6},{8,9},{9,8},{10,11... | collective-permute-start | bytes 2752520 | tf_op jit(solution)/shard_map/ppermute | solution.py:18
  126.7 13.5 %collective-permute-start.43 = (bf16[4,32,3584]{2,1,0:T(8,128)(2,1)S(1)}, bf16[4,32,3584]{2,1,0:T(8,128)(2,1)S(1)}, u32[]{:S(2)}, u32[]{:S(2)}) collective-permute-start(bf16[4,32,3584]{2,1,0:T(8,128)(2,1)S(1)} %pad_maximum_fusion.2), channel_id=1, source_target_pairs={{0,1},{1,0},{2,3},{3,2},{4,5},{5,4},{6,7},{7,6},{8,9},{9,8},{10,11... | collective-permute-start | bytes 2752520 | tf_op jit(solution)/shard_map/ppermute | solution.py:18
  135.9 9.8 %collective-permute-start.32 = (bf16[128,3584]{1,0:T(8,128)(2,1)S(1)}, bf16[128,3584]{1,0:T(8,128)(2,1)S(1)}, u32[]{:S(2)}, u32[]{:S(2)}) collective-permute-start(bf16[128,3584]{1,0:T(8,128)(2,1)S(1)} %slice.912), channel_id=1, source_target_pairs={{0,1},{1,0},{2,3},{3,2},{4,5},{5,4},{6,7},{7,6},{8,9},{9,8},{10,11... | collective-permute-start | bytes 2752520 | tf_op jit(solution)/shard_map/ppermute | solution.py:18
  146.1 13.4 %collective-permute-start.33 = (bf16[2,32,3584]{2,1,0:T(8,128)(2,1)S(1)}, bf16[2,32,3584]{2,1,0:T(8,128)(2,1)S(1)}, u32[]{:S(2)}, u32[]{:S(2)}) collective-permute-start(bf16[2,32,3584]{2,1,0:T(8,128)(2,1)S(1)} %pad_maximum_fusion.9), channel_id=1, source_target_pairs={{0,4},{1,5},{2,6},{3,7},{4,0},{5,1},{6,2},{7,3},{8,12},{9,13},{10,... | collective-permute-start | bytes 1376264 | tf_op jit(solution)/shard_map/ppermute | solution.py:18
  147.8 13.5 %collective-permute-start.30 = (bf16[2,32,3584]{2,1,0:T(8,128)(2,1)S(1)}, bf16[2,32,3584]{2,1,0:T(8,128)(2,1)S(1)}, u32[]{:S(2)}, u32[]{:S(2)}) collective-permute-start(bf16[2,32,3584]{2,1,0:T(8,128)(2,1)S(1)} %pad_maximum_fusion.8), channel_id=1, source_target_pairs={{0,2},{1,3},{2,0},{3,1},{4,6},{5,7},{6,4},{7,5},{8,10},{9,11},{10,... | collective-permute-start | bytes 1376264 | tf_op jit(solution)/shard_map/ppermute | solution.py:18
  149.1 20.2 %collective-permute-start.51 = (bf16[2,32,3584]{2,1,0:T(8,128)(2,1)S(1)}, bf16[2,32,3584]{2,1,0:T(8,128)(2,1)S(1)}, u32[]{:S(2)}, u32[]{:S(2)}) collective-permute-start(bf16[2,32,3584]{2,1,0:T(8,128)(2,1)S(1)} %pad_maximum_fusion.14), channel_id=1, source_target_pairs={{0,4},{1,5},{2,6},{3,7},{4,0},{5,1},{6,2},{7,3},{8,12},{9,13},{10,... | collective-permute-start | bytes 1376264 | tf_op jit(solution)/shard_map/ppermute | solution.py:18
  150.9 20.2 %collective-permute-start.48 = (bf16[2,32,3584]{2,1,0:T(8,128)(2,1)S(1)}, bf16[2,32,3584]{2,1,0:T(8,128)(2,1)S(1)}, u32[]{:S(2)}, u32[]{:S(2)}) collective-permute-start(bf16[2,32,3584]{2,1,0:T(8,128)(2,1)S(1)} %pad_maximum_fusion.13), channel_id=1, source_target_pairs={{0,2},{1,3},{2,0},{3,1},{4,6},{5,7},{6,4},{7,5},{8,10},{9,11},{10,... | collective-permute-start | bytes 1376264 | tf_op jit(solution)/shard_map/ppermute | solution.py:18
  159.6 16.4 %collective-permute-start.34 = (bf16[1,32,3584]{2,1,0:T(8,128)(2,1)S(1)}, bf16[1,32,3584]{2,1,0:T(8,128)(2,1)S(1)}, u32[]{:S(2)}, u32[]{:S(2)}) collective-permute-start(bf16[1,32,3584]{2,1,0:T(8,128)(2,1)S(1)} %slice.917), channel_id=1, source_target_pairs={{0,2},{1,3},{2,0},{3,1},{4,6},{5,7},{6,4},{7,5},{8,10},{9,11},{10,... | collective-permute-start | bytes 688136 | tf_op jit(solution)/shard_map/ppermute | solution.py:18
  161.4 14.7 %collective-permute-start.31 = (bf16[1,32,3584]{2,1,0:T(8,128)(2,1)S(1)}, bf16[1,32,3584]{2,1,0:T(8,128)(2,1)S(1)}, u32[]{:S(2)}, u32[]{:S(2)}) collective-permute-start(bf16[1,32,3584]{2,1,0:T(8,128)(2,1)S(1)} %slice.918), channel_id=1, source_target_pairs={{0,4},{1,5},{2,6},{3,7},{4,0},{5,1},{6,2},{7,3},{8,12},{9,13},{10,... | collective-permute-start | bytes 688136 | tf_op jit(solution)/shard_map/ppermute | solution.py:18
  169.4 10.3 %collective-permute-start.52 = (bf16[1,32,3584]{2,1,0:T(8,128)(2,1)S(1)}, bf16[1,32,3584]{2,1,0:T(8,128)(2,1)S(1)}, u32[]{:S(2)}, u32[]{:S(2)}) collective-permute-start(bf16[1,32,3584]{2,1,0:T(8,128)(2,1)S(1)} %slice.915), channel_id=1, source_target_pairs={{0,2},{1,3},{2,0},{3,1},{4,6},{5,7},{6,4},{7,5},{8,10},{9,11},{10,... | collective-permute-start | bytes 688136 | tf_op jit(solution)/shard_map/ppermute | solution.py:18
  177.2 17.1 %collective-permute-start.36 = (bf16[8,7168]{1,0:T(8,128)(2,1)S(1)}, bf16[8,7168]{1,0:T(8,128)(2,1)S(1)}, u32[]{:S(2)}, u32[]{:S(2)}) collective-permute-start(bf16[8,7168]{1,0:T(8,128)(2,1)S(1)} %get-tuple-element.42), channel_id=1, source_target_pairs={{0,16},{8,24},{16,0},{24,8},{1,17},{9,25},{17,1},{25,9},{2,18},{10... | collective-permute-start | bytes 344072 | tf_op jit(solution)/shard_map/ppermute | solution.py:18
  179.9 14.6 %collective-permute-start.53 = (bf16[8,7168]{1,0:T(8,128)(2,1)S(1)}, bf16[8,7168]{1,0:T(8,128)(2,1)S(1)}, u32[]{:S(2)}, u32[]{:S(2)}) collective-permute-start(bf16[8,7168]{1,0:T(8,128)(2,1)S(1)} %get-tuple-element.47), channel_id=1, source_target_pairs={{0,8},{8,0},{16,24},{24,16},{1,9},{9,1},{17,25},{25,17},{2,10},{10... | collective-permute-start | bytes 344072 | tf_op jit(solution)/shard_map/ppermute | solution.py:18
  180.9 13.5 %collective-permute-start.55 = (bf16[8,7168]{1,0:T(8,128)(2,1)S(1)}, bf16[8,7168]{1,0:T(8,128)(2,1)S(1)}, u32[]{:S(2)}, u32[]{:S(2)}) collective-permute-start(bf16[8,7168]{1,0:T(8,128)(2,1)S(1)} %get-tuple-element.48), channel_id=1, source_target_pairs={{0,24},{8,16},{16,8},{24,0},{1,25},{9,17},{17,9},{25,1},{2,26},{10... | collective-permute-start | bytes 344072 | tf_op jit(solution)/shard_map/ppermute | solution.py:18
  184.3 12.9 %collective-permute-start.54 = (bf16[8,7168]{1,0:T(8,128)(2,1)S(1)}, bf16[8,7168]{1,0:T(8,128)(2,1)S(1)}, u32[]{:S(2)}, u32[]{:S(2)}) collective-permute-start(bf16[8,7168]{1,0:T(8,128)(2,1)S(1)} %get-tuple-element.49), channel_id=1, source_target_pairs={{0,16},{8,24},{16,0},{24,8},{1,17},{9,25},{17,1},{25,9},{2,18},{10... | collective-permute-start | bytes 344072 | tf_op jit(solution)/shard_map/ppermute | solution.py:18
  (50 other events, 361.4 us)
where the time goes:
time: 198 us
  waiting for transfers between devices  91.6 us (46%)
  starting transfers between devices  59.2 us (30%)
  matrix products  14.2 us (7%)
  local copies, waits for them, and re-layouts  12.8 us (6%)
  Pallas kernels  8.82 us (4%)
  other arithmetic  7.47 us (4%)
  between operations  4.06 us (2%)
    ppermute x56, waiting for transfers between devices, swap(): return lax.ppermute(x, axis, [(i, i ^ distance) for i in range(size)])  91.6 us
    ppermute x56, starting transfers between devices, swap(): return lax.ppermute(x, axis, [(i, i ^ distance) for i in range(size)])  59.2 us
    unnamed x86, local copies, waits for them, and re-layouts  6.55 us
    dot_general x4, matrix products, experts(): out = jnp.dot(active, matrix, preferred_element_type=jnp.float32)  4.61 us
    dot_general x4, matrix products, project(): jnp.dot(left, matrix[:half_width], preferred_element_type=jnp.float32)  4.51 us
    dot_general x4, matrix products, project(): jnp.dot(right, matrix[half_width:], preferred_element_type=jnp.float32)  4.41 us
  transfers between devices with their start and end apart: 56, of which 30 were waited for; matrix products, arithmetic and copies ran while one was open for 12% of the time, Pallas kernels for 2%

commit v1 on v0

--- a/solution.py
+++ b/solution.py
@@ -10,7 +10,6 @@
 
 score_scale = 192.0 ** (-0.5)
 norm_eps = 1e-06
-chunk_count = 2
 
 
 def swap(x, axis, distance):
@@ -18,10 +17,14 @@
     return lax.ppermute(x, axis, [(i, i ^ distance) for i in range(size)])
 
 
+def after(x, *others):
+    return lax.optimization_barrier((x,) + others)[0]
+
+
 def pick_kernel(plan, place, lists, pool, *outs):
     req_count, per_index, depth_here, pool_rows, width, far_width, far_split, near_split = plan
     slots = per_index * depth_here
-    req_index, exp_index = place[0], place[1]
+    req_index = place[0]
     row = lax.broadcasted_iota(jnp.int32, (16, pool_rows), 0)
     column = lax.broadcasted_iota(jnp.int32, (16, pool_rows), 1)
 
@@ -33,20 +36,18 @@
             hot = hot | ((row == slot) & (column == page - req_index * pool_rows))
         return hot.astype(jnp.float32)
 
-    def lay(hot, start, split, piece):
+    piece = far_width // far_split
+    for out, j in zip(outs, range(1, req_count)):
+        hot = wanted(req_index ^ j)
         total = jnp.zeros((16, piece), jnp.float32)
-        for part in range(split):
+        for part in range(far_split):
             shifted = hot if part == 0 else pltpu.roll(hot, part * slots, 0)
-            cols = pl.ds(pl.multiple_of(start + part * piece, 128), piece)
             total = total + jnp.dot(
-                shifted.astype(jnp.bfloat16), pool[:, cols], preferred_element_type=jnp.float32
+                shifted.astype(jnp.bfloat16),
+                pool[:, part * piece : (part + 1) * piece],
+                preferred_element_type=jnp.float32,
             )
-        return total.astype(jnp.bfloat16)
-
-    for out, j in zip(outs, range(1, req_count)):
-        out[...] = lay(
-            wanted(req_index ^ j), exp_index * far_width, far_split, far_width // far_split
-        )
+        out[...] = total.astype(jnp.bfloat16)
 
 
 def near_kernel(plan, place, lists, pool, out):
@@ -77,7 +78,7 @@
     plan, place, near, far, new, q_even, q_odd, bias_even, bias_odd, bias_new, uv, out,
     k_even, k_odd, s_even, s_odd, heads,
 ):
-    per_index, latent, kv_rank, head_here, tok_rows, order, sub_rows, chunks = plan
+    per_index, latent, kv_rank, head_here, tok_rows, order, own_rows = plan
     pair = 2 * latent
     window = latent + 64
     lead = pair - window
@@ -136,15 +137,14 @@
             uv[h],
             preferred_element_type=jnp.float32,
         )
-    if sub_rows % 8:
+    if own_rows % 8:
         out[...] = heads[...].astype(jnp.bfloat16)
         return
     exp_index = place[1]
     blocks = []
     for m in order:
-        for c in range(chunks):
-            at = ((exp_index ^ m) * chunks + c) * sub_rows
-            blocks.append(heads[pl.ds(pl.multiple_of(at, 8), sub_rows), :])
+        at = (exp_index ^ m) * own_rows
+        blocks.append(heads[pl.ds(pl.multiple_of(at, 8), own_rows), :])
     out[...] = jnp.concatenate(blocks, axis=0).astype(jnp.bfloat16)
 
 
@@ -182,7 +182,6 @@
     col_width = width // req_count
     half_width = width // 2
     own_rows = tok_rows // exp_count
-    sub_rows = own_rows // chunk_count
     outer = exp_count // 2
     req_rel = req_index ^ jnp.arange(req_count, dtype=jnp.int32)
     rel_order = [2 * k for k in range(outer)] + [2 * k + 1 for k in range(outer)]
@@ -205,8 +204,12 @@
     sent = pl.pallas_call(
         functools.partial(pick_kernel, plan),
         out_shape=[far_shape] * (req_count - 1),
-        in_specs=[scalars, scalars, whole],
-        out_specs=[whole] * (req_count - 1),
+        grid_spec=pltpu.PrefetchScalarGridSpec(
+            num_scalar_prefetch=2,
+            grid=(1,),
+            in_specs=[pl.BlockSpec((pool_rows, far_width), lambda n, place, lists: (0, place[1]))],
+            out_specs=[whole] * (req_count - 1),
+        ),
         name="pick_far",
     )(place, page_list, pool)
     near = pl.pallas_call(
@@ -223,6 +226,20 @@
     def positions(tokens, holder_ids, split, slot_row):
         depth = holder_ids * depth_here + slot_row % slots % depth_here
         return jnp.where(slot_row < slots * split, depth * page_size + tokens, list_depth * page_size)
+
+    chosen = route_ids == exp_index
+    token_weight = jnp.sum(jnp.where(chosen, route_weight, 0.0), axis=1)
+    token_weight = token_weight.reshape(exp_count, own_rows)[exp_rel]
+    behind = [after(token_weight, far)] * (req_count - 1)
+    weight_all = jnp.stack(
+        [token_weight] + [swap(behind[j - 1], "req", j) for j in range(1, req_count)], axis=1
+    )
+    hidden_cols = []
+    for j in range(req_count):
+        piece = lax.dynamic_slice_in_dim(hidden_in, req_rel[j] * col_width, col_width, 1)
+        hidden_cols.append(piece if j == 0 else swap(after(piece, far), "req", j))
+    hidden_cols = jnp.concatenate(hidden_cols, axis=0)
+    near, hidden_cols, weight_all = lax.optimization_barrier((near, hidden_cols, weight_all))
 
     near_piece = page_size // near_split
     pairs = np.arange(near_piece // 2)[:, None]
@@ -262,8 +279,7 @@
         functools.partial(
             attention_kernel,
             (
-                per_index, latent, kv_rank, head_here, tok_rows, tuple(rel_order), sub_rows,
-                chunk_count,
+                per_index, latent, kv_rank, head_here, tok_rows, tuple(rel_order), own_rows,
             ),
         ),
         out_shape=jax.ShapeDtypeStruct((tok_rows, head_cols), jnp.bfloat16),
@@ -279,78 +295,86 @@
         compiler_params=pltpu.CompilerParams(vmem_limit_bytes=40 * 1024 * 1024),
         name="attention",
     )(place, near, far_all, new_keys, q_even, q_odd, bias_even, bias_odd, bias_new, uv_weight)
-    head_out = head_out.reshape(exp_count, chunk_count, sub_rows, head_cols)
-    if sub_rows % 8:
+    head_out = head_out.reshape(exp_count, own_rows, head_cols)
+    if own_rows % 8:
         head_out = head_out[exp_rel]
 
-    chosen = route_ids == exp_index
-    token_weight = jnp.sum(jnp.where(chosen, route_weight, 0.0), axis=1)
-    token_weight = token_weight.reshape(exp_count, chunk_count, sub_rows)[exp_rel]
-    weight_all = jnp.stack(
-        [token_weight] + [swap(token_weight, "req", j) for j in range(1, req_count)]
-    ).transpose(2, 1, 0, 3)
-
-    hidden_cols = []
-    for j in range(req_count):
-        piece = lax.dynamic_slice_in_dim(hidden_in, req_rel[j] * col_width, col_width, 1)
-        hidden_cols.append(piece if j == 0 else swap(piece, "req", j))
-    hidden_cols = jnp.stack(hidden_cols).reshape(req_count, chunk_count, sub_rows, col_width)
-    hidden_cols = hidden_cols.transpose(1, 0, 2, 3)
-
     heads_all = jnp.stack(
-        [head_out] + [swap(head_out, "req", j) for j in range(1, req_count)], axis=2
-    )
-    block = req_count * sub_rows
-    own_block = chunk_count * block
+        [head_out] + [swap(head_out, "req", j) for j in range(1, req_count)], axis=1
+    )
+    block = req_count * own_rows
     partial = jnp.dot(
-        heads_all.reshape(exp_count * own_block, head_cols),
+        heads_all.reshape(exp_count * block, head_cols),
         out_weight,
         preferred_element_type=jnp.float32,
     )
-    cut = outer * own_block
+    cut = outer * block
     other = swap(partial[cut:].astype(jnp.bfloat16), "exp", 1)
-    pair_sum = (partial[:cut] + other.astype(jnp.float32)).reshape(outer, own_block, col_width)
+    pair_sum = (partial[:cut] + other.astype(jnp.float32)).reshape(outer, block, col_width)
     attn = pair_sum[0]
     for k in range(1, outer):
         attn = attn + swap(pair_sum[k].astype(jnp.bfloat16), "exp", 2 * k).astype(jnp.float32)
-    attn = attn.reshape(chunk_count, req_count, sub_rows, col_width)
-    resid_cols = (hidden_cols.astype(jnp.float32) + attn).astype(jnp.bfloat16)
-
-    def gather_columns(resid):
-        slices = [resid]
-        for j in range(1, req_count):
-            got = swap(resid, "req", j)
-            slices.append(jnp.stack([got[i ^ j] for i in range(req_count)]))
-        ordered = jnp.stack(slices)[req_rel]
-        return ordered.transpose(1, 2, 0, 3).reshape(block, width)
-
-    def normalise(full):
-        widened = full.astype(jnp.float32)
-        inv_scale = lax.rsqrt(jnp.mean(widened * widened, axis=-1, keepdims=True) + norm_eps)
-        return (widened * inv_scale * norm_gain.astype(jnp.float32)).astype(jnp.bfloat16)
+    resid = (hidden_cols.astype(jnp.float32) + attn).astype(jnp.bfloat16)
+
+    pieces = [resid]
+    for b in range(1, req_count):
+        got = swap(resid if b < 3 else after(resid, pieces[b - 2]), "req", b)
+        got = got.reshape(req_count, own_rows, col_width)
+        pieces.append(jnp.concatenate([got[i ^ b] for i in range(req_count)], axis=0))
 
     outer_bits = []
     bit = 1
     while bit < outer:
         outer_bits.append(bit)
         bit *= 2
-    sides = (outer_bits, outer_bits[::-1])
-
-    def gather_plane(piece, bits):
+    orders = (outer_bits, outer_bits[::-1])
+
+    def gather_side(piece, bits):
         held = piece[None]
         ids = [0]
         for bit in bits:
             held = jnp.concatenate([held, swap(held, "exp", 2 * bit)], axis=0)
             ids = ids + [k ^ bit for k in ids]
-        back = [ids.index(k) for k in range(outer)]
-        other = swap(held, "exp", 1)
-        picks = [held[k] for k in back] + [other[k] for k in back]
-        return jnp.concatenate(picks, axis=0)
-
-    def scatter_plane(partial, bits):
-        cut = outer * block
-        other = swap(partial[cut:].astype(jnp.bfloat16), "exp", 1)
-        held = (partial[:cut] + other.astype(jnp.float32)).reshape(outer, block, half_width)
+        return [held[ids.index(k)] for k in range(outer)]
+
+    def gather_plane(piece):
+        half = piece.shape[0] // 2
+        first = gather_side(piece[:half], orders[0])
+        second = gather_side(piece[half:], orders[1])
+        same = jnp.concatenate([p for pair in zip(first, second) for p in pair], axis=0)
+        return jnp.concatenate([same, swap(same, "exp", 1)], axis=0)
+
+    gate_here = gate_weight[0]
+    up_here = up_weight[0]
+    down_here = down_weight[0]
+    gain = norm_gain.astype(jnp.float32)
+    gate_val = up_val = squares = 0.0
+    span = max(1, req_count // 4)
+    slices = []
+    for b in range(0, req_count, span):
+        rows = gather_plane(jnp.concatenate(pieces[b : b + span], axis=0))
+        rows = rows.reshape(exp_count, span, block, col_width)
+        slices += [rows[:, n].reshape(exp_count * block, col_width) for n in range(span)]
+    for b in range(req_count):
+        start = req_rel[b] * col_width
+        rows = slices[b].astype(jnp.float32)
+        squares = squares + jnp.sum(rows * rows, axis=-1, keepdims=True)
+        scaled = (rows * lax.dynamic_slice_in_dim(gain, start, col_width)).astype(jnp.bfloat16)
+        gate_val = gate_val + jnp.dot(
+            scaled,
+            lax.dynamic_slice_in_dim(gate_here, start, col_width),
+            preferred_element_type=jnp.float32,
+        )
+        up_val = up_val + jnp.dot(
+            scaled,
+            lax.dynamic_slice_in_dim(up_here, start, col_width),
+            preferred_element_type=jnp.float32,
+        )
+    inv_scale = lax.rsqrt(squares / width + norm_eps)
+    active = (jax.nn.silu(gate_val * inv_scale) * (up_val * inv_scale)).astype(jnp.bfloat16)
+    active = active.reshape(exp_count, req_count, own_rows, -1)
+
+    def scatter_side(held, bits):
         ids = list(range(outer))
         for bit in bits:
             keep = [n for n, k in enumerate(ids) if not k & bit]
@@ -362,39 +386,29 @@
             ids = [ids[n] for n in keep]
         return held[0].astype(jnp.bfloat16)
 
-    gate_here = gate_weight[0]
-    up_here = up_weight[0]
-    down_here = down_weight[0]
-
-    def experts(left, right, weights):
-        def project(matrix):
-            return jnp.dot(
-                left, matrix[:half_width], preferred_element_type=jnp.float32
-            ) + jnp.dot(right, matrix[half_width:], preferred_element_type=jnp.float32)
-
-        active = (jax.nn.silu(project(gate_here)) * project(up_here)).astype(jnp.bfloat16)
-        outs = []
-        for matrix in (down_here[:, :half_width], down_here[:, half_width:]):
-            out = jnp.dot(active, matrix, preferred_element_type=jnp.float32)
-            outs.append(out * weights[:, None])
-        return outs
-
-    results = []
-    for c in range(chunk_count):
-        full = gather_columns(resid_cols[c])
-        normed = normalise(full)
-        rows = [
-            gather_plane(normed[:, n * half_width : (n + 1) * half_width], sides[n])
-            for n in range(2)
+    own = jnp.stack([piece[:own_rows] for piece in pieces])[req_rel]
+    total = own.transpose(1, 0, 2).reshape(own_rows, width).astype(jnp.float32)
+    previous = None
+    for j in reversed(range(0, req_count, span)):
+        rows = active[:, j : j + span].reshape(span * tok_rows, -1)
+        if previous is not None:
+            rows = after(rows, previous)
+        out = jnp.dot(rows, down_here, preferred_element_type=jnp.float32)
+        out = out * weight_all[:, j : j + span].reshape(span * tok_rows, 1)
+        cut = span * tok_rows // 2
+        previous = out[cut:].astype(jnp.bfloat16)
+        pair_sum = out[:cut] + swap(previous, "exp", 1).astype(jnp.float32)
+        pair_sum = pair_sum.reshape(outer, span * own_rows, width)
+        sums = [
+            scatter_side(pair_sum[:, :, :half_width], orders[0]),
+            scatter_side(pair_sum[:, :, half_width:], orders[1]),
         ]
-        outs = experts(rows[0], rows[1], weight_all[c].reshape(-1))
-        sums = jnp.concatenate([scatter_plane(outs[n], sides[n]) for n in range(2)], axis=1)
-        sums = sums.reshape(req_count, sub_rows, width)
-        total = full[:sub_rows].astype(jnp.float32) + sums[0].astype(jnp.float32)
-        for j in range(1, req_count):
-            total = total + swap(sums[j], "req", j).astype(jnp.float32)
-        results.append(total.astype(jnp.bfloat16))
-    return jnp.concatenate(results, axis=0)
+        sums = jnp.concatenate(sums, axis=1)
+        for n in reversed(range(span)):
+            part = sums[n * own_rows : (n + 1) * own_rows]
+            part = swap(part, "req", j + n) if j + n else part
+            total = total + part.astype(jnp.float32)
+    return total.astype(jnp.bfloat16)
 
 
 def solution(mesh):

time: 198 us -> 214 us (1.081)
  local copies, waits for them, and re-layouts: 12.8 us -> 29.1 us
  waiting for transfers between devices: 91.6 us -> 76 us
  starting transfers between devices: 59.2 us -> 68.3 us
  other arithmetic: 7.47 us -> 10.1 us
  matrix products: 14.2 us -> 16.6 us
    ppermute x56 -> x66, waiting for transfers between devices: 91.6 us -> 76 us  [swap(): return lax.ppermute(x, axis, [(i, i ^ distance) for i in range(size)])]
    unnamed x86 -> x134, local copies, waits for them, and re-layouts: 6.55 us -> 18.1 us
    ppermute x56 -> x66, starting transfers between devices: 59.2 us -> 68.3 us  [swap(): return lax.ppermute(x, axis, [(i, i ^ distance) for i in range(size)])]
    dot_general x13, matrix products: 14.2 us -> 16.6 us  [the longest x4 6.58 us: local(): jnp.dot(scaled, lax.dynamic_slice_in_dim(up_here, start, col_width), pref...]
    another operation x15 -> x11, other arithmetic: 3.1 us -> 0.71 us
    mul x2 -> x4, local copies, waits for them, and re-layouts: 0.19 us -> 2.54 us  [local(): out = out * weight_all[:, j:j + span].reshape(span * tok_rows, 1)]
  transfers between devices with their start and end apart: 56 -> 66, of which waited for: 30 -> 25; matrix products, arithmetic and copies ran while one was open for 12% -> 20% of each run, Pallas kernels for 2% -> 1%
where the time goes in v1:
time: 214 us; the launch traced here: 213 us
  waiting for transfers between devices  76 us (36%)
  starting transfers between devices  68.3 us (32%)
  local copies, waits for them, and re-layouts  29.1 us (14%)
  matrix products  16.6 us (8%)
  other arithmetic  10.1 us (5%)
  Pallas kernels  8.86 us (4%)
  between operations  4.21 us (2%)
    ppermute x66, waiting for transfers between devices, swap(): return lax.ppermute(x, axis, [(i, i ^ distance) for i in range(size)])  76 us
    ppermute x66, starting transfers between devices, swap(): return lax.ppermute(x, axis, [(i, i ^ distance) for i in range(size)])  68.3 us
    unnamed x134, local copies, waits for them, and re-layouts  18.1 us
    dot_general x4, matrix products, local(): jnp.dot(scaled, lax.dynamic_slice_in_dim(up_here, start, col_width), pref...  6.58 us
    dot_general x4, matrix products, local(): out = jnp.dot(rows, down_here, preferred_element_type=jnp.float32)  4.88 us
    dot_general x4, matrix products, local(): jnp.dot(scaled, lax.dynamic_slice_in_dim(gate_here, start, col_width), pr...  4.52 us
  transfers between devices with their start and end apart: 66, of which 25 were waited for; matrix products, arithmetic and copies ran while one was open for 20% of the time, Pallas kernels for 1%

profile of v1, /device:TPU:0, one launch (start us, length us, event | category | flops | bytes accessed | tf_op | source)
XLA Modules:
  0.0 213.3 jit_solution(906716568528461503)
XLA Ops:
  0.7 2.6 %pick_far.1 = (bf16[16,2304]{1,0:T(8,128)(2,1)}, bf16[16,2304]{1,0:T(8,128)(2,1)}, bf16[16,2304]{1,0:T(8,128)(2,1)}) custom-call(s32[2]{0:T(128)} %pad_add_fusion.1.place, s32[8,16]{1,0:T(8,128)} %lists.3, bf16[32,36864]{1,0:T(8,128)(2,1)} %pool.3), custom_call_target="tpu_custom_call" | custom-call | tf_op jit(solution)/shard_map/pick_far/pallas_call | solution.py:204
  3.3 3.1 %collective-permute-start = (bf16[16,2304]{1,0:T(8,128)(2,1)}, bf16[16,2304]{1,0:T(8,128)(2,1)S(1)}, u32[]{:S(2)}, u32[]{:S(2)}) collective-permute-start(bf16[16,2304]{1,0:T(8,128)(2,1)} %get-tuple-element.18), channel_id=1, source_target_pairs={{0,8},{8,0},{16,24},{24,16},{1,9},{9,1},{17,25},{25,17},{2,10},{10... | collective-permute-start | bytes 221192 | tf_op jit(solution)/shard_map/ppermute | solution.py:17
  6.4 2.6 %collective-permute-start.1 = (bf16[16,2304]{1,0:T(8,128)(2,1)}, bf16[16,2304]{1,0:T(8,128)(2,1)S(1)}, u32[]{:S(2)}, u32[]{:S(2)}) collective-permute-start(bf16[16,2304]{1,0:T(8,128)(2,1)} %get-tuple-element.19), channel_id=1, source_target_pairs={{0,16},{8,24},{16,0},{24,8},{1,17},{9,25},{17,1},{25,9},{2,18},{10... | collective-permute-start | bytes 221192 | tf_op jit(solution)/shard_map/ppermute | solution.py:17
  12.9 3.1 %pick_near.1.near = bf16[16,18432]{1,0:T(8,128)(2,1)} custom-call(s32[2]{0:T(128)} %pad_add_fusion.1.place, s32[8,16]{1,0:T(8,128)} %lists.3, bf16[32,36864]{1,0:T(8,128)(2,1)} %pool.3), custom_call_target="tpu_custom_call" | custom-call | tf_op jit(solution)/shard_map/pick_near/pallas_call | solution.py:215
  17.8 3.9 %collective-permute-start.8 = (f32[8,16]{1,0:T(8,128)S(1)}, f32[8,16]{1,0:T(8,128)S(1)}, u32[]{:S(2)}, u32[]{:S(2)}) collective-permute-start(f32[8,16]{1,0:T(8,128)S(1)} %gather_fusion), channel_id=1, source_target_pairs={{0,24},{8,16},{16,8},{24,0},{1,25},{9,17},{17,9},{25,1},{2,26},{10... | collective-permute-start | bytes 1544 | tf_op jit(solution)/shard_map/ppermute | solution.py:17
  22.3 2.6 %collective-permute-start.11 = (bf16[48,2304]{1,0:T(8,128)(2,1)S(1)}, bf16[48,2304]{1,0:T(8,128)(2,1)S(1)}, u32[]{:S(2)}, u32[]{:S(2)}) collective-permute-start(bf16[48,2304]{1,0:T(8,128)(2,1)S(1)} %constant_dynamic-update-slice_fusion), channel_id=1, source_target_pairs={{0,6},{1,7},{2,4},{3,5},{4,2},{5,3},{6,0},{7,1},{8,14},{9,15},{10,... | collective-permute-start | bytes 663560 | tf_op jit(solution)/shard_map/ppermute | solution.py:17
  25.4 2.2 %collective-permute-start.4 = (bf16[16,1792]{1,0:T(8,128)(2,1)S(1)}, bf16[16,1792]{1,0:T(8,128)(2,1)S(1)}, u32[]{:S(2)}, u32[]{:S(2)}) collective-permute-start(bf16[16,1792]{1,0:T(8,128)(2,1)S(1)} %get-tuple-element.22), channel_id=1, source_target_pairs={{0,16},{8,24},{16,0},{24,8},{1,17},{9,25},{17,1},{25,9},{2,18},{10... | collective-permute-start | bytes 172040 | tf_op jit(solution)/shard_map/ppermute | solution.py:17
  29.8 1.7 collective-permute-done.4
  34.0 3.4 %collective-permute-done.9 = bf16[48,2304]{1,0:T(8,128)(2,1)S(1)} collective-permute-done((bf16[48,2304]{1,0:T(8,128)(2,1)S(1)}, bf16[48,2304]{1,0:T(8,128)(2,1)S(1)}, u32[]{:S(2)}, u32[]{:S(2)}) %collective-permute-start.9) | collective-permute-done | bytes 221216 | tf_op jit(solution)/shard_map/ppermute | solution.py:17
  37.7 2.3 %collective-permute-done.12 = bf16[4,48,2304]{2,1,0:T(8,128)(2,1)S(1)} collective-permute-done((bf16[4,48,2304]{2,1,0:T(8,128)(2,1)S(1)}, bf16[4,48,2304]{2,1,0:T(8,128)(2,1)S(1)}, u32[]{:S(2)}, u32[]{:S(2)}) %collective-permute-start.12) | collective-permute-done | bytes 884768 | tf_op jit(solution)/shard_map/ppermute | solution.py:17
  40.2 3.2 %attention.1 = bf16[128,256]{1,0:T(8,128)(2,1)S(1)} custom-call(s32[2]{0:T(128)S(1)} %copy-done.5, bf16[16,18432]{1,0:T(8,128)(2,1)S(1)} %copy-done.2, bf16[8,48,2304]{2,1,0:T(8,128)(2,1)S(1)} %constant_dynamic-update-slice_fusion.3.far, bf16[128,640]{1,0:T(8,128)(2,1)S(1)} %pad.12.new, bf16[256,640]{1,0:T(8,128)(2,1)S(1)} %get-tuple-element.59.q_even, ...), custom_call_target="tpu_custom_call" | custom-call | tf_op jit(solution)/shard_map/attention/pallas_call | solution.py:278
  43.4 2.8 %collective-permute-start.15 = (bf16[8,16,256]{2,1,0:T(8,128)(2,1)S(1)}, bf16[8,16,256]{2,1,0:T(8,128)(2,1)S(1)}, u32[]{:S(2)}, u32[]{:S(2)}) collective-permute-start(bf16[8,16,256]{2,1,0:T(8,128)(2,1)S(1)} %bitcast.279), channel_id=1, source_target_pairs={{0,24},{8,16},{16,8},{24,0},{1,25},{9,17},{17,9},{25,1},{2,26},{10... | collective-permute-start | bytes 196616 | tf_op jit(solution)/shard_map/ppermute | solution.py:17
  47.9 2.3 %collective-permute-done.15 = bf16[8,16,256]{2,1,0:T(8,128)(2,1)S(1)} collective-permute-done((bf16[8,16,256]{2,1,0:T(8,128)(2,1)S(1)}, bf16[8,16,256]{2,1,0:T(8,128)(2,1)S(1)}, u32[]{:S(2)}, u32[]{:S(2)}) %collective-permute-start.15) | collective-permute-done | bytes 65568 | tf_op jit(solution)/shard_map/ppermute | solution.py:17
  50.2 2.0 collective-permute-done.14
  57.0 2.4 %collective-permute-start.19 = (bf16[64,1792]{1,0:T(8,128)(2,1)S(1)}, bf16[64,1792]{1,0:T(8,128)(2,1)S(1)}, u32[]{:S(2)}, u32[]{:S(2)}) collective-permute-start(bf16[64,1792]{1,0:T(8,128)(2,1)S(1)} %get-tuple-element.52), channel_id=1, source_target_pairs={{0,6},{1,7},{2,4},{3,5},{4,2},{5,3},{6,0},{7,1},{8,14},{9,15},{10,... | collective-permute-start | bytes 688136 | tf_op jit(solution)/shard_map/ppermute | solution.py:17
  63.1 2.0 collective-permute-done.17
  65.2 5.2 %collective-permute-done.19 = bf16[64,1792]{1,0:T(8,128)(2,1)S(1)} collective-permute-done((bf16[64,1792]{1,0:T(8,128)(2,1)S(1)}, bf16[64,1792]{1,0:T(8,128)(2,1)S(1)}, u32[]{:S(2)}, u32[]{:S(2)}) %collective-permute-start.19) | collective-permute-done | bytes 229408 | tf_op jit(solution)/shard_map/ppermute | solution.py:17
  73.3 2.3 %collective-permute-start.21 = (bf16[64,1792]{1,0:T(8,128)(2,1)S(1)}, bf16[64,1792]{1,0:T(8,128)(2,1)S(1)}, u32[]{:S(2)}, u32[]{:S(2)}) collective-permute-start(bf16[64,1792]{1,0:T(8,128)(2,1)S(1)} %get-tuple-element.32), channel_id=1, source_target_pairs={{0,16},{8,24},{16,0},{24,8},{1,17},{9,25},{17,1},{25,9},{2,18},{10... | collective-permute-start | bytes 688136 | tf_op jit(solution)/shard_map/ppermute | solution.py:17
  79.5 1.9 collective-permute-done.24
  83.4 8.1 %collective-permute-done.21 = bf16[64,1792]{1,0:T(8,128)(2,1)S(1)} collective-permute-done((bf16[64,1792]{1,0:T(8,128)(2,1)S(1)}, bf16[64,1792]{1,0:T(8,128)(2,1)S(1)}, u32[]{:S(2)}, u32[]{:S(2)}) %collective-permute-start.21) | collective-permute-done | bytes 229408 | tf_op jit(solution)/shard_map/ppermute | solution.py:17
  123.5 5.6 %collective-permute-done.35 = bf16[2,32,1792]{2,1,0:T(8,128)(2,1)S(1)} collective-permute-done((bf16[2,32,1792]{2,1,0:T(8,128)(2,1)S(1)}, bf16[2,32,1792]{2,1,0:T(8,128)(2,1)S(1)}, u32[]{:S(2)}, u32[]{:S(2)}) %collective-permute-start.35) | collective-permute-done | bytes 229408 | tf_op jit(solution)/shard_map/ppermute | solution.py:17
  130.8 3.2 %collective-permute-done.30 = bf16[2,32,1792]{2,1,0:T(8,128)(2,1)S(1)} collective-permute-done((bf16[2,32,1792]{2,1,0:T(8,128)(2,1)S(1)}, bf16[2,32,1792]{2,1,0:T(8,128)(2,1)S(1)}, u32[]{:S(2)}, u32[]{:S(2)}) %collective-permute-start.30) | collective-permute-done | bytes 229408 | tf_op jit(solution)/shard_map/ppermute | solution.py:17
  134.8 3.5 %collective-permute-done.40 = bf16[2,32,1792]{2,1,0:T(8,128)(2,1)S(1)} collective-permute-done((bf16[2,32,1792]{2,1,0:T(8,128)(2,1)S(1)}, bf16[2,32,1792]{2,1,0:T(8,128)(2,1)S(1)}, u32[]{:S(2)}, u32[]{:S(2)}) %collective-permute-start.40) | collective-permute-done | bytes 229408 | tf_op jit(solution)/shard_map/ppermute | solution.py:17
  139.2 2.9 %fusion.14 = f32[512,512]{1,0:T(8,128)S(1)} fusion(bf16[1,7168,512]{2,1,0:T(8,128)(2,1)} %param.36, s32[]{:T(128)S(6)} %select_n.78, bf16[512,1792]{1,0:T(8,128)(2,1)S(1)} %constant_dynamic-update-slice_fusion.52, f32[1792]{0:T(1024)S(1)} %copy-done.24), kind=kOutput, calls=%fused_computation.38 | convolution fusion | flops 942276608 | bytes 4725764 | tf_op jit(solution)/shard_map/dot_general | solution.py:368
  168.3 4.2 %collective-permute-done.46 = bf16[2,16,3584]{2,1,0:T(8,128)(2,1)S(1)} collective-permute-done((bf16[2,16,3584]{2,1,0:T(8,128)(2,1)S(1)}, bf16[2,16,3584]{2,1,0:T(8,128)(2,1)S(1)}, u32[]{:S(2)}, u32[]{:S(2)}) %collective-permute-start.46) | collective-permute-done | bytes 229408 | tf_op jit(solution)/shard_map/ppermute | solution.py:17
  173.1 4.4 %collective-permute-done.52 = bf16[2,16,3584]{2,1,0:T(8,128)(2,1)S(1)} collective-permute-done((bf16[2,16,3584]{2,1,0:T(8,128)(2,1)S(1)}, bf16[2,16,3584]{2,1,0:T(8,128)(2,1)S(1)}, u32[]{:S(2)}, u32[]{:S(2)}) %collective-permute-start.52) | collective-permute-done | bytes 229408 | tf_op jit(solution)/shard_map/ppermute | solution.py:17
  179.2 3.2 %collective-permute-done.58 = bf16[2,16,3584]{2,1,0:T(8,128)(2,1)S(1)} collective-permute-done((bf16[2,16,3584]{2,1,0:T(8,128)(2,1)S(1)}, bf16[2,16,3584]{2,1,0:T(8,128)(2,1)S(1)}, u32[]{:S(2)}, u32[]{:S(2)}) %collective-permute-start.58) | collective-permute-done | bytes 229408 | tf_op jit(solution)/shard_map/ppermute | solution.py:17
  184.1 3.1 %collective-permute-done.64 = bf16[2,16,3584]{2,1,0:T(8,128)(2,1)S(1)} collective-permute-done((bf16[2,16,3584]{2,1,0:T(8,128)(2,1)S(1)}, bf16[2,16,3584]{2,1,0:T(8,128)(2,1)S(1)}, u32[]{:S(2)}, u32[]{:S(2)}) %collective-permute-start.64) | collective-permute-done | bytes 229408 | tf_op jit(solution)/shard_map/ppermute | solution.py:17
  194.5 2.3 %collective-permute-start.48 = (bf16[16,7168]{1,0:T(8,128)(2,1)S(1)}, bf16[16,7168]{1,0:T(8,128)(2,1)S(1)}, u32[]{:S(2)}, u32[]{:S(2)}) collective-permute-start(bf16[16,7168]{1,0:T(8,128)(2,1)S(1)} %pad_maximum_fusion.13), channel_id=1, source_target_pairs={{0,24},{8,16},{16,8},{24,0},{1,25},{9,17},{17,9},{25,1},{2,26},{10... | collective-permute-start | bytes 688136 | tf_op jit(solution)/shard_map/ppermute | solution.py:17
  197.0 2.2 %collective-permute-start.60 = (bf16[16,7168]{1,0:T(8,128)(2,1)S(1)}, bf16[16,7168]{1,0:T(8,128)(2,1)S(1)}, u32[]{:S(2)}, u32[]{:S(2)}) collective-permute-start(bf16[16,7168]{1,0:T(8,128)(2,1)S(1)} %pad_maximum_fusion.17), channel_id=1, source_target_pairs={{0,8},{8,0},{16,24},{24,16},{1,9},{9,1},{17,25},{25,17},{2,10},{10... | collective-permute-start | bytes 688136 | tf_op jit(solution)/shard_map/ppermute | solution.py:17
  199.3 5.6 %collective-permute-done.48 = bf16[16,7168]{1,0:T(8,128)(2,1)S(1)} collective-permute-done((bf16[16,7168]{1,0:T(8,128)(2,1)S(1)}, bf16[16,7168]{1,0:T(8,128)(2,1)S(1)}, u32[]{:S(2)}, u32[]{:S(2)}) %collective-permute-start.48) | collective-permute-done | bytes 229408 | tf_op jit(solution)/shard_map/ppermute | solution.py:17
  204.9 7.6 %collective-permute-done.54 = bf16[16,7168]{1,0:T(8,128)(2,1)S(1)} collective-permute-done((bf16[16,7168]{1,0:T(8,128)(2,1)S(1)}, bf16[16,7168]{1,0:T(8,128)(2,1)S(1)}, u32[]{:S(2)}, u32[]{:S(2)}) %collective-permute-start.54) | collective-permute-done | bytes 229408 | tf_op jit(solution)/shard_map/ppermute | solution.py:17
  (391 shorter events, 101.4 us)
Async XLA Ops:
  3.3 14.4 %collective-permute-start = (bf16[16,2304]{1,0:T(8,128)(2,1)}, bf16[16,2304]{1,0:T(8,128)(2,1)S(1)}, u32[]{:S(2)}, u32[]{:S(2)}) collective-permute-start(bf16[16,2304]{1,0:T(8,128)(2,1)} %get-tuple-element.18), channel_id=1, source_target_pairs={{0,8},{8,0},{16,24},{24,16},{1,9},{9,1},{17,25},{25,17},{2,10},{10... | collective-permute-start | bytes 221192 | tf_op jit(solution)/shard_map/ppermute | solution.py:17
  6.4 11.3 %collective-permute-start.1 = (bf16[16,2304]{1,0:T(8,128)(2,1)}, bf16[16,2304]{1,0:T(8,128)(2,1)S(1)}, u32[]{:S(2)}, u32[]{:S(2)}) collective-permute-start(bf16[16,2304]{1,0:T(8,128)(2,1)} %get-tuple-element.19), channel_id=1, source_target_pairs={{0,16},{8,24},{16,0},{24,8},{1,17},{9,25},{17,1},{25,9},{2,18},{10... | collective-permute-start | bytes 221192 | tf_op jit(solution)/shard_map/ppermute | solution.py:17
  22.3 11.7 %collective-permute-start.11 = (bf16[48,2304]{1,0:T(8,128)(2,1)S(1)}, bf16[48,2304]{1,0:T(8,128)(2,1)S(1)}, u32[]{:S(2)}, u32[]{:S(2)}) collective-permute-start(bf16[48,2304]{1,0:T(8,128)(2,1)S(1)} %constant_dynamic-update-slice_fusion), channel_id=1, source_target_pairs={{0,6},{1,7},{2,4},{3,5},{4,2},{5,3},{6,0},{7,1},{8,14},{9,15},{10,... | collective-permute-start | bytes 663560 | tf_op jit(solution)/shard_map/ppermute | solution.py:17
  24.9 9.1 %collective-permute-start.10 = (bf16[48,2304]{1,0:T(8,128)(2,1)S(1)}, bf16[48,2304]{1,0:T(8,128)(2,1)S(1)}, u32[]{:S(2)}, u32[]{:S(2)}) collective-permute-start(bf16[48,2304]{1,0:T(8,128)(2,1)S(1)} %constant_dynamic-update-slice_fusion), channel_id=1, source_target_pairs={{0,4},{1,5},{2,6},{3,7},{4,0},{5,1},{6,2},{7,3},{8,12},{9,13},{10,... | collective-permute-start | bytes 663560 | tf_op jit(solution)/shard_map/ppermute | solution.py:17
  57.0 13.3 %collective-permute-start.19 = (bf16[64,1792]{1,0:T(8,128)(2,1)S(1)}, bf16[64,1792]{1,0:T(8,128)(2,1)S(1)}, u32[]{:S(2)}, u32[]{:S(2)}) collective-permute-start(bf16[64,1792]{1,0:T(8,128)(2,1)S(1)} %get-tuple-element.52), channel_id=1, source_target_pairs={{0,6},{1,7},{2,4},{3,5},{4,2},{5,3},{6,0},{7,1},{8,14},{9,15},{10,... | collective-permute-start | bytes 688136 | tf_op jit(solution)/shard_map/ppermute | solution.py:17
  59.5 12.0 %collective-permute-start.18 = (bf16[64,1792]{1,0:T(8,128)(2,1)S(1)}, bf16[64,1792]{1,0:T(8,128)(2,1)S(1)}, u32[]{:S(2)}, u32[]{:S(2)}) collective-permute-start(bf16[64,1792]{1,0:T(8,128)(2,1)S(1)} %get-tuple-element.53), channel_id=1, source_target_pairs={{0,4},{1,5},{2,6},{3,7},{4,0},{5,1},{6,2},{7,3},{8,12},{9,13},{10,... | collective-permute-start | bytes 688136 | tf_op jit(solution)/shard_map/ppermute | solution.py:17
  71.7 21.8 %collective-permute-start.20 = (bf16[64,1792]{1,0:T(8,128)(2,1)S(1)}, bf16[64,1792]{1,0:T(8,128)(2,1)S(1)}, u32[]{:S(2)}, u32[]{:S(2)}) collective-permute-start(bf16[64,1792]{1,0:T(8,128)(2,1)S(1)} %get-tuple-element.32), channel_id=1, source_target_pairs={{0,8},{8,0},{16,24},{24,16},{1,9},{9,1},{17,25},{25,17},{2,10},{10... | collective-permute-start | bytes 688136 | tf_op jit(solution)/shard_map/ppermute | solution.py:17
  73.3 18.2 %collective-permute-start.21 = (bf16[64,1792]{1,0:T(8,128)(2,1)S(1)}, bf16[64,1792]{1,0:T(8,128)(2,1)S(1)}, u32[]{:S(2)}, u32[]{:S(2)}) collective-permute-start(bf16[64,1792]{1,0:T(8,128)(2,1)S(1)} %get-tuple-element.32), channel_id=1, source_target_pairs={{0,16},{8,24},{16,0},{24,8},{1,17},{9,25},{17,1},{25,9},{2,18},{10... | collective-permute-start | bytes 688136 | tf_op jit(solution)/shard_map/ppermute | solution.py:17
  76.1 19.2 %collective-permute-start.22 = (bf16[64,1792]{1,0:T(8,128)(2,1)S(1)}, bf16[64,1792]{1,0:T(8,128)(2,1)S(1)}, u32[]{:S(2)}, u32[]{:S(2)}) collective-permute-start(bf16[64,1792]{1,0:T(8,128)(2,1)S(1)} %get-tuple-element.32), channel_id=1, source_target_pairs={{0,24},{8,16},{16,8},{24,0},{1,25},{9,17},{17,9},{25,1},{2,26},{10... | collective-permute-start | bytes 688136 | tf_op jit(solution)/shard_map/ppermute | solution.py:17
  78.2 28.7 %collective-permute-start.26 = (bf16[2,32,1792]{2,1,0:T(8,128)(2,1)}, bf16[2,32,1792]{2,1,0:T(8,128)(2,1)}, u32[]{:S(2)}, u32[]{:S(2)}) collective-permute-start(bf16[2,32,1792]{2,1,0:T(8,128)(2,1)} %pad_maximum_fusion.5), channel_id=1, source_target_pairs={{0,4},{1,5},{2,6},{3,7},{4,0},{5,1},{6,2},{7,3},{8,12},{9,13},{10,... | collective-permute-start | bytes 688136 | tf_op jit(solution)/shard_map/ppermute | solution.py:17
  82.1 21.6 %collective-permute-start.25 = (bf16[2,32,1792]{2,1,0:T(8,128)(2,1)}, bf16[2,32,1792]{2,1,0:T(8,128)(2,1)}, u32[]{:S(2)}, u32[]{:S(2)}) collective-permute-start(bf16[2,32,1792]{2,1,0:T(8,128)(2,1)} %pad_maximum_fusion.4), channel_id=1, source_target_pairs={{0,2},{1,3},{2,0},{3,1},{4,6},{5,7},{6,4},{7,5},{8,10},{9,11},{10,... | collective-permute-start | bytes 688136 | tf_op jit(solution)/shard_map/ppermute | solution.py:17
  92.9 26.0 %collective-permute-start.34 = (bf16[1,32,1792]{2,1,0:T(8,128)(2,1)S(1)}, bf16[1,32,1792]{2,1,0:T(8,128)(2,1)S(1)}, u32[]{:S(2)}, u32[]{:S(2)}) collective-permute-start(bf16[1,32,1792]{2,1,0:T(8,128)(2,1)S(1)} %get-tuple-element.104), channel_id=1, source_target_pairs={{0,4},{1,5},{2,6},{3,7},{4,0},{5,1},{6,2},{7,3},{8,12},{9,13},{10,... | collective-permute-start | bytes 344072 | tf_op jit(solution)/shard_map/ppermute | solution.py:17
  93.4 19.8 %collective-permute-start.33 = (bf16[1,32,1792]{2,1,0:T(8,128)(2,1)}, bf16[1,32,1792]{2,1,0:T(8,128)(2,1)}, u32[]{:S(2)}, u32[]{:S(2)}) collective-permute-start(bf16[1,32,1792]{2,1,0:T(8,128)(2,1)} %get-tuple-element.105), channel_id=1, source_target_pairs={{0,2},{1,3},{2,0},{3,1},{4,6},{5,7},{6,4},{7,5},{8,10},{9,11},{10,... | collective-permute-start | bytes 344072 | tf_op jit(solution)/shard_map/ppermute | solution.py:17
  95.3 21.1 %collective-permute-start.28 = (bf16[1,32,1792]{2,1,0:T(8,128)(2,1)S(1)}, bf16[1,32,1792]{2,1,0:T(8,128)(2,1)}, u32[]{:S(2)}, u32[]{:S(2)}) collective-permute-start(bf16[1,32,1792]{2,1,0:T(8,128)(2,1)S(1)} %maximum_bitcast_fusion), channel_id=1, source_target_pairs={{0,2},{1,3},{2,0},{3,1},{4,6},{5,7},{6,4},{7,5},{8,10},{9,11},{10,... | collective-permute-start | bytes 344072 | tf_op jit(solution)/shard_map/ppermute | solution.py:17
  103.7 16.9 %collective-permute-start.29 = (bf16[1,32,1792]{2,1,0:T(8,128)(2,1)S(1)}, bf16[1,32,1792]{2,1,0:T(8,128)(2,1)S(1)}, u32[]{:S(2)}, u32[]{:S(2)}) collective-permute-start(bf16[1,32,1792]{2,1,0:T(8,128)(2,1)S(1)} %maximum_bitcast_fusion.1), channel_id=1, source_target_pairs={{0,4},{1,5},{2,6},{3,7},{4,0},{5,1},{6,2},{7,3},{8,12},{9,13},{10,... | collective-permute-start | bytes 344072 | tf_op jit(solution)/shard_map/ppermute | solution.py:17
  106.9 14.8 %collective-permute-start.38 = (bf16[1,32,1792]{2,1,0:T(8,128)(2,1)S(1)}, bf16[1,32,1792]{2,1,0:T(8,128)(2,1)S(1)}, u32[]{:S(2)}, u32[]{:S(2)}) collective-permute-start(bf16[1,32,1792]{2,1,0:T(8,128)(2,1)S(1)} %maximum_bitcast_fusion.2), channel_id=1, source_target_pairs={{0,2},{1,3},{2,0},{3,1},{4,6},{5,7},{6,4},{7,5},{8,10},{9,11},{10,... | collective-permute-start | bytes 344072 | tf_op jit(solution)/shard_map/ppermute | solution.py:17
  113.3 9.6 %collective-permute-start.39 = (bf16[1,32,1792]{2,1,0:T(8,128)(2,1)S(1)}, bf16[1,32,1792]{2,1,0:T(8,128)(2,1)S(1)}, u32[]{:S(2)}, u32[]{:S(2)}) collective-permute-start(bf16[1,32,1792]{2,1,0:T(8,128)(2,1)S(1)} %maximum_bitcast_fusion.3), channel_id=1, source_target_pairs={{0,4},{1,5},{2,6},{3,7},{4,0},{5,1},{6,2},{7,3},{8,12},{9,13},{10,... | collective-permute-start | bytes 344072 | tf_op jit(solution)/shard_map/ppermute | solution.py:17
  116.4 22.0 %collective-permute-start.27 = (bf16[256,1792]{1,0:T(8,128)(2,1)}, bf16[256,1792]{1,0:T(8,128)(2,1)S(1)}, u32[]{:S(2)}, u32[]{:S(2)}) collective-permute-start(bf16[256,1792]{1,0:T(8,128)(2,1)} %get-tuple-element.74), channel_id=1, source_target_pairs={{0,1},{1,0},{2,3},{3,2},{4,5},{5,4},{6,7},{7,6},{8,9},{9,8},{10,11... | collective-permute-start | bytes 2752520 | tf_op jit(solution)/shard_map/ppermute | solution.py:17
  119.0 11.1 %collective-permute-start.36 = (bf16[2,32,1792]{2,1,0:T(8,128)(2,1)S(1)}, bf16[2,32,1792]{2,1,0:T(8,128)(2,1)S(1)}, u32[]{:S(2)}, u32[]{:S(2)}) collective-permute-start(bf16[2,32,1792]{2,1,0:T(8,128)(2,1)S(1)} %pad_maximum_fusion.9), channel_id=1, source_target_pairs={{0,4},{1,5},{2,6},{3,7},{4,0},{5,1},{6,2},{7,3},{8,12},{9,13},{10,... | collective-permute-start | bytes 688136 | tf_op jit(solution)/shard_map/ppermute | solution.py:17
  121.7 12.4 %collective-permute-start.30 = (bf16[2,32,1792]{2,1,0:T(8,128)(2,1)S(1)}, bf16[2,32,1792]{2,1,0:T(8,128)(2,1)S(1)}, u32[]{:S(2)}, u32[]{:S(2)}) collective-permute-start(bf16[2,32,1792]{2,1,0:T(8,128)(2,1)S(1)} %pad_maximum_fusion.6), channel_id=1, source_target_pairs={{0,2},{1,3},{2,0},{3,1},{4,6},{5,7},{6,4},{7,5},{8,10},{9,11},{10,... | collective-permute-start | bytes 688136 | tf_op jit(solution)/shard_map/ppermute | solution.py:17
  122.9 11.2 %collective-permute-start.31 = (bf16[2,32,1792]{2,1,0:T(8,128)(2,1)S(1)}, bf16[2,32,1792]{2,1,0:T(8,128)(2,1)S(1)}, u32[]{:S(2)}, u32[]{:S(2)}) collective-permute-start(bf16[2,32,1792]{2,1,0:T(8,128)(2,1)S(1)} %pad_maximum_fusion.7), channel_id=1, source_target_pairs={{0,4},{1,5},{2,6},{3,7},{4,0},{5,1},{6,2},{7,3},{8,12},{9,13},{10,... | collective-permute-start | bytes 688136 | tf_op jit(solution)/shard_map/ppermute | solution.py:17
  129.1 9.1 %collective-permute-start.40 = (bf16[2,32,1792]{2,1,0:T(8,128)(2,1)S(1)}, bf16[2,32,1792]{2,1,0:T(8,128)(2,1)S(1)}, u32[]{:S(2)}, u32[]{:S(2)}) collective-permute-start(bf16[2,32,1792]{2,1,0:T(8,128)(2,1)S(1)} %pad_maximum_fusion.10), channel_id=1, source_target_pairs={{0,2},{1,3},{2,0},{3,1},{4,6},{5,7},{6,4},{7,5},{8,10},{9,11},{10,... | collective-permute-start | bytes 688136 | tf_op jit(solution)/shard_map/ppermute | solution.py:17
  134.2 9.1 %collective-permute-start.32 = (bf16[256,1792]{1,0:T(8,128)(2,1)S(1)}, bf16[256,1792]{1,0:T(8,128)(2,1)S(1)}, u32[]{:S(2)}, u32[]{:S(2)}) collective-permute-start(bf16[256,1792]{1,0:T(8,128)(2,1)S(1)} %get-tuple-element.84), channel_id=1, source_target_pairs={{0,1},{1,0},{2,3},{3,2},{4,5},{5,4},{6,7},{7,6},{8,9},{9,8},{10,11... | collective-permute-start | bytes 2752520 | tf_op jit(solution)/shard_map/ppermute | solution.py:17
  163.0 15.5 %collective-permute-start.44 = (bf16[2,16,3584]{2,1,0:T(8,128)(2,1)S(1)}, bf16[2,16,3584]{2,1,0:T(8,128)(2,1)S(1)}, u32[]{:S(2)}, u32[]{:S(2)}) collective-permute-start(bf16[2,16,3584]{2,1,0:T(8,128)(2,1)S(1)} %pad_maximum_fusion.12), channel_id=1, source_target_pairs={{0,2},{1,3},{2,0},{3,1},{4,6},{5,7},{6,4},{7,5},{8,10},{9,11},{10,... | collective-permute-start | bytes 688136 | tf_op jit(solution)/shard_map/ppermute | solution.py:17
  164.6 18.3 %collective-permute-start.50 = (bf16[2,16,3584]{2,1,0:T(8,128)(2,1)S(1)}, bf16[2,16,3584]{2,1,0:T(8,128)(2,1)S(1)}, u32[]{:S(2)}, u32[]{:S(2)}) collective-permute-start(bf16[2,16,3584]{2,1,0:T(8,128)(2,1)S(1)} %pad_maximum_fusion.14), channel_id=1, source_target_pairs={{0,2},{1,3},{2,0},{3,1},{4,6},{5,7},{6,4},{7,5},{8,10},{9,11},{10,... | collective-permute-start | bytes 688136 | tf_op jit(solution)/shard_map/ppermute | solution.py:17
  165.7 11.7 %collective-permute-start.52 = (bf16[2,16,3584]{2,1,0:T(8,128)(2,1)S(1)}, bf16[2,16,3584]{2,1,0:T(8,128)(2,1)S(1)}, u32[]{:S(2)}, u32[]{:S(2)}) collective-permute-start(bf16[2,16,3584]{2,1,0:T(8,128)(2,1)S(1)} %stack.147), channel_id=1, source_target_pairs={{0,4},{1,5},{2,6},{3,7},{4,0},{5,1},{6,2},{7,3},{8,12},{9,13},{10,... | collective-permute-start | bytes 688136 | tf_op jit(solution)/shard_map/ppermute | solution.py:17
  167.3 20.6 %collective-permute-start.56 = (bf16[2,16,3584]{2,1,0:T(8,128)(2,1)S(1)}, bf16[2,16,3584]{2,1,0:T(8,128)(2,1)S(1)}, u32[]{:S(2)}, u32[]{:S(2)}) collective-permute-start(bf16[2,16,3584]{2,1,0:T(8,128)(2,1)S(1)} %pad_maximum_fusion.16), channel_id=1, source_target_pairs={{0,2},{1,3},{2,0},{3,1},{4,6},{5,7},{6,4},{7,5},{8,10},{9,11},{10,... | collective-permute-start | bytes 688136 | tf_op jit(solution)/shard_map/ppermute | solution.py:17
  172.5 9.8 %collective-permute-start.58 = (bf16[2,16,3584]{2,1,0:T(8,128)(2,1)S(1)}, bf16[2,16,3584]{2,1,0:T(8,128)(2,1)S(1)}, u32[]{:S(2)}, u32[]{:S(2)}) collective-permute-start(bf16[2,16,3584]{2,1,0:T(8,128)(2,1)S(1)} %stack.149), channel_id=1, source_target_pairs={{0,4},{1,5},{2,6},{3,7},{4,0},{5,1},{6,2},{7,3},{8,12},{9,13},{10,... | collective-permute-start | bytes 688136 | tf_op jit(solution)/shard_map/ppermute | solution.py:17
  177.4 11.6 %collective-permute-start.62 = (bf16[2,16,3584]{2,1,0:T(8,128)(2,1)S(1)}, bf16[2,16,3584]{2,1,0:T(8,128)(2,1)S(1)}, u32[]{:S(2)}, u32[]{:S(2)}) collective-permute-start(bf16[2,16,3584]{2,1,0:T(8,128)(2,1)S(1)} %pad_maximum_fusion.18), channel_id=1, source_target_pairs={{0,2},{1,3},{2,0},{3,1},{4,6},{5,7},{6,4},{7,5},{8,10},{9,11},{10,... | collective-permute-start | bytes 688136 | tf_op jit(solution)/shard_map/ppermute | solution.py:17
  194.5 10.4 %collective-permute-start.48 = (bf16[16,7168]{1,0:T(8,128)(2,1)S(1)}, bf16[16,7168]{1,0:T(8,128)(2,1)S(1)}, u32[]{:S(2)}, u32[]{:S(2)}) collective-permute-start(bf16[16,7168]{1,0:T(8,128)(2,1)S(1)} %pad_maximum_fusion.13), channel_id=1, source_target_pairs={{0,24},{8,16},{16,8},{24,0},{1,25},{9,17},{17,9},{25,1},{2,26},{10... | collective-permute-start | bytes 688136 | tf_op jit(solution)/shard_map/ppermute | solution.py:17
  196.8 15.6 %collective-permute-start.54 = (bf16[16,7168]{1,0:T(8,128)(2,1)S(1)}, bf16[16,7168]{1,0:T(8,128)(2,1)S(1)}, u32[]{:S(2)}, u32[]{:S(2)}) collective-permute-start(bf16[16,7168]{1,0:T(8,128)(2,1)S(1)} %pad_maximum_fusion.15), channel_id=1, source_target_pairs={{0,16},{8,24},{16,0},{24,8},{1,17},{9,25},{17,1},{25,9},{2,18},{10... | collective-permute-start | bytes 688136 | tf_op jit(solution)/shard_map/ppermute | solution.py:17
  197.0 15.4 %collective-permute-start.60 = (bf16[16,7168]{1,0:T(8,128)(2,1)S(1)}, bf16[16,7168]{1,0:T(8,128)(2,1)S(1)}, u32[]{:S(2)}, u32[]{:S(2)}) collective-permute-start(bf16[16,7168]{1,0:T(8,128)(2,1)S(1)} %pad_maximum_fusion.17), channel_id=1, source_target_pairs={{0,8},{8,0},{16,24},{24,16},{1,9},{9,1},{17,25},{25,17},{2,10},{10... | collective-permute-start | bytes 688136 | tf_op jit(solution)/shard_map/ppermute | solution.py:17
  (80 other events, 592.2 us)

commit v2 on v1

--- a/solution.py
+++ b/solution.py
@@ -15,10 +15,6 @@
 def swap(x, axis, distance):
     size = lax.axis_size(axis)
     return lax.ppermute(x, axis, [(i, i ^ distance) for i in range(size)])
-
-
-def after(x, *others):
-    return lax.optimization_barrier((x,) + others)[0]
 
 
 def pick_kernel(plan, place, lists, pool, *outs):
@@ -75,7 +71,7 @@
 
 
 def attention_kernel(
-    plan, place, near, far, new, q_even, q_odd, bias_even, bias_odd, bias_new, uv, out,
+    plan, place, near, far, new, q_even, q_odd, bias_even, bias_odd, bias_new, uv, extra, out,
     k_even, k_odd, s_even, s_odd, heads,
 ):
     per_index, latent, kv_rank, head_here, tok_rows, order, own_rows = plan
@@ -137,15 +133,90 @@
             uv[h],
             preferred_element_type=jnp.float32,
         )
+    out[tok_rows:, :] = extra[...]
     if own_rows % 8:
-        out[...] = heads[...].astype(jnp.bfloat16)
+        out[:tok_rows, :] = heads[...].astype(jnp.bfloat16)
         return
     exp_index = place[1]
     blocks = []
     for m in order:
         at = (exp_index ^ m) * own_rows
         blocks.append(heads[pl.ds(pl.multiple_of(at, 8), own_rows), :])
-    out[...] = jnp.concatenate(blocks, axis=0).astype(jnp.bfloat16)
+    out[:tok_rows, :] = jnp.concatenate(blocks, axis=0).astype(jnp.bfloat16)
+
+
+def hold_kernel(x, other, out):
+    del other
+    out[...] = x[...]
+
+
+def collect_kernel(*refs):
+    out, base = refs[-1], 0
+    for ref in refs[:-2]:
+        out[base : base + ref.shape[0], :] = ref[...]
+        base += ref.shape[0]
+
+
+def multiply_kernel(plan, place, same, other, gain, gate, up, *refs):
+    shift, req_count, own_rows, width, first, last = plan
+    old, refs = (None, refs) if first else (refs[:3], refs[3:])
+    outs, (scaled, sums) = refs[:-2], refs[-2:]
+    rows, columns = same.shape
+    start = pl.multiple_of((place[0] ^ shift) * columns, 128)
+    gains = gain[:, pl.ds(start, columns)]
+    unit = own_rows if own_rows % 16 == 0 else req_count * own_rows
+    for half, ref in enumerate((same, other)):
+        for n in range(rows // unit):
+            to = n if unit > own_rows else n ^ shift
+            at = half * rows + to * unit
+            block = ref[n * unit : (n + 1) * unit, :].astype(jnp.float32)
+            scaled[at : at + unit, :] = (block * gains).astype(jnp.bfloat16)
+            block = block * block
+            total = block[:, :128]
+            for c in range(128, columns, 128):
+                total = total + block[:, c : c + 128]
+            sums[at : at + unit, :] = total
+    if first:
+        squares = sums[...]
+    else:
+        squares = old[2][...] + sums[...]
+    if last:
+        mean = jnp.sum(squares, axis=-1, keepdims=True) / width
+        inv_scale = lax.rsqrt(mean + norm_eps)
+    else:
+        outs[2][...] = squares
+    tile = min(256, gate.shape[1])
+    for n in range(0, gate.shape[1], tile):
+        cols = slice(n, n + tile)
+        values = []
+        for k, weight in enumerate((gate, up)):
+            value = jnp.dot(
+                scaled[...], weight[pl.ds(start, columns), cols], preferred_element_type=jnp.float32
+            )
+            values.append(value if first else value + old[k][:, cols])
+        if last:
+            gate_val, up_val = (value * inv_scale for value in values)
+            active = gate_val / (1.0 + jnp.exp(-gate_val)) * up_val
+            outs[0][:, cols] = active.astype(jnp.bfloat16)
+        else:
+            outs[0][:, cols] = values[0]
+            outs[1][:, cols] = values[1]
+
+
+def down_kernel(rows, down, weights, other, give, keep):
+    del other
+    half = keep.shape[0]
+    tile = 512
+
+    def step(n, carry):
+        cols = pl.ds(pl.multiple_of(n * tile, tile), tile)
+        out = jnp.dot(rows[...], down[:, cols], preferred_element_type=jnp.float32)
+        out = out * weights[...]
+        keep[:, cols] = out[:half]
+        give[:, cols] = out[half:].astype(jnp.bfloat16)
+        return carry
+
+    lax.fori_loop(0, down.shape[1] // tile, step, 0)
 
 
 def local(
@@ -229,17 +300,23 @@
 
     chosen = route_ids == exp_index
     token_weight = jnp.sum(jnp.where(chosen, route_weight, 0.0), axis=1)
-    token_weight = token_weight.reshape(exp_count, own_rows)[exp_rel]
-    behind = [after(token_weight, far)] * (req_count - 1)
-    weight_all = jnp.stack(
-        [token_weight] + [swap(behind[j - 1], "req", j) for j in range(1, req_count)], axis=1
-    )
+    token_weight = token_weight.reshape(exp_count, own_rows)[exp_rel].reshape(-1)
+    parts, left = [], token_weight
+    for n in range(3):
+        part = lax.reduce_precision(left, 8, 7)
+        left = left - part
+        parts.append(part.astype(jnp.bfloat16))
+    head_cols = head_here * value_width
+    extra_rows = -(-3 * tok_rows // (16 * head_cols)) * 16
+    extra = jnp.concatenate(parts)
+    extra = jnp.pad(extra, (0, extra_rows * head_cols - 3 * tok_rows))
+    extra = extra.reshape(extra_rows, head_cols)
+
     hidden_cols = []
     for j in range(req_count):
         piece = lax.dynamic_slice_in_dim(hidden_in, req_rel[j] * col_width, col_width, 1)
-        hidden_cols.append(piece if j == 0 else swap(after(piece, far), "req", j))
+        hidden_cols.append(piece if j == 0 else swap(piece, "req", j))
     hidden_cols = jnp.concatenate(hidden_cols, axis=0)
-    near, hidden_cols, weight_all = lax.optimization_barrier((near, hidden_cols, weight_all))
 
     near_piece = page_size // near_split
     pairs = np.arange(near_piece // 2)[:, None]
@@ -274,7 +351,6 @@
     new_keys = jnp.pad(new_latent, ((0, 0), (0, 64)))
     key_count = key_req.shape[1]
     q_rows = head_here * tok_rows
-    head_cols = head_here * value_width
     head_out = pl.pallas_call(
         functools.partial(
             attention_kernel,
@@ -282,8 +358,8 @@
                 per_index, latent, kv_rank, head_here, tok_rows, tuple(rel_order), own_rows,
             ),
         ),
-        out_shape=jax.ShapeDtypeStruct((tok_rows, head_cols), jnp.bfloat16),
-        in_specs=[scalars] + [whole] * 9,
+        out_shape=jax.ShapeDtypeStruct((tok_rows + extra_rows, head_cols), jnp.bfloat16),
+        in_specs=[scalars] + [whole] * 10,
         out_specs=whole,
         scratch_shapes=[
             pltpu.VMEM((key_count, latent + 64), jnp.bfloat16),
@@ -294,14 +370,18 @@
         ],
         compiler_params=pltpu.CompilerParams(vmem_limit_bytes=40 * 1024 * 1024),
         name="attention",
-    )(place, near, far_all, new_keys, q_even, q_odd, bias_even, bias_odd, bias_new, uv_weight)
-    head_out = head_out.reshape(exp_count, own_rows, head_cols)
+    )(place, near, far_all, new_keys, q_even, q_odd, bias_even, bias_odd, bias_new, uv_weight, extra)
     if own_rows % 8:
-        head_out = head_out[exp_rel]
-
+        ordered = head_out[:tok_rows].reshape(exp_count, own_rows, head_cols)[exp_rel]
+        head_out = jnp.concatenate([ordered.reshape(tok_rows, head_cols), head_out[tok_rows:]])
+
+    heads = [head_out] + [swap(head_out, "req", j) for j in range(1, req_count)]
     heads_all = jnp.stack(
-        [head_out] + [swap(head_out, "req", j) for j in range(1, req_count)], axis=1
+        [h[:tok_rows].reshape(exp_count, own_rows, head_cols) for h in heads], axis=1
     )
+    weight_all = jnp.stack([h[tok_rows:].reshape(-1)[: 3 * tok_rows] for h in heads])
+    weight_all = weight_all.astype(jnp.float32).reshape(req_count, 3, exp_count, own_rows)
+    weight_all = (weight_all[:, 0] + weight_all[:, 1] + weight_all[:, 2]).transpose(1, 0, 2)
     block = req_count * own_rows
     partial = jnp.dot(
         heads_all.reshape(exp_count * block, head_cols),
@@ -316,98 +396,137 @@
         attn = attn + swap(pair_sum[k].astype(jnp.bfloat16), "exp", 2 * k).astype(jnp.float32)
     resid = (hidden_cols.astype(jnp.float32) + attn).astype(jnp.bfloat16)
 
-    pieces = [resid]
-    for b in range(1, req_count):
-        got = swap(resid if b < 3 else after(resid, pieces[b - 2]), "req", b)
-        got = got.reshape(req_count, own_rows, col_width)
-        pieces.append(jnp.concatenate([got[i ^ b] for i in range(req_count)], axis=0))
-
     outer_bits = []
     bit = 1
     while bit < outer:
         outer_bits.append(bit)
         bit *= 2
-    orders = (outer_bits, outer_bits[::-1])
-
-    def gather_side(piece, bits):
+    somewhere = pl.BlockSpec(memory_space=pl.ANY)
+
+    def hold(x, other):
+        return pl.pallas_call(
+            hold_kernel,
+            out_shape=jax.ShapeDtypeStruct(x.shape, x.dtype),
+            in_specs=[whole, somewhere],
+            out_specs=whole,
+            name="hold",
+        )(x, other)
+
+    def collect(blocks, other):
+        rows = sum(x.shape[0] for x in blocks)
+        return pl.pallas_call(
+            collect_kernel,
+            out_shape=jax.ShapeDtypeStruct((rows, blocks[0].shape[1]), blocks[0].dtype),
+            in_specs=[whole] * len(blocks) + [somewhere],
+            out_specs=whole,
+            name="collect",
+        )(*blocks, other)
+
+    def gather_outer(piece):
+        if outer == 4:
+            half = piece.shape[0] // 2
+            along_x, along_y = swap(piece, "exp", 2), swap(piece, "exp", 4)
+            near_half = swap(along_x[:half], "exp", 4)
+            far_half = swap(along_y[half:], "exp", 2)
+            return [piece, along_x, along_y, near_half, far_half]
         held = piece[None]
-        ids = [0]
-        for bit in bits:
+        for bit in outer_bits:
             held = jnp.concatenate([held, swap(held, "exp", 2 * bit)], axis=0)
-            ids = ids + [k ^ bit for k in ids]
-        return [held[ids.index(k)] for k in range(outer)]
-
-    def gather_plane(piece):
-        half = piece.shape[0] // 2
-        first = gather_side(piece[:half], orders[0])
-        second = gather_side(piece[half:], orders[1])
-        same = jnp.concatenate([p for pair in zip(first, second) for p in pair], axis=0)
-        return jnp.concatenate([same, swap(same, "exp", 1)], axis=0)
-
-    gate_here = gate_weight[0]
-    up_here = up_weight[0]
-    down_here = down_weight[0]
-    gain = norm_gain.astype(jnp.float32)
-    gate_val = up_val = squares = 0.0
+        return list(held)
+
+    def scatter_outer(held):
+        if outer == 4:
+            half = held.shape[2] // 2
+            from_x = swap(held[3, :, :half].astype(jnp.bfloat16), "exp", 2)
+            from_y = swap(held[3, :, half:].astype(jnp.bfloat16), "exp", 4)
+            to_x = jnp.concatenate([held[1, :, :half], held[1, :, half:] + from_y], axis=1)
+            to_y = jnp.concatenate([held[2, :, :half] + from_x, held[2, :, half:]], axis=1)
+            return (
+                held[0]
+                + swap(to_x.astype(jnp.bfloat16), "exp", 2)
+                + swap(to_y.astype(jnp.bfloat16), "exp", 4)
+            )
+        for bit in reversed(outer_bits):
+            sent = swap(held[bit:].astype(jnp.bfloat16), "exp", 2 * bit)
+            held = held[:bit] + sent.astype(jnp.float32)
+        return held[0]
+
+    pieces = [resid]
+    for b in range(1, req_count):
+        pieces.append(swap(resid if b < 3 else hold(resid, pieces[b - 2]), "req", b))
+    aligned = own_rows % 16 == 0
+    if not aligned:
+        for b in range(1, req_count):
+            got = pieces[b].reshape(req_count, own_rows, col_width)
+            pieces[b] = jnp.concatenate([got[i ^ b] for i in range(req_count)], axis=0)
     span = max(1, req_count // 4)
-    slices = []
+    ffe = gate_weight.shape[2]
+    rows_all = exp_count * block
+    gain = norm_gain.astype(jnp.float32).reshape(1, width)
+    sum_shape = jax.ShapeDtypeStruct((rows_all, ffe), jnp.float32)
+    square_shape = jax.ShapeDtypeStruct((rows_all, 128), jnp.float32)
+    carry = []
     for b in range(0, req_count, span):
-        rows = gather_plane(jnp.concatenate(pieces[b : b + span], axis=0))
-        rows = rows.reshape(exp_count, span, block, col_width)
-        slices += [rows[:, n].reshape(exp_count * block, col_width) for n in range(span)]
-    for b in range(req_count):
-        start = req_rel[b] * col_width
-        rows = slices[b].astype(jnp.float32)
-        squares = squares + jnp.sum(rows * rows, axis=-1, keepdims=True)
-        scaled = (rows * lax.dynamic_slice_in_dim(gain, start, col_width)).astype(jnp.bfloat16)
-        gate_val = gate_val + jnp.dot(
-            scaled,
-            lax.dynamic_slice_in_dim(gate_here, start, col_width),
-            preferred_element_type=jnp.float32,
-        )
-        up_val = up_val + jnp.dot(
-            scaled,
-            lax.dynamic_slice_in_dim(up_here, start, col_width),
-            preferred_element_type=jnp.float32,
-        )
-    inv_scale = lax.rsqrt(squares / width + norm_eps)
-    active = (jax.nn.silu(gate_val * inv_scale) * (up_val * inv_scale)).astype(jnp.bfloat16)
-    active = active.reshape(exp_count, req_count, own_rows, -1)
-
-    def scatter_side(held, bits):
-        ids = list(range(outer))
-        for bit in bits:
-            keep = [n for n, k in enumerate(ids) if not k & bit]
-            give = [ids.index(ids[n] ^ bit) for n in keep]
-            sent = jnp.stack([held[n] for n in give]).astype(jnp.bfloat16)
-            held = jnp.stack([held[n] for n in keep]) + swap(sent, "exp", 2 * bit).astype(
-                jnp.float32
-            )
-            ids = [ids[n] for n in keep]
-        return held[0].astype(jnp.bfloat16)
-
-    own = jnp.stack([piece[:own_rows] for piece in pieces])[req_rel]
+        piece = jnp.concatenate(pieces[b : b + span], axis=0)
+        same = collect(gather_outer(piece), carry[0] if carry else extra)
+        other = swap(same, "exp", 1)
+        for n in range(span):
+            first, last = b + n == 0, b + n == req_count - 1
+            plan = (b + n, req_count, own_rows, width, first, last)
+            pair_rows = [
+                x if span == 1 else x.reshape(outer, span, block, col_width)[:, n].reshape(
+                    outer * block, col_width
+                )
+                for x in (same, other)
+            ]
+            operands = [place, *pair_rows, gain, gate_weight[0], up_weight[0], *carry]
+            carry = pl.pallas_call(
+                functools.partial(multiply_kernel, plan),
+                out_shape=(
+                    [jax.ShapeDtypeStruct((rows_all, ffe), jnp.bfloat16)]
+                    if last
+                    else [sum_shape, sum_shape, square_shape]
+                ),
+                in_specs=[scalars] + [whole] * (len(operands) - 1),
+                out_specs=[whole] * (1 if last else 3),
+                scratch_shapes=[
+                    pltpu.VMEM((rows_all, col_width), jnp.bfloat16),
+                    pltpu.VMEM((rows_all, 128), jnp.float32),
+                ],
+                compiler_params=pltpu.CompilerParams(vmem_limit_bytes=24 * 1024 * 1024),
+                name="multiply",
+            )(*operands)
+    active = carry[0].reshape(exp_count, req_count, own_rows, ffe)
+
+    own = [piece[:own_rows] for piece in pieces]
+    if aligned:
+        own = [p[b * own_rows : (b + 1) * own_rows] for b, p in enumerate(pieces)]
+    own = jnp.stack(own)[req_rel]
     total = own.transpose(1, 0, 2).reshape(own_rows, width).astype(jnp.float32)
-    previous = None
+    previous = extra
     for j in reversed(range(0, req_count, span)):
-        rows = active[:, j : j + span].reshape(span * tok_rows, -1)
-        if previous is not None:
-            rows = after(rows, previous)
-        out = jnp.dot(rows, down_here, preferred_element_type=jnp.float32)
-        out = out * weight_all[:, j : j + span].reshape(span * tok_rows, 1)
+        rows = active[:, j : j + span].reshape(span * tok_rows, ffe)
+        row_weight = weight_all[:, j : j + span].reshape(span * tok_rows, 1)
         cut = span * tok_rows // 2
-        previous = out[cut:].astype(jnp.bfloat16)
-        pair_sum = out[:cut] + swap(previous, "exp", 1).astype(jnp.float32)
-        pair_sum = pair_sum.reshape(outer, span * own_rows, width)
-        sums = [
-            scatter_side(pair_sum[:, :, :half_width], orders[0]),
-            scatter_side(pair_sum[:, :, half_width:], orders[1]),
-        ]
-        sums = jnp.concatenate(sums, axis=1)
+        give, keep = pl.pallas_call(
+            down_kernel,
+            out_shape=[
+                jax.ShapeDtypeStruct((cut, width), jnp.bfloat16),
+                jax.ShapeDtypeStruct((cut, width), jnp.float32),
+            ],
+            in_specs=[whole, whole, whole, somewhere],
+            out_specs=[whole, whole],
+            compiler_params=pltpu.CompilerParams(vmem_limit_bytes=24 * 1024 * 1024),
+            name="down",
+        )(rows, down_weight[0], row_weight, previous)
+        previous = give
+        pair_sum = keep + swap(give, "exp", 1).astype(jnp.float32)
+        sums = scatter_outer(pair_sum.reshape(outer, span * own_rows, width))
         for n in reversed(range(span)):
             part = sums[n * own_rows : (n + 1) * own_rows]
-            part = swap(part, "req", j + n) if j + n else part
-            total = total + part.astype(jnp.float32)
+            if j + n:
+                part = swap(part.astype(jnp.bfloat16), "req", j + n).astype(jnp.float32)
+            total = total + part
     return total.astype(jnp.bfloat16)
 
 

time: 214 us -> 276 us (1.29)
  local copies, waits for them, and re-layouts: 29.1 us -> 64.4 us
  Pallas kernels: 8.86 us -> 44.1 us
  matrix products: 16.6 us -> 0.64 us
  waiting for transfers between devices: 76 us -> 85.8 us
    pallas_call x0 -> x13, Pallas kernels: none -> 35.2 us  [the longest x4 13.7 us: local(): pl.pallas_call(down_kernel, out_shape=[jax.ShapeDtypeStruct((cut, width),...]
    unnamed x134 -> x158, local copies, waits for them, and re-layouts: 18.1 us -> 51.7 us
    dot_general x12 -> x0, matrix products: 16 us -> none  [the longest x4 6.58 us: local(): jnp.dot(scaled, lax.dynamic_slice_in_dim(up_here, start, col_width), pref...]
    ppermute x66 -> x63, waiting for transfers between devices: 76 us -> 85.8 us  [swap(): return lax.ppermute(x, axis, [(i, i ^ distance) for i in range(size)])]
    another operation x5 -> x8, local copies, waits for them, and re-layouts: 0.07 us -> 3.63 us  [the longest x4 3.29 us: local(): own = jnp.stack(own)[req_rel]]
    concatenate x12 -> x9, other arithmetic: 3.58 us -> 0.15 us  [the longest x4 0.07 us: scatter_outer(): jnp.concatenate([held[2, :, :half] + from_x, held[2, :, half:]], axis=1)]
    ppermute x66 -> x63, starting transfers between devices: 68.3 us -> 68.2 us  [swap(): return lax.ppermute(x, axis, [(i, i ^ distance) for i in range(size)])]
  transfers between devices with their start and end apart: 66 -> 63, of which waited for: 25 -> 25; matrix products, arithmetic and copies ran while one was open for 20% -> 7% of each run, Pallas kernels for 1% -> 9%
where the time goes in v2:
time: 276 us; the launch traced here: 274 us
  waiting for transfers between devices  85.8 us (31%)
  starting transfers between devices  68.2 us (25%)
  local copies, waits for them, and re-layouts  64.4 us (23%)
  Pallas kernels  44.1 us (16%)
  other arithmetic  7.57 us (3%)
  between operations  3.61 us (1%)
    ppermute x63, waiting for transfers between devices, swap(): return lax.ppermute(x, axis, [(i, i ^ distance) for i in range(size)])  85.8 us
    ppermute x63, starting transfers between devices, swap(): return lax.ppermute(x, axis, [(i, i ^ distance) for i in range(size)])  68.2 us
    unnamed x158, local copies, waits for them, and re-layouts  51.7 us
    pallas_call x4, Pallas kernels, local(): pl.pallas_call(down_kernel, out_shape=[jax.ShapeDtypeStruct((cut, width),...  13.7 us
    pallas_call x4, Pallas kernels, local(): pl.pallas_call(functools.partial(multiply_kernel, plan), out_shape=[jax.S...  10.8 us
    pallas_call x4, Pallas kernels, collect(): pl.pallas_call(collect_kernel, out_shape=jax.ShapeDtypeStruct((rows, bloc...  9.13 us
  transfers between devices with their start and end apart: 63, of which 25 were waited for; matrix products, arithmetic and copies ran while one was open for 7% of the time, Pallas kernels for 9%

profile of v2, /device:TPU:0, one launch (start us, length us, event | category | flops | bytes accessed | tf_op | source)
XLA Modules:
  0.0 274.2 jit_solution(7946279898131282869)
XLA Ops:
  3.3 3.1 %collective-permute-start.3 = (bf16[16,2304]{1,0:T(8,128)(2,1)}, bf16[16,2304]{1,0:T(8,128)(2,1)S(1)}, u32[]{:S(2)}, u32[]{:S(2)}) collective-permute-start(bf16[16,2304]{1,0:T(8,128)(2,1)} %get-tuple-element.25), channel_id=1, source_target_pairs={{0,8},{8,0},{16,24},{24,16},{1,9},{9,1},{17,25},{25,17},{2,10},{10... | collective-permute-start | bytes 221192 | tf_op jit(solution)/shard_map/ppermute | solution.py:17
  9.7 3.1 %pick_near.1.near = bf16[16,18432]{1,0:T(8,128)(2,1)} custom-call(s32[2]{0:T(128)} %pad_add_fusion.1.place, s32[8,16]{1,0:T(8,128)} %lists.3, bf16[32,36864]{1,0:T(8,128)(2,1)} %pool.3), custom_call_target="tpu_custom_call" | custom-call | tf_op jit(solution)/shard_map/pick_near/pallas_call | solution.py:286
  18.9 4.8 %collective-permute-done.6 = bf16[48,2304]{1,0:T(8,128)(2,1)S(1)} collective-permute-done((bf16[48,2304]{1,0:T(8,128)(2,1)S(1)}, bf16[48,2304]{1,0:T(8,128)(2,1)S(1)}, u32[]{:S(2)}, u32[]{:S(2)}) %collective-permute-start.6) | collective-permute-done | bytes 221216 | tf_op jit(solution)/shard_map/ppermute | solution.py:17
  23.7 3.6 %collective-permute-done.7 = bf16[48,2304]{1,0:T(8,128)(2,1)S(1)} collective-permute-done((bf16[48,2304]{1,0:T(8,128)(2,1)S(1)}, bf16[48,2304]{1,0:T(8,128)(2,1)S(1)}, u32[]{:S(2)}, u32[]{:S(2)}) %collective-permute-start.7) | collective-permute-done | bytes 221216 | tf_op jit(solution)/shard_map/ppermute | solution.py:17
  30.1 3.2 %attention.1 = bf16[144,256]{1,0:T(8,128)(2,1)S(1)} custom-call(s32[2]{0:T(128)S(1)} %copy-done.36, bf16[16,18432]{1,0:T(8,128)(2,1)S(1)} %copy-done.22, bf16[8,48,2304]{2,1,0:T(8,128)(2,1)S(1)} %constant_dynamic-update-slice_fusion.3.far, bf16[128,640]{1,0:T(8,128)(2,1)S(1)} %pad.16.new, bf16[256,640]{1,0:T(8,128)(2,1)S(1)} %get-tuple-element.79.q_even, ...), custom_call_target="tpu_custom_call" | custom-call | tf_op jit(solution)/shard_map/attention/pallas_call | solution.py:354
  34.1 3.4 %collective-permute-start.11 = (bf16[144,256]{1,0:T(8,128)(2,1)S(1)}, bf16[144,256]{1,0:T(8,128)(2,1)S(1)}, u32[]{:S(2)}, u32[]{:S(2)}) collective-permute-start(bf16[144,256]{1,0:T(8,128)(2,1)S(1)} %attention.1), channel_id=1, source_target_pairs={{0,16},{8,24},{16,0},{24,8},{1,17},{9,25},{17,1},{25,9},{2,18},{10... | collective-permute-start | bytes 221192 | tf_op jit(solution)/shard_map/ppermute | solution.py:17
  37.8 4.9 %collective-permute-done.11 = bf16[144,256]{1,0:T(8,128)(2,1)S(1)} collective-permute-done((bf16[144,256]{1,0:T(8,128)(2,1)S(1)}, bf16[144,256]{1,0:T(8,128)(2,1)S(1)}, u32[]{:S(2)}, u32[]{:S(2)}) %collective-permute-start.11) | collective-permute-done | bytes 73760 | tf_op jit(solution)/shard_map/ppermute | solution.py:17
  63.1 2.8 %collective-permute-done.2 = bf16[16,1792]{1,0:T(8,128)(2,1)S(1)} collective-permute-done((bf16[16,1792]{1,0:T(8,128)(2,1)S(1)}, bf16[16,1792]{1,0:T(8,128)(2,1)S(1)}, u32[]{:S(2)}, u32[]{:S(2)}) %collective-permute-start.2) | collective-permute-done | bytes 57376 | tf_op jit(solution)/shard_map/ppermute | solution.py:17
  68.5 4.9 %collective-permute-done.32.refs_1_ = bf16[64,1792]{1,0:T(8,128)(2,1)S(1)} collective-permute-done((bf16[64,1792]{1,0:T(8,128)(2,1)S(1)}, bf16[64,1792]{1,0:T(8,128)(2,1)S(1)}, u32[]{:S(2)}, u32[]{:S(2)}) %collective-permute-start.32) | collective-permute-done | bytes 229408 | tf_op jit(solution)/shard_map/ppermute | solution.py:17
  75.5 2.8 %collective-permute-done.34.refs_3_ = bf16[32,1792]{1,0:T(8,128)(2,1)S(1)} collective-permute-done((bf16[32,1792]{1,0:T(8,128)(2,1)S(1)}, bf16[32,1792]{1,0:T(8,128)(2,1)S(1)}, u32[]{:S(2)}, u32[]{:S(2)}) %collective-permute-start.34) | collective-permute-done | bytes 114720 | tf_op jit(solution)/shard_map/ppermute | solution.py:17
  83.2 6.9 %collective-permute-done.17.other.refs_0_ = bf16[64,1792]{1,0:T(8,128)(2,1)S(1)} collective-permute-done((bf16[64,1792]{1,0:T(8,128)(2,1)}, bf16[64,1792]{1,0:T(8,128)(2,1)S(1)}, u32[]{:S(2)}, u32[]{:S(2)}) %collective-permute-start.17) | collective-permute-done | bytes 229408 | tf_op jit(solution)/shard_map/ppermute | solution.py:17
  92.1 5.2 %collective-permute-done.28.refs_1_ = bf16[64,1792]{1,0:T(8,128)(2,1)S(1)} collective-permute-done((bf16[64,1792]{1,0:T(8,128)(2,1)S(1)}, bf16[64,1792]{1,0:T(8,128)(2,1)S(1)}, u32[]{:S(2)}, u32[]{:S(2)}) %collective-permute-start.28) | collective-permute-done | bytes 229408 | tf_op jit(solution)/shard_map/ppermute | solution.py:17
  99.5 3.1 %copy-done.2 = bf16[1,7168,512]{2,1,0:T(8,128)(2,1)S(1)} copy-done((bf16[1,7168,512]{2,1,0:T(8,128)(2,1)S(1)}, bf16[1,7168,512]{2,1,0:T(8,128)(2,1)}, u32[]{:S(2)}) %copy-start.2) | copy-done | bytes 7340056
  102.6 3.1 %copy-done.6 = bf16[1,7168,512]{2,1,0:T(8,128)(2,1)S(1)} copy-done((bf16[1,7168,512]{2,1,0:T(8,128)(2,1)S(1)}, bf16[1,7168,512]{2,1,0:T(8,128)(2,1)}, u32[]{:S(2)}) %copy-start.6) | copy-done | bytes 7340056
  117.5 11.5 %collective-permute-done.18.refs_0_ = bf16[64,1792]{1,0:T(8,128)(2,1)S(1)} collective-permute-done((bf16[64,1792]{1,0:T(8,128)(2,1)S(1)}, bf16[64,1792]{1,0:T(8,128)(2,1)S(1)}, u32[]{:S(2)}, u32[]{:S(2)}) %collective-permute-start.18) | collective-permute-done | bytes 229408 | tf_op jit(solution)/shard_map/ppermute | solution.py:17
  131.0 5.2 %collective-permute-done.24.refs_1_ = bf16[64,1792]{1,0:T(8,128)(2,1)S(1)} collective-permute-done((bf16[64,1792]{1,0:T(8,128)(2,1)S(1)}, bf16[64,1792]{1,0:T(8,128)(2,1)S(1)}, u32[]{:S(2)}, u32[]{:S(2)}) %collective-permute-start.24) | collective-permute-done | bytes 229408 | tf_op jit(solution)/shard_map/ppermute | solution.py:17
  143.9 3.1 %copy-done.3 = bf16[1,7168,512]{2,1,0:T(8,128)(2,1)S(1)} copy-done((bf16[1,7168,512]{2,1,0:T(8,128)(2,1)S(1)}, bf16[1,7168,512]{2,1,0:T(8,128)(2,1)}, u32[]{:S(2)}) %copy-start.3) | copy-done | bytes 7340056
  147.0 3.1 %copy-done.7 = bf16[1,7168,512]{2,1,0:T(8,128)(2,1)S(1)} copy-done((bf16[1,7168,512]{2,1,0:T(8,128)(2,1)S(1)}, bf16[1,7168,512]{2,1,0:T(8,128)(2,1)}, u32[]{:S(2)}) %copy-start.7) | copy-done | bytes 7340056
  153.4 2.8 %multiply.7 = (f32[512,512]{1,0:T(8,128)S(1)}, f32[512,512]{1,0:T(8,128)S(1)}, f32[512,128]{1,0:T(8,128)S(1)}) custom-call(s32[2]{0:T(128)S(1)} %copy-done.36, bf16[256,1792]{1,0:T(8,128)(2,1)S(1)} %copy-done.20, bf16[256,1792]{1,0:T(8,128)(2,1)S(1)} %collective-permute-done.37.other, f32[1,7168]{1,0:T(1,128)S(1)} %bitcast.191, ...), custom_call_target="tpu_custom_call" | custom-call | tf_op jit(solution)/shard_map/multiply/pallas_call | solution.py:483
  164.1 5.4 %collective-permute-done.20.refs_1_ = bf16[64,1792]{1,0:T(8,128)(2,1)} collective-permute-done((bf16[64,1792]{1,0:T(8,128)(2,1)}, bf16[64,1792]{1,0:T(8,128)(2,1)}, u32[]{:S(2)}, u32[]{:S(2)}) %collective-permute-start.20) | collective-permute-done | bytes 229408 | tf_op jit(solution)/shard_map/ppermute | solution.py:17
  173.4 3.1 %copy-done.4 = bf16[1,7168,512]{2,1,0:T(8,128)(2,1)S(1)} copy-done((bf16[1,7168,512]{2,1,0:T(8,128)(2,1)S(1)}, bf16[1,7168,512]{2,1,0:T(8,128)(2,1)}, u32[]{:S(2)}) %copy-start.4) | copy-done | bytes 7340056
  176.5 3.1 %copy-done.8 = bf16[1,7168,512]{2,1,0:T(8,128)(2,1)S(1)} copy-done((bf16[1,7168,512]{2,1,0:T(8,128)(2,1)S(1)}, bf16[1,7168,512]{2,1,0:T(8,128)(2,1)}, u32[]{:S(2)}) %copy-start.8) | copy-done | bytes 7340056
  192.3 3.1 %copy-done.5 = bf16[1,7168,512]{2,1,0:T(8,128)(2,1)S(1)} copy-done((bf16[1,7168,512]{2,1,0:T(8,128)(2,1)S(1)}, bf16[1,7168,512]{2,1,0:T(8,128)(2,1)}, u32[]{:S(2)}) %copy-start.5) | copy-done | bytes 7340056
  195.4 3.1 %copy-done.9 = bf16[1,7168,512]{2,1,0:T(8,128)(2,1)S(1)} copy-done((bf16[1,7168,512]{2,1,0:T(8,128)(2,1)S(1)}, bf16[1,7168,512]{2,1,0:T(8,128)(2,1)}, u32[]{:S(2)}) %copy-start.9) | copy-done | bytes 7340056
  202.4 3.1 %copy-done.10 = bf16[1,512,7168]{2,1,0:T(8,128)(2,1)S(1)} copy-done((bf16[1,512,7168]{2,1,0:T(8,128)(2,1)S(1)}, bf16[1,512,7168]{2,1,0:T(8,128)(2,1)}, u32[]{:S(2)}) %copy-start.10) | copy-done | bytes 7340056
  205.5 3.4 %down.4 = (bf16[64,7168]{1,0:T(8,128)(2,1)S(1)}, f32[64,7168]{1,0:T(8,128)S(1)}) custom-call(bf16[128,512]{1,0:T(8,128)(2,1)S(1)} %bitcast.197, bf16[512,7168]{1,0:T(8,128)(2,1)S(1)} %bitcast.185, f32[128,1]{1,0:T(8,128)S(1)} %copy-done.31, bf16[16,256]{1,0:T(8,128)(2,1)S(1)} %copy-done.34), custom_call_target="tpu_custom_call" | custom-call | tf_op jit(solution)/shard_map/down/pallas_call | solution.py:511
  214.0 3.1 %copy-done.11 = bf16[1,512,7168]{2,1,0:T(8,128)(2,1)S(1)} copy-done((bf16[1,512,7168]{2,1,0:T(8,128)(2,1)S(1)}, bf16[1,512,7168]{2,1,0:T(8,128)(2,1)}, u32[]{:S(2)}) %copy-start.11) | copy-done | bytes 7340056
  217.1 3.4 %down.5 = (bf16[64,7168]{1,0:T(8,128)(2,1)S(1)}, f32[64,7168]{1,0:T(8,128)S(1)}) custom-call(bf16[128,512]{1,0:T(8,128)(2,1)S(1)} %bitcast.196, bf16[512,7168]{1,0:T(8,128)(2,1)S(1)} %bitcast.186, f32[128,1]{1,0:T(8,128)S(1)} %reshape.336.weights, bf16[64,7168]{1,0:T(8,128)(2,1)S(1)} %get-tuple-element.38.other), custom_call_target="tpu_custom_call" | custom-call | tf_op jit(solution)/shard_map/down/pallas_call | solution.py:511
  220.6 3.4 %down.6 = (bf16[64,7168]{1,0:T(8,128)(2,1)S(1)}, f32[64,7168]{1,0:T(8,128)S(1)}) custom-call(bf16[128,512]{1,0:T(8,128)(2,1)S(1)} %bitcast.195, bf16[512,7168]{1,0:T(8,128)(2,1)S(1)} %bitcast.187, f32[128,1]{1,0:T(8,128)S(1)} %reshape.337.weights, bf16[64,7168]{1,0:T(8,128)(2,1)S(1)} %get-tuple-element.40.other), custom_call_target="tpu_custom_call" | custom-call | tf_op jit(solution)/shard_map/down/pallas_call | solution.py:511
  224.5 3.4 %down.7 = (bf16[64,7168]{1,0:T(8,128)(2,1)S(1)}, f32[64,7168]{1,0:T(8,128)S(1)}) custom-call(bf16[128,512]{1,0:T(8,128)(2,1)S(1)} %bitcast.194, bf16[512,7168]{1,0:T(8,128)(2,1)S(1)} %bitcast.188, f32[128,1]{1,0:T(8,128)S(1)} %reshape.338.weights, bf16[64,7168]{1,0:T(8,128)(2,1)S(1)} %get-tuple-element.42.other), custom_call_target="tpu_custom_call" | custom-call | tf_op jit(solution)/shard_map/down/pallas_call | solution.py:511
  245.7 3.9 %collective-permute-done.42 = bf16[16,7168]{1,0:T(8,128)(2,1)S(1)} collective-permute-done((bf16[16,7168]{1,0:T(8,128)(2,1)S(1)}, bf16[16,7168]{1,0:T(8,128)(2,1)S(1)}, u32[]{:S(2)}, u32[]{:S(2)}) %collective-permute-start.42) | collective-permute-done | bytes 229408 | tf_op jit(solution)/shard_map/ppermute | solution.py:17
  265.8 7.5 %collective-permute-done.51 = bf16[16,7168]{1,0:T(8,128)(2,1)S(1)} collective-permute-done((bf16[16,7168]{1,0:T(8,128)(2,1)S(1)}, bf16[16,7168]{1,0:T(8,128)(2,1)S(1)}, u32[]{:S(2)}, u32[]{:S(2)}) %collective-permute-start.51) | collective-permute-done | bytes 229408 | tf_op jit(solution)/shard_map/ppermute | solution.py:17
  (377 shorter events, 141.2 us)
Async XLA Ops:
  3.3 11.3 %collective-permute-start.3 = (bf16[16,2304]{1,0:T(8,128)(2,1)}, bf16[16,2304]{1,0:T(8,128)(2,1)S(1)}, u32[]{:S(2)}, u32[]{:S(2)}) collective-permute-start(bf16[16,2304]{1,0:T(8,128)(2,1)} %get-tuple-element.25), channel_id=1, source_target_pairs={{0,8},{8,0},{16,24},{24,16},{1,9},{9,1},{17,25},{25,17},{2,10},{10... | collective-permute-start | bytes 221192 | tf_op jit(solution)/shard_map/ppermute | solution.py:17
  16.9 10.4 %collective-permute-start.7 = (bf16[48,2304]{1,0:T(8,128)(2,1)S(1)}, bf16[48,2304]{1,0:T(8,128)(2,1)S(1)}, u32[]{:S(2)}, u32[]{:S(2)}) collective-permute-start(bf16[48,2304]{1,0:T(8,128)(2,1)S(1)} %constant_dynamic-update-slice_fusion), channel_id=1, source_target_pairs={{0,4},{1,5},{2,6},{3,7},{4,0},{5,1},{6,2},{7,3},{8,12},{9,13},{10,... | collective-permute-start | bytes 663560 | tf_op jit(solution)/shard_map/ppermute | solution.py:17
  18.4 8.9 %collective-permute-start.8 = (bf16[48,2304]{1,0:T(8,128)(2,1)S(1)}, bf16[48,2304]{1,0:T(8,128)(2,1)S(1)}, u32[]{:S(2)}, u32[]{:S(2)}) collective-permute-start(bf16[48,2304]{1,0:T(8,128)(2,1)S(1)} %constant_dynamic-update-slice_fusion), channel_id=1, source_target_pairs={{0,6},{1,7},{2,4},{3,5},{4,2},{5,3},{6,0},{7,1},{8,14},{9,15},{10,... | collective-permute-start | bytes 663560 | tf_op jit(solution)/shard_map/ppermute | solution.py:17
  52.0 13.9 %collective-permute-start.14 = (bf16[64,1792]{1,0:T(8,128)(2,1)S(1)}, bf16[64,1792]{1,0:T(8,128)(2,1)S(1)}, u32[]{:S(2)}, u32[]{:S(2)}) collective-permute-start(bf16[64,1792]{1,0:T(8,128)(2,1)S(1)} %get-tuple-element.71), channel_id=1, source_target_pairs={{0,2},{1,3},{2,0},{3,1},{4,6},{5,7},{6,4},{7,5},{8,10},{9,11},{10,... | collective-permute-start | bytes 688136 | tf_op jit(solution)/shard_map/ppermute | solution.py:17
  53.3 12.6 %collective-permute-start.15 = (bf16[64,1792]{1,0:T(8,128)(2,1)S(1)}, bf16[64,1792]{1,0:T(8,128)(2,1)S(1)}, u32[]{:S(2)}, u32[]{:S(2)}) collective-permute-start(bf16[64,1792]{1,0:T(8,128)(2,1)S(1)} %get-tuple-element.73), channel_id=1, source_target_pairs={{0,4},{1,5},{2,6},{3,7},{4,0},{5,1},{6,2},{7,3},{8,12},{9,13},{10,... | collective-permute-start | bytes 688136 | tf_op jit(solution)/shard_map/ppermute | solution.py:17
  54.1 11.8 %collective-permute-start.16 = (bf16[64,1792]{1,0:T(8,128)(2,1)S(1)}, bf16[64,1792]{1,0:T(8,128)(2,1)S(1)}, u32[]{:S(2)}, u32[]{:S(2)}) collective-permute-start(bf16[64,1792]{1,0:T(8,128)(2,1)S(1)} %get-tuple-element.72), channel_id=1, source_target_pairs={{0,6},{1,7},{2,4},{3,5},{4,2},{5,3},{6,0},{7,1},{8,14},{9,15},{10,... | collective-permute-start | bytes 688136 | tf_op jit(solution)/shard_map/ppermute | solution.py:17
  81.8 17.7 %collective-permute-start.36 = (bf16[256,1792]{1,0:T(8,128)(2,1)}, bf16[256,1792]{1,0:T(8,128)(2,1)S(1)}, u32[]{:S(2)}, u32[]{:S(2)}) collective-permute-start(bf16[256,1792]{1,0:T(8,128)(2,1)} %collect.4.same), channel_id=1, source_target_pairs={{0,1},{1,0},{2,3},{3,2},{4,5},{5,4},{6,7},{7,6},{8,9},{9,8},{10,11... | collective-permute-start | bytes 2752520 | tf_op jit(solution)/shard_map/ppermute | solution.py:17
  97.3 14.9 %collective-permute-start.30 = (bf16[32,1792]{1,0:T(8,128)(2,1)S(1)}, bf16[32,1792]{1,0:T(8,128)(2,1)S(1)}, u32[]{:S(2)}, u32[]{:S(2)}) collective-permute-start(bf16[32,1792]{1,0:T(8,128)(2,1)S(1)} %slice.346), channel_id=1, source_target_pairs={{0,4},{1,5},{2,6},{3,7},{4,0},{5,1},{6,2},{7,3},{8,12},{9,13},{10,... | collective-permute-start | bytes 344072 | tf_op jit(solution)/shard_map/ppermute | solution.py:17
  98.9 13.3 %collective-permute-start.31 = (bf16[32,1792]{1,0:T(8,128)(2,1)S(1)}, bf16[32,1792]{1,0:T(8,128)(2,1)S(1)}, u32[]{:S(2)}, u32[]{:S(2)}) collective-permute-start(bf16[32,1792]{1,0:T(8,128)(2,1)S(1)} %slice.347), channel_id=1, source_target_pairs={{0,2},{1,3},{2,0},{3,1},{4,6},{5,7},{6,4},{7,5},{8,10},{9,11},{10,... | collective-permute-start | bytes 344072 | tf_op jit(solution)/shard_map/ppermute | solution.py:17
  115.2 28.7 %collective-permute-start.37 = (bf16[256,1792]{1,0:T(8,128)(2,1)}, bf16[256,1792]{1,0:T(8,128)(2,1)S(1)}, u32[]{:S(2)}, u32[]{:S(2)}) collective-permute-start(bf16[256,1792]{1,0:T(8,128)(2,1)} %collect.5.same), channel_id=1, source_target_pairs={{0,1},{1,0},{2,3},{3,2},{4,5},{5,4},{6,7},{7,6},{8,9},{9,8},{10,11... | collective-permute-start | bytes 2752520 | tf_op jit(solution)/shard_map/ppermute | solution.py:17
  115.2 13.8 %collective-permute-start.18 = (bf16[64,1792]{1,0:T(8,128)(2,1)S(1)}, bf16[64,1792]{1,0:T(8,128)(2,1)S(1)}, u32[]{:S(2)}, u32[]{:S(2)}) collective-permute-start(bf16[64,1792]{1,0:T(8,128)(2,1)S(1)} %copy-done.39), channel_id=1, source_target_pairs={{0,16},{8,24},{16,0},{24,8},{1,17},{9,25},{17,1},{25,9},{2,18},{10... | collective-permute-start | bytes 688136 | tf_op jit(solution)/shard_map/ppermute | solution.py:17
  137.0 20.2 %collective-permute-start.26 = (bf16[32,1792]{1,0:T(8,128)(2,1)}, bf16[32,1792]{1,0:T(8,128)(2,1)}, u32[]{:S(2)}, u32[]{:S(2)}) collective-permute-start(bf16[32,1792]{1,0:T(8,128)(2,1)} %slice.344), channel_id=1, source_target_pairs={{0,4},{1,5},{2,6},{3,7},{4,0},{5,1},{6,2},{7,3},{8,12},{9,13},{10,... | collective-permute-start | bytes 344072 | tf_op jit(solution)/shard_map/ppermute | solution.py:17
  139.0 18.2 %collective-permute-start.27 = (bf16[32,1792]{1,0:T(8,128)(2,1)}, bf16[32,1792]{1,0:T(8,128)(2,1)}, u32[]{:S(2)}, u32[]{:S(2)}) collective-permute-start(bf16[32,1792]{1,0:T(8,128)(2,1)} %slice.345), channel_id=1, source_target_pairs={{0,2},{1,3},{2,0},{3,1},{4,6},{5,7},{6,4},{7,5},{8,10},{9,11},{10,... | collective-permute-start | bytes 344072 | tf_op jit(solution)/shard_map/ppermute | solution.py:17
  141.4 19.7 %collective-permute-start.19 = (bf16[64,1792]{1,0:T(8,128)(2,1)}, bf16[64,1792]{1,0:T(8,128)(2,1)}, u32[]{:S(2)}, u32[]{:S(2)}) collective-permute-start(bf16[64,1792]{1,0:T(8,128)(2,1)} %hold.1), channel_id=1, source_target_pairs={{0,24},{8,16},{16,8},{24,0},{1,25},{9,17},{17,9},{25,1},{2,26},{10... | collective-permute-start | bytes 688136 | tf_op jit(solution)/shard_map/ppermute | solution.py:17
  159.5 13.9 %collective-permute-start.38 = (bf16[256,1792]{1,0:T(8,128)(2,1)}, bf16[256,1792]{1,0:T(8,128)(2,1)S(1)}, u32[]{:S(2)}, u32[]{:S(2)}) collective-permute-start(bf16[256,1792]{1,0:T(8,128)(2,1)} %collect.6.same), channel_id=1, source_target_pairs={{0,1},{1,0},{2,3},{3,2},{4,5},{5,4},{6,7},{7,6},{8,9},{9,8},{10,11... | collective-permute-start | bytes 2752520 | tf_op jit(solution)/shard_map/ppermute | solution.py:17
  162.5 9.4 %collective-permute-start.21 = (bf16[64,1792]{1,0:T(8,128)(2,1)}, bf16[64,1792]{1,0:T(8,128)(2,1)}, u32[]{:S(2)}, u32[]{:S(2)}) collective-permute-start(bf16[64,1792]{1,0:T(8,128)(2,1)} %collective-permute-done.19.refs_0_), channel_id=1, source_target_pairs={{0,4},{1,5},{2,6},{3,7},{4,0},{5,1},{6,2},{7,3},{8,12},{9,13},{10,... | collective-permute-start | bytes 688136 | tf_op jit(solution)/shard_map/ppermute | solution.py:17
  170.4 15.6 %collective-permute-start.22 = (bf16[32,1792]{1,0:T(8,128)(2,1)S(1)}, bf16[32,1792]{1,0:T(8,128)(2,1)S(1)}, u32[]{:S(2)}, u32[]{:S(2)}) collective-permute-start(bf16[32,1792]{1,0:T(8,128)(2,1)S(1)} %slice.342), channel_id=1, source_target_pairs={{0,4},{1,5},{2,6},{3,7},{4,0},{5,1},{6,2},{7,3},{8,12},{9,13},{10,... | collective-permute-start | bytes 344072 | tf_op jit(solution)/shard_map/ppermute | solution.py:17
  172.8 13.3 %collective-permute-start.23 = (bf16[32,1792]{1,0:T(8,128)(2,1)S(1)}, bf16[32,1792]{1,0:T(8,128)(2,1)S(1)}, u32[]{:S(2)}, u32[]{:S(2)}) collective-permute-start(bf16[32,1792]{1,0:T(8,128)(2,1)S(1)} %slice.343), channel_id=1, source_target_pairs={{0,2},{1,3},{2,0},{3,1},{4,6},{5,7},{6,4},{7,5},{8,10},{9,11},{10,... | collective-permute-start | bytes 344072 | tf_op jit(solution)/shard_map/ppermute | solution.py:17
  208.9 19.2 %collective-permute-start.40 = (bf16[64,7168]{1,0:T(8,128)(2,1)S(1)}, bf16[64,7168]{1,0:T(8,128)(2,1)}, u32[]{:S(2)}, u32[]{:S(2)}) collective-permute-start(bf16[64,7168]{1,0:T(8,128)(2,1)S(1)} %get-tuple-element.38.other), channel_id=1, source_target_pairs={{0,1},{1,0},{2,3},{3,2},{4,5},{5,4},{6,7},{7,6},{8,9},{9,8},{10,11... | collective-permute-start | bytes 2752520 | tf_op jit(solution)/shard_map/ppermute | solution.py:17
  220.5 11.1 %collective-permute-start.46 = (bf16[64,7168]{1,0:T(8,128)(2,1)S(1)}, bf16[64,7168]{1,0:T(8,128)(2,1)S(1)}, u32[]{:S(2)}, u32[]{:S(2)}) collective-permute-start(bf16[64,7168]{1,0:T(8,128)(2,1)S(1)} %get-tuple-element.40.other), channel_id=1, source_target_pairs={{0,1},{1,0},{2,3},{3,2},{4,5},{5,4},{6,7},{7,6},{8,9},{9,8},{10,11... | collective-permute-start | bytes 2752520 | tf_op jit(solution)/shard_map/ppermute | solution.py:17
  224.0 9.4 %collective-permute-start.52 = (bf16[64,7168]{1,0:T(8,128)(2,1)S(1)}, bf16[64,7168]{1,0:T(8,128)(2,1)S(1)}, u32[]{:S(2)}, u32[]{:S(2)}) collective-permute-start(bf16[64,7168]{1,0:T(8,128)(2,1)S(1)} %get-tuple-element.42.other), channel_id=1, source_target_pairs={{0,1},{1,0},{2,3},{3,2},{4,5},{5,4},{6,7},{7,6},{8,9},{9,8},{10,11... | collective-permute-start | bytes 2752520 | tf_op jit(solution)/shard_map/ppermute | solution.py:17
  239.5 10.1 %collective-permute-start.42 = (bf16[16,7168]{1,0:T(8,128)(2,1)S(1)}, bf16[16,7168]{1,0:T(8,128)(2,1)S(1)}, u32[]{:S(2)}, u32[]{:S(2)}) collective-permute-start(bf16[16,7168]{1,0:T(8,128)(2,1)S(1)} %pad_maximum_fusion.3), channel_id=1, source_target_pairs={{0,2},{1,3},{2,0},{3,1},{4,6},{5,7},{6,4},{7,5},{8,10},{9,11},{10,... | collective-permute-start | bytes 688136 | tf_op jit(solution)/shard_map/ppermute | solution.py:17
  240.7 9.9 %collective-permute-start.44 = (bf16[16,7168]{1,0:T(8,128)(2,1)S(1)}, bf16[16,7168]{1,0:T(8,128)(2,1)S(1)}, u32[]{:S(2)}, u32[]{:S(2)}) collective-permute-start(bf16[16,7168]{1,0:T(8,128)(2,1)S(1)} %pad_maximum_fusion.4), channel_id=1, source_target_pairs={{0,4},{1,5},{2,6},{3,7},{4,0},{5,1},{6,2},{7,3},{8,12},{9,13},{10,... | collective-permute-start | bytes 688136 | tf_op jit(solution)/shard_map/ppermute | solution.py:17
  242.2 12.3 %collective-permute-start.48 = (bf16[16,7168]{1,0:T(8,128)(2,1)S(1)}, bf16[16,7168]{1,0:T(8,128)(2,1)S(1)}, u32[]{:S(2)}, u32[]{:S(2)}) collective-permute-start(bf16[16,7168]{1,0:T(8,128)(2,1)S(1)} %pad_maximum_fusion.5), channel_id=1, source_target_pairs={{0,2},{1,3},{2,0},{3,1},{4,6},{5,7},{6,4},{7,5},{8,10},{9,11},{10,... | collective-permute-start | bytes 688136 | tf_op jit(solution)/shard_map/ppermute | solution.py:17
  242.7 12.8 %collective-permute-start.50 = (bf16[16,7168]{1,0:T(8,128)(2,1)S(1)}, bf16[16,7168]{1,0:T(8,128)(2,1)S(1)}, u32[]{:S(2)}, u32[]{:S(2)}) collective-permute-start(bf16[16,7168]{1,0:T(8,128)(2,1)S(1)} %pad_maximum_fusion.6), channel_id=1, source_target_pairs={{0,4},{1,5},{2,6},{3,7},{4,0},{5,1},{6,2},{7,3},{8,12},{9,13},{10,... | collective-permute-start | bytes 688136 | tf_op jit(solution)/shard_map/ppermute | solution.py:17
  244.6 14.7 %collective-permute-start.54 = (bf16[16,7168]{1,0:T(8,128)(2,1)S(1)}, bf16[16,7168]{1,0:T(8,128)(2,1)S(1)}, u32[]{:S(2)}, u32[]{:S(2)}) collective-permute-start(bf16[16,7168]{1,0:T(8,128)(2,1)S(1)} %pad_maximum_fusion.7), channel_id=1, source_target_pairs={{0,2},{1,3},{2,0},{3,1},{4,6},{5,7},{6,4},{7,5},{8,10},{9,11},{10,... | collective-permute-start | bytes 688136 | tf_op jit(solution)/shard_map/ppermute | solution.py:17
  249.6 9.8 %collective-permute-start.56 = (bf16[16,7168]{1,0:T(8,128)(2,1)S(1)}, bf16[16,7168]{1,0:T(8,128)(2,1)S(1)}, u32[]{:S(2)}, u32[]{:S(2)}) collective-permute-start(bf16[16,7168]{1,0:T(8,128)(2,1)S(1)} %pad_maximum_fusion.8), channel_id=1, source_target_pairs={{0,4},{1,5},{2,6},{3,7},{4,0},{5,1},{6,2},{7,3},{8,12},{9,13},{10,... | collective-permute-start | bytes 688136 | tf_op jit(solution)/shard_map/ppermute | solution.py:17
  250.6 12.6 %collective-permute-start.60 = (bf16[16,7168]{1,0:T(8,128)(2,1)S(1)}, bf16[16,7168]{1,0:T(8,128)(2,1)S(1)}, u32[]{:S(2)}, u32[]{:S(2)}) collective-permute-start(bf16[16,7168]{1,0:T(8,128)(2,1)S(1)} %pad_maximum_fusion.9), channel_id=1, source_target_pairs={{0,2},{1,3},{2,0},{3,1},{4,6},{5,7},{6,4},{7,5},{8,10},{9,11},{10,... | collective-permute-start | bytes 688136 | tf_op jit(solution)/shard_map/ppermute | solution.py:17
  254.5 8.7 %collective-permute-start.62 = (bf16[16,7168]{1,0:T(8,128)(2,1)S(1)}, bf16[16,7168]{1,0:T(8,128)(2,1)S(1)}, u32[]{:S(2)}, u32[]{:S(2)}) collective-permute-start(bf16[16,7168]{1,0:T(8,128)(2,1)S(1)} %pad_maximum_fusion.10), channel_id=1, source_target_pairs={{0,4},{1,5},{2,6},{3,7},{4,0},{5,1},{6,2},{7,3},{8,12},{9,13},{10,... | collective-permute-start | bytes 688136 | tf_op jit(solution)/shard_map/ppermute | solution.py:17
  255.5 10.3 %collective-permute-start.45 = (bf16[16,7168]{1,0:T(8,128)(2,1)S(1)}, bf16[16,7168]{1,0:T(8,128)(2,1)S(1)}, u32[]{:S(2)}, u32[]{:S(2)}) collective-permute-start(bf16[16,7168]{1,0:T(8,128)(2,1)S(1)} %fusion.8), channel_id=1, source_target_pairs={{0,24},{8,16},{16,8},{24,0},{1,25},{9,17},{17,9},{25,1},{2,26},{10... | collective-permute-start | bytes 688136 | tf_op jit(solution)/shard_map/ppermute | solution.py:17
  259.4 13.9 %collective-permute-start.51 = (bf16[16,7168]{1,0:T(8,128)(2,1)S(1)}, bf16[16,7168]{1,0:T(8,128)(2,1)S(1)}, u32[]{:S(2)}, u32[]{:S(2)}) collective-permute-start(bf16[16,7168]{1,0:T(8,128)(2,1)S(1)} %fusion.6), channel_id=1, source_target_pairs={{0,16},{8,24},{16,0},{24,8},{1,17},{9,25},{17,1},{25,9},{2,18},{10... | collective-permute-start | bytes 688136 | tf_op jit(solution)/shard_map/ppermute | solution.py:17
  259.5 13.8 %collective-permute-start.57 = (bf16[16,7168]{1,0:T(8,128)(2,1)S(1)}, bf16[16,7168]{1,0:T(8,128)(2,1)S(1)}, u32[]{:S(2)}, u32[]{:S(2)}) collective-permute-start(bf16[16,7168]{1,0:T(8,128)(2,1)S(1)} %fusion.4), channel_id=1, source_target_pairs={{0,8},{8,0},{16,24},{24,16},{1,9},{9,1},{17,25},{25,17},{2,10},{10... | collective-permute-start | bytes 688136 | tf_op jit(solution)/shard_map/ppermute | solution.py:17
  (102 other events, 653.3 us)

commit v3 on v1

--- a/solution.py
+++ b/solution.py
@@ -15,10 +15,6 @@
 def swap(x, axis, distance):
     size = lax.axis_size(axis)
     return lax.ppermute(x, axis, [(i, i ^ distance) for i in range(size)])
-
-
-def after(x, *others):
-    return lax.optimization_barrier((x,) + others)[0]
 
 
 def pick_kernel(plan, place, lists, pool, *outs):
@@ -75,7 +71,7 @@
 
 
 def attention_kernel(
-    plan, place, near, far, new, q_even, q_odd, bias_even, bias_odd, bias_new, uv, out,
+    plan, place, near, far, new, q_even, q_odd, bias_even, bias_odd, bias_new, uv, extra, out,
     k_even, k_odd, s_even, s_odd, heads,
 ):
     per_index, latent, kv_rank, head_here, tok_rows, order, own_rows = plan
@@ -137,15 +133,99 @@
             uv[h],
             preferred_element_type=jnp.float32,
         )
+    out[tok_rows:, :] = extra[...]
     if own_rows % 8:
-        out[...] = heads[...].astype(jnp.bfloat16)
+        out[:tok_rows, :] = heads[...].astype(jnp.bfloat16)
         return
     exp_index = place[1]
     blocks = []
     for m in order:
         at = (exp_index ^ m) * own_rows
         blocks.append(heads[pl.ds(pl.multiple_of(at, 8), own_rows), :])
-    out[...] = jnp.concatenate(blocks, axis=0).astype(jnp.bfloat16)
+    out[:tok_rows, :] = jnp.concatenate(blocks, axis=0).astype(jnp.bfloat16)
+
+
+def hold_kernel(x, other, out):
+    del other
+    out[...] = x[...]
+
+
+def collect_kernel(count, *refs):
+    out, base = refs[-1], 0
+    for ref in refs[:count]:
+        out[base : base + ref.shape[0], :] = ref[...]
+        base += ref.shape[0]
+
+
+def project_kernel(plan, *refs):
+    req_count, exp_count, own_rows = plan
+    heads, (weight, keep, give, rows, held, sem) = refs[:req_count], refs[req_count:]
+    fetch = pltpu.make_async_copy(weight, held, sem)
+    fetch.start()
+    for j in range(req_count):
+        for m in range(exp_count):
+            at = (m * req_count + j) * own_rows
+            rows[at : at + own_rows, :] = heads[j][m * own_rows : (m + 1) * own_rows, :]
+    fetch.wait()
+    half = keep.shape[0]
+    for n in range(0, keep.shape[1], 256):
+        cols = slice(n, n + 256)
+        out = jnp.dot(rows[...], held[:, cols], preferred_element_type=jnp.float32)
+        keep[:, cols] = out[:half]
+        give[:, cols] = out[half:].astype(jnp.bfloat16)
+
+
+def pair_kernel(keep, got, *outs):
+    rows = outs[0].shape[0]
+    for k, out in enumerate(outs):
+        at = slice(k * rows, (k + 1) * rows)
+        out[...] = (keep[at, :] + got[at, :].astype(jnp.float32)).astype(out.dtype)
+
+
+def hidden_kernel(req_count, place, hidden, other, *outs):
+    del other
+    columns = outs[0].shape[1]
+    for j in range(req_count):
+        start = pl.multiple_of((place[0] ^ j) * columns, 128)
+        outs[j][...] = hidden[:, pl.ds(start, columns)]
+
+
+def resid_kernel(own, *refs):
+    req_count = 4
+    sums, hidden, outs = refs[:3], refs[3 : 3 + req_count], refs[3 + req_count :]
+    rows = hidden[0].shape[0]
+    in_chunk = req_count // len(outs)
+    for j in range(req_count):
+        at = slice(j * rows, (j + 1) * rows)
+        total = own[at, :]
+        for ref in sums:
+            total = total + ref[at, :].astype(jnp.float32)
+        total = (hidden[j][...].astype(jnp.float32) + total).astype(jnp.bfloat16)
+        to = j % in_chunk * rows
+        outs[j // in_chunk][to : to + rows, :] = total
+
+
+def norm_kernel(plan, place, gain, *refs):
+    req_count, own_rows, others = plan
+    pieces, (left, right, first, full) = refs[:req_count], refs[req_count + others :]
+    rows, columns = pieces[0].shape
+    in_chunk = rows // own_rows
+    width = columns * req_count
+    for b, piece in enumerate(pieces):
+        start = pl.multiple_of((place[0] ^ b) * columns, 128)
+        for n in range(in_chunk):
+            m = n ^ (b % in_chunk)
+            got = piece[m * own_rows : (m + 1) * own_rows, :]
+            full[n * own_rows : (n + 1) * own_rows, pl.ds(start, columns)] = got
+    first[...] = full[:own_rows, :]
+    half = width // 2
+    for n in range(in_chunk):
+        at = slice(n * own_rows, (n + 1) * own_rows)
+        widened = full[at, :].astype(jnp.float32)
+        mean = jnp.sum(widened * widened, axis=-1, keepdims=True) / width
+        normed = (widened * lax.rsqrt(mean + norm_eps) * gain[...]).astype(jnp.bfloat16)
+        left[at, :] = normed[:, :half]
+        right[at, :] = normed[:, half:]
 
 
 def local(
@@ -229,17 +309,17 @@
 
     chosen = route_ids == exp_index
     token_weight = jnp.sum(jnp.where(chosen, route_weight, 0.0), axis=1)
-    token_weight = token_weight.reshape(exp_count, own_rows)[exp_rel]
-    behind = [after(token_weight, far)] * (req_count - 1)
-    weight_all = jnp.stack(
-        [token_weight] + [swap(behind[j - 1], "req", j) for j in range(1, req_count)], axis=1
-    )
-    hidden_cols = []
-    for j in range(req_count):
-        piece = lax.dynamic_slice_in_dim(hidden_in, req_rel[j] * col_width, col_width, 1)
-        hidden_cols.append(piece if j == 0 else swap(after(piece, far), "req", j))
-    hidden_cols = jnp.concatenate(hidden_cols, axis=0)
-    near, hidden_cols, weight_all = lax.optimization_barrier((near, hidden_cols, weight_all))
+    token_weight = token_weight.reshape(exp_count, own_rows)[exp_rel].reshape(-1)
+    parts, left = [], token_weight
+    for n in range(3):
+        part = lax.reduce_precision(left, 8, 7)
+        left = left - part
+        parts.append(part.astype(jnp.bfloat16))
+    head_cols = head_here * value_width
+    extra_rows = -(-3 * tok_rows // (16 * head_cols)) * 16
+    extra = jnp.concatenate(parts)
+    extra = jnp.pad(extra, (0, extra_rows * head_cols - 3 * tok_rows))
+    extra = extra.reshape(extra_rows, head_cols)
 
     near_piece = page_size // near_split
     pairs = np.arange(near_piece // 2)[:, None]
@@ -274,7 +354,6 @@
     new_keys = jnp.pad(new_latent, ((0, 0), (0, 64)))
     key_count = key_req.shape[1]
     q_rows = head_here * tok_rows
-    head_cols = head_here * value_width
     head_out = pl.pallas_call(
         functools.partial(
             attention_kernel,
@@ -282,8 +361,8 @@
                 per_index, latent, kv_rank, head_here, tok_rows, tuple(rel_order), own_rows,
             ),
         ),
-        out_shape=jax.ShapeDtypeStruct((tok_rows, head_cols), jnp.bfloat16),
-        in_specs=[scalars] + [whole] * 9,
+        out_shape=jax.ShapeDtypeStruct((tok_rows + extra_rows, head_cols), jnp.bfloat16),
+        in_specs=[scalars] + [whole] * 10,
         out_specs=whole,
         scratch_shapes=[
             pltpu.VMEM((key_count, latent + 64), jnp.bfloat16),
@@ -292,35 +371,144 @@
             pltpu.VMEM((q_rows, key_count), jnp.float32),
             pltpu.VMEM((tok_rows, head_cols), jnp.float32),
         ],
-        compiler_params=pltpu.CompilerParams(vmem_limit_bytes=40 * 1024 * 1024),
+        compiler_params=pltpu.CompilerParams(vmem_limit_bytes=12 * 1024 * 1024),
         name="attention",
-    )(place, near, far_all, new_keys, q_even, q_odd, bias_even, bias_odd, bias_new, uv_weight)
-    head_out = head_out.reshape(exp_count, own_rows, head_cols)
+    )(place, near, far_all, new_keys, q_even, q_odd, bias_even, bias_odd, bias_new, uv_weight, extra)
     if own_rows % 8:
-        head_out = head_out[exp_rel]
-
-    heads_all = jnp.stack(
-        [head_out] + [swap(head_out, "req", j) for j in range(1, req_count)], axis=1
-    )
+        ordered = head_out[:tok_rows].reshape(exp_count, own_rows, head_cols)[exp_rel]
+        head_out = jnp.concatenate([ordered.reshape(tok_rows, head_cols), head_out[tok_rows:]])
+
+    heads = [head_out] + [swap(head_out, "req", j) for j in range(1, req_count)]
+    weight_all = jnp.stack([h[tok_rows:].reshape(-1)[: 3 * tok_rows] for h in heads])
+    weight_all = weight_all.astype(jnp.float32).reshape(req_count, 3, exp_count, own_rows)
+    weight_all = (weight_all[:, 0] + weight_all[:, 1] + weight_all[:, 2]).transpose(1, 0, 2)
     block = req_count * own_rows
-    partial = jnp.dot(
-        heads_all.reshape(exp_count * block, head_cols),
-        out_weight,
-        preferred_element_type=jnp.float32,
-    )
+    aligned = own_rows % 16 == 0 and outer == 4
+    somewhere = pl.BlockSpec(memory_space=pl.ANY)
+    in_hbm = pl.BlockSpec(memory_space=pltpu.HBM)
     cut = outer * block
-    other = swap(partial[cut:].astype(jnp.bfloat16), "exp", 1)
-    pair_sum = (partial[:cut] + other.astype(jnp.float32)).reshape(outer, block, col_width)
-    attn = pair_sum[0]
-    for k in range(1, outer):
-        attn = attn + swap(pair_sum[k].astype(jnp.bfloat16), "exp", 2 * k).astype(jnp.float32)
-    resid = (hidden_cols.astype(jnp.float32) + attn).astype(jnp.bfloat16)
-
-    pieces = [resid]
-    for b in range(1, req_count):
-        got = swap(resid if b < 3 else after(resid, pieces[b - 2]), "req", b)
-        got = got.reshape(req_count, own_rows, col_width)
-        pieces.append(jnp.concatenate([got[i ^ b] for i in range(req_count)], axis=0))
+
+    def grant(mib):
+        return pltpu.CompilerParams(vmem_limit_bytes=mib * 1024 * 1024)
+
+    def pair_blocks(keep, got):
+        rows, columns = keep.shape[0] // 4, keep.shape[1]
+        return pl.pallas_call(
+            pair_kernel,
+            out_shape=[jax.ShapeDtypeStruct((rows, columns), jnp.float32)]
+            + [jax.ShapeDtypeStruct((rows, columns), jnp.bfloat16)] * 3,
+            in_specs=[whole, whole],
+            out_specs=[whole] * 4,
+            compiler_params=grant(4),
+            name="pair",
+        )(keep, got)
+
+    if aligned:
+        keep, give = pl.pallas_call(
+            functools.partial(project_kernel, (req_count, exp_count, own_rows)),
+            out_shape=[
+                jax.ShapeDtypeStruct((cut, col_width), jnp.float32),
+                jax.ShapeDtypeStruct((cut, col_width), jnp.bfloat16),
+            ],
+            in_specs=[whole] * req_count + [in_hbm],
+            out_specs=[whole, whole],
+            scratch_shapes=[
+                pltpu.VMEM((2 * cut, head_cols), jnp.bfloat16),
+                pltpu.VMEM(out_weight.shape, jnp.bfloat16),
+                pltpu.SemaphoreType.DMA,
+            ],
+            compiler_params=grant(6),
+            name="project",
+        )(*heads, out_weight)
+        parts = pair_blocks(keep, swap(give, "exp", 1))
+    else:
+        heads_all = jnp.stack(
+            [h[:tok_rows].reshape(exp_count, own_rows, head_cols) for h in heads], axis=1
+        )
+        partial = jnp.dot(
+            heads_all.reshape(exp_count * block, head_cols),
+            out_weight,
+            preferred_element_type=jnp.float32,
+        )
+        other = swap(partial[cut:].astype(jnp.bfloat16), "exp", 1)
+        parts = partial[:cut] + other.astype(jnp.float32)
+        parts = list(parts.reshape(outer, block, col_width))
+    chunks = 2
+    in_chunk = req_count // chunks
+    chunk_block = in_chunk * own_rows
+    along = [swap(parts[k].astype(jnp.bfloat16), "exp", 2 * k) for k in range(1, outer)]
+
+    def collect(blocks, others):
+        rows = sum(x.shape[0] for x in blocks)
+        return pl.pallas_call(
+            functools.partial(collect_kernel, len(blocks)),
+            out_shape=jax.ShapeDtypeStruct((rows, blocks[0].shape[1]), blocks[0].dtype),
+            in_specs=[whole] * len(blocks) + [somewhere] * len(others),
+            out_specs=whole,
+            compiler_params=grant(2),
+            name="collect",
+        )(*blocks, *others)
+
+    if aligned and in_chunk == 2:
+        hidden = pl.pallas_call(
+            functools.partial(hidden_kernel, req_count),
+            out_shape=[jax.ShapeDtypeStruct((own_rows, col_width), jnp.bfloat16)] * req_count,
+            in_specs=[scalars, whole, somewhere],
+            out_specs=[whole] * req_count,
+            compiler_params=grant(2),
+            name="hidden",
+        )(place, hidden_in, parts[0])
+        hidden = [x if j == 0 else swap(x, "req", j) for j, x in enumerate(hidden)]
+        resid = pl.pallas_call(
+            resid_kernel,
+            out_shape=[jax.ShapeDtypeStruct((chunk_block, col_width), jnp.bfloat16)] * chunks,
+            in_specs=[whole] * (4 + req_count),
+            out_specs=[whole] * chunks,
+            compiler_params=grant(2),
+            name="resid",
+        )(parts[0], *along, *hidden)
+        gain = norm_gain.astype(jnp.float32).reshape(1, width)
+
+        def normalise(c, after_slices, after_norm):
+            sent = resid
+            if after_slices:
+                sent = [collect([x], after_slices) for x in resid]
+            slices = [resid[c]]
+            for b in range(1, req_count):
+                slices.append(swap(sent[c ^ b // in_chunk], "req", b))
+            half_shape = jax.ShapeDtypeStruct((chunk_block, half_width), jnp.bfloat16)
+            *halves, first = pl.pallas_call(
+                functools.partial(norm_kernel, (req_count, own_rows, len(after_norm))),
+                out_shape=[half_shape, half_shape]
+                + [jax.ShapeDtypeStruct((own_rows, width), jnp.bfloat16)],
+                in_specs=[scalars] + [whole] * (1 + req_count) + [somewhere] * len(after_norm),
+                out_specs=[whole] * 3,
+                scratch_shapes=[pltpu.VMEM((chunk_block, width), jnp.bfloat16)],
+                compiler_params=grant(4),
+                name="norm",
+            )(place, gain, *slices, *after_norm)
+            return slices, halves, first
+    else:
+        hidden = [
+            lax.dynamic_slice_in_dim(hidden_in, req_rel[j] * col_width, col_width, 1)
+            for j in range(req_count)
+        ]
+        hidden = [x if j == 0 else swap(x, "req", j) for j, x in enumerate(hidden)]
+        attn = sum([x.astype(jnp.float32) for x in along], parts[0])
+        resid = jnp.concatenate(hidden, axis=0).astype(jnp.float32) + attn
+        resid = resid.astype(jnp.bfloat16)
+        pieces = [resid]
+        for b in range(1, req_count):
+            got = swap(resid, "req", b).reshape(req_count, own_rows, col_width)
+            pieces.append(jnp.concatenate([got[i ^ b] for i in range(req_count)], axis=0))
+        full = jnp.stack(pieces)[req_rel].transpose(1, 0, 2).reshape(block, width)
+        widened = full.astype(jnp.float32)
+        inv_scale = lax.rsqrt(jnp.mean(widened * widened, axis=-1, keepdims=True) + norm_eps)
+        normed = (widened * inv_scale * norm_gain.astype(jnp.float32)).astype(jnp.bfloat16)
+        normed = normed.reshape(chunks, chunk_block, 2, half_width)
+
+        def normalise(c, after_slices, after_norm):
+            return [], [normed[c, :, n] for n in range(2)], full[:own_rows]
 
     outer_bits = []
     bit = 1
@@ -329,86 +517,71 @@
         bit *= 2
     orders = (outer_bits, outer_bits[::-1])
 
-    def gather_side(piece, bits):
+    def gather_plane(piece, bits, others):
         held = piece[None]
         ids = [0]
+        firsts = []
         for bit in bits:
-            held = jnp.concatenate([held, swap(held, "exp", 2 * bit)], axis=0)
+            firsts.append(swap(held, "exp", 2 * bit))
+            held = jnp.concatenate([held, firsts[-1]], axis=0)
             ids = ids + [k ^ bit for k in ids]
-        return [held[ids.index(k)] for k in range(outer)]
-
-    def gather_plane(piece):
-        half = piece.shape[0] // 2
-        first = gather_side(piece[:half], orders[0])
-        second = gather_side(piece[half:], orders[1])
-        same = jnp.concatenate([p for pair in zip(first, second) for p in pair], axis=0)
-        return jnp.concatenate([same, swap(same, "exp", 1)], axis=0)
+        same = [held[ids.index(k)] for k in range(outer)]
+        same = collect(same, others) if others else jnp.concatenate(same, axis=0)
+        return jnp.concatenate([same, swap(same, "exp", 1)], axis=0), firsts[0]
+
+    def scatter_plane(partial, bits):
+        cut = outer * chunk_block
+        other = swap(partial[cut:].astype(jnp.bfloat16), "exp", 1)
+        held = (partial[:cut] + other.astype(jnp.float32)).reshape(outer, chunk_block, half_width)
+        ids = list(range(outer))
+        firsts = []
+        for bit in bits:
+            keep = [n for n, k in enumerate(ids) if not k & bit]
+            give = [ids.index(ids[n] ^ bit) for n in keep]
+            sent = swap(jnp.stack([held[n] for n in give]).astype(jnp.bfloat16), "exp", 2 * bit)
+            firsts.append(sent)
+            held = jnp.stack([held[n] for n in keep]) + sent.astype(jnp.float32)
+            ids = [ids[n] for n in keep]
+        return held[0].astype(jnp.bfloat16), firsts[0]
 
     gate_here = gate_weight[0]
     up_here = up_weight[0]
     down_here = down_weight[0]
-    gain = norm_gain.astype(jnp.float32)
-    gate_val = up_val = squares = 0.0
-    span = max(1, req_count // 4)
-    slices = []
-    for b in range(0, req_count, span):
-        rows = gather_plane(jnp.concatenate(pieces[b : b + span], axis=0))
-        rows = rows.reshape(exp_count, span, block, col_width)
-        slices += [rows[:, n].reshape(exp_count * block, col_width) for n in range(span)]
-    for b in range(req_count):
-        start = req_rel[b] * col_width
-        rows = slices[b].astype(jnp.float32)
-        squares = squares + jnp.sum(rows * rows, axis=-1, keepdims=True)
-        scaled = (rows * lax.dynamic_slice_in_dim(gain, start, col_width)).astype(jnp.bfloat16)
-        gate_val = gate_val + jnp.dot(
-            scaled,
-            lax.dynamic_slice_in_dim(gate_here, start, col_width),
-            preferred_element_type=jnp.float32,
+    total = 0.0
+    slices, arrived, before_gather, before_down = [], [], [], []
+    for c in reversed(range(chunks)):
+        slices, halves, resid_own = normalise(c, slices[1:], arrived)
+        (left, *arrived), (right, *last) = (
+            gather_plane(halves[n], orders[n], before_gather) for n in range(2)
         )
-        up_val = up_val + jnp.dot(
-            scaled,
-            lax.dynamic_slice_in_dim(up_here, start, col_width),
-            preferred_element_type=jnp.float32,
-        )
-    inv_scale = lax.rsqrt(squares / width + norm_eps)
-    active = (jax.nn.silu(gate_val * inv_scale) * (up_val * inv_scale)).astype(jnp.bfloat16)
-    active = active.reshape(exp_count, req_count, own_rows, -1)
-
-    def scatter_side(held, bits):
-        ids = list(range(outer))
-        for bit in bits:
-            keep = [n for n, k in enumerate(ids) if not k & bit]
-            give = [ids.index(ids[n] ^ bit) for n in keep]
-            sent = jnp.stack([held[n] for n in give]).astype(jnp.bfloat16)
-            held = jnp.stack([held[n] for n in keep]) + swap(sent, "exp", 2 * bit).astype(
-                jnp.float32
-            )
-            ids = [ids[n] for n in keep]
-        return held[0].astype(jnp.bfloat16)
-
-    own = jnp.stack([piece[:own_rows] for piece in pieces])[req_rel]
-    total = own.transpose(1, 0, 2).reshape(own_rows, width).astype(jnp.float32)
-    previous = None
-    for j in reversed(range(0, req_count, span)):
-        rows = active[:, j : j + span].reshape(span * tok_rows, -1)
-        if previous is not None:
-            rows = after(rows, previous)
-        out = jnp.dot(rows, down_here, preferred_element_type=jnp.float32)
-        out = out * weight_all[:, j : j + span].reshape(span * tok_rows, 1)
-        cut = span * tok_rows // 2
-        previous = out[cut:].astype(jnp.bfloat16)
-        pair_sum = out[:cut] + swap(previous, "exp", 1).astype(jnp.float32)
-        pair_sum = pair_sum.reshape(outer, span * own_rows, width)
-        sums = [
-            scatter_side(pair_sum[:, :, :half_width], orders[0]),
-            scatter_side(pair_sum[:, :, half_width:], orders[1]),
-        ]
-        sums = jnp.concatenate(sums, axis=1)
-        for n in reversed(range(span)):
+        arrived = arrived + last
+
+        def project(matrix):
+            return jnp.dot(
+                left, matrix[:half_width], preferred_element_type=jnp.float32
+            ) + jnp.dot(right, matrix[half_width:], preferred_element_type=jnp.float32)
+
+        active = (jax.nn.silu(project(gate_here)) * project(up_here)).astype(jnp.bfloat16)
+        if before_down:
+            active = collect([active], before_down)
+        reqs = range(c * in_chunk, (c + 1) * in_chunk)
+        row_weight = weight_all[:, reqs[0] : reqs[-1] + 1].reshape(-1, 1)
+        sides, before_gather, before_down = [], [], []
+        for n in range(2):
+            cols = slice(n * half_width, (n + 1) * half_width)
+            out = jnp.dot(active, down_here[:, cols], preferred_element_type=jnp.float32)
+            out = out * row_weight
+            before_gather.append(out)
+            side, first = scatter_plane(out, orders[n])
+            sides.append(side)
+            before_down.append(first)
+        sums = jnp.concatenate(sides, axis=1)
+        for n, j in reversed(list(enumerate(reqs))):
             part = sums[n * own_rows : (n + 1) * own_rows]
-            part = swap(part, "req", j + n) if j + n else part
+            if j:
+                part = swap(part, "req", j)
             total = total + part.astype(jnp.float32)
-    return total.astype(jnp.bfloat16)
+    return (total + resid_own.astype(jnp.float32)).astype(jnp.bfloat16)
 
 
 def solution(mesh):

time: 214 us -> 177 us (0.83)
  local copies, waits for them, and re-layouts: 29.1 us -> 5.86 us
  starting transfers between devices: 68.3 us -> 52.9 us
  waiting for transfers between devices: 76 us -> 85.2 us
  other arithmetic: 10.1 us -> 4.12 us
  Pallas kernels: 8.86 us -> 14.1 us
  between operations: 4.21 us -> 1.12 us
  matrix products: 16.6 us -> 13.7 us
    unnamed x134 -> x71, local copies, waits for them, and re-layouts: 18.1 us -> 2.6 us
    ppermute x66 -> x50, starting transfers between devices: 68.3 us -> 52.9 us  [swap(): return lax.ppermute(x, axis, [(i, i ^ distance) for i in range(size)])]
    ppermute x66 -> x50, waiting for transfers between devices: 76 us -> 85.2 us  [swap(): return lax.ppermute(x, axis, [(i, i ^ distance) for i in range(size)])]
    pallas_call x0 -> x11, Pallas kernels: none -> 5.26 us  [the longest x2 2.25 us: normalise(): pl.pallas_call(functools.partial(norm_kernel, (req_count, own_rows, len(a...]
    concatenate x12 -> x9, other arithmetic: 3.58 us -> 0.36 us  [the longest x4 0.17 us: gather_plane(): held = jnp.concatenate([held, firsts[-1]], axis=0)]
    dot_general x13 -> x12, matrix products: 16.6 us -> 13.7 us  [the longest x4 4.74 us: project(): jnp.dot(left, matrix[:half_width], preferred_element_type=jnp.float32)]
    slice x28 -> x23, local copies, waits for them, and re-layouts: 3.61 us -> 0.87 us  [the longest x4 0.37 us: scatter_plane(): other = swap(partial[cut:].astype(jnp.bfloat16), 'exp', 1)]
    mul x4 -> x2, local copies, waits for them, and re-layouts: 2.54 us -> 0.18 us  [local(): out = out * row_weight]
  transfers between devices with their start and end apart: 66 -> 50, of which waited for: 25 -> 30; matrix products, arithmetic and copies ran while one was open for 20% -> 11% of each run, Pallas kernels for 1% -> 3%
where the time goes in v3:
time: 177 us
  waiting for transfers between devices  85.2 us (48%)
  starting transfers between devices  52.9 us (30%)
  Pallas kernels  14.1 us (8%)
  matrix products  13.7 us (8%)
  local copies, waits for them, and re-layouts  5.86 us (3%)
  other arithmetic  4.12 us (2%)
    ppermute x50, waiting for transfers between devices, swap(): return lax.ppermute(x, axis, [(i, i ^ distance) for i in range(size)])  85.2 us
    ppermute x50, starting transfers between devices, swap(): return lax.ppermute(x, axis, [(i, i ^ distance) for i in range(size)])  52.9 us
    dot_general x4, matrix products, project(): jnp.dot(left, matrix[:half_width], preferred_element_type=jnp.float32)  4.74 us
    dot_general x4, matrix products, local(): jnp.dot(active, down_here[:, cols], preferred_element_type=jnp.float32)  4.53 us
    dot_general x4, matrix products, project(): jnp.dot(right, matrix[half_width:], preferred_element_type=jnp.float32)  4.41 us
  transfers between devices with their start and end apart: 50, of which 30 were waited for; matrix products, arithmetic and copies ran while one was open for 11% of the time, Pallas kernels for 3%

profile of v3, /device:TPU:0, one launch (start us, length us, event | category | flops | bytes accessed | tf_op | source)
XLA Modules:
  0.0 177.0 jit_solution(17695641923499370856)
XLA Ops:
  0.6 2.6 %pick_far.1 = (bf16[16,2304]{1,0:T(8,128)(2,1)}, bf16[16,2304]{1,0:T(8,128)(2,1)}, bf16[16,2304]{1,0:T(8,128)(2,1)}) custom-call(s32[2]{0:T(128)} %pad_add_fusion.1.place, s32[8,16]{1,0:T(8,128)} %lists.3, bf16[32,36864]{1,0:T(8,128)(2,1)} %pool.3), custom_call_target="tpu_custom_call" | custom-call | tf_op jit(solution)/shard_map/pick_far/pallas_call | solution.py:284
  3.3 3.1 %collective-permute-start = (bf16[16,2304]{1,0:T(8,128)(2,1)}, bf16[16,2304]{1,0:T(8,128)(2,1)S(1)}, u32[]{:S(2)}, u32[]{:S(2)}) collective-permute-start(bf16[16,2304]{1,0:T(8,128)(2,1)} %get-tuple-element.25), channel_id=1, source_target_pairs={{0,8},{8,0},{16,24},{24,16},{1,9},{9,1},{17,25},{25,17},{2,10},{10... | collective-permute-start | bytes 221192 | tf_op jit(solution)/shard_map/ppermute | solution.py:17
  6.4 2.6 %collective-permute-start.1 = (bf16[16,2304]{1,0:T(8,128)(2,1)}, bf16[16,2304]{1,0:T(8,128)(2,1)S(1)}, u32[]{:S(2)}, u32[]{:S(2)}) collective-permute-start(bf16[16,2304]{1,0:T(8,128)(2,1)} %get-tuple-element.26), channel_id=1, source_target_pairs={{0,16},{8,24},{16,0},{24,8},{1,17},{9,25},{17,1},{25,9},{2,18},{10... | collective-permute-start | bytes 221192 | tf_op jit(solution)/shard_map/ppermute | solution.py:17
  9.7 3.0 %pick_near.1.near = bf16[16,18432]{1,0:T(8,128)(2,1)} custom-call(s32[2]{0:T(128)} %pad_add_fusion.1.place, s32[8,16]{1,0:T(8,128)} %lists.3, bf16[32,36864]{1,0:T(8,128)(2,1)} %pool.3), custom_call_target="tpu_custom_call" | custom-call | tf_op jit(solution)/shard_map/pick_near/pallas_call | solution.py:295
  15.4 2.4 %collective-permute-start.5 = (bf16[48,2304]{1,0:T(8,128)(2,1)S(1)}, bf16[48,2304]{1,0:T(8,128)(2,1)S(1)}, u32[]{:S(2)}, u32[]{:S(2)}) collective-permute-start(bf16[48,2304]{1,0:T(8,128)(2,1)S(1)} %constant_dynamic-update-slice_fusion), channel_id=1, source_target_pairs={{0,6},{1,7},{2,4},{3,5},{4,2},{5,3},{6,0},{7,1},{8,14},{9,15},{10,... | collective-permute-start | bytes 663560 | tf_op jit(solution)/shard_map/ppermute | solution.py:17
  18.9 5.7 %collective-permute-done.5 = bf16[48,2304]{1,0:T(8,128)(2,1)S(1)} collective-permute-done((bf16[48,2304]{1,0:T(8,128)(2,1)S(1)}, bf16[48,2304]{1,0:T(8,128)(2,1)S(1)}, u32[]{:S(2)}, u32[]{:S(2)}) %collective-permute-start.5) | collective-permute-done | bytes 221216 | tf_op jit(solution)/shard_map/ppermute | solution.py:17
  24.6 2.3 %collective-permute-done.4 = bf16[48,2304]{1,0:T(8,128)(2,1)S(1)} collective-permute-done((bf16[48,2304]{1,0:T(8,128)(2,1)S(1)}, bf16[48,2304]{1,0:T(8,128)(2,1)S(1)}, u32[]{:S(2)}, u32[]{:S(2)}) %collective-permute-start.4) | collective-permute-done | bytes 221216 | tf_op jit(solution)/shard_map/ppermute | solution.py:17
  27.4 2.3 %collective-permute-done.6 = bf16[4,48,2304]{2,1,0:T(8,128)(2,1)S(1)} collective-permute-done((bf16[4,48,2304]{2,1,0:T(8,128)(2,1)S(1)}, bf16[4,48,2304]{2,1,0:T(8,128)(2,1)S(1)}, u32[]{:S(2)}, u32[]{:S(2)}) %collective-permute-start.6) | collective-permute-done | bytes 884768 | tf_op jit(solution)/shard_map/ppermute | solution.py:17
  29.8 3.2 %attention.1.refs_0_ = bf16[144,256]{1,0:T(8,128)(2,1)S(1)} custom-call(s32[2]{0:T(128)S(1)} %copy-done.5, bf16[16,18432]{1,0:T(8,128)(2,1)S(1)} %copy-done, bf16[8,48,2304]{2,1,0:T(8,128)(2,1)S(1)} %constant_dynamic-update-slice_fusion.3.far, bf16[128,640]{1,0:T(8,128)(2,1)S(1)} %pad.16.new, bf16[256,640]{1,0:T(8,128)(2,1)S(1)} %get-tuple-element.80.q_even, ...), custom_call_target="tpu_custom_call" | custom-call | tf_op jit(solution)/shard_map/attention/pallas_call | solution.py:357
  33.1 3.6 %collective-permute-start.9 = (bf16[144,256]{1,0:T(8,128)(2,1)S(1)}, bf16[144,256]{1,0:T(8,128)(2,1)S(1)}, u32[]{:S(2)}, u32[]{:S(2)}) collective-permute-start(bf16[144,256]{1,0:T(8,128)(2,1)S(1)} %attention.1.refs_0_), channel_id=1, source_target_pairs={{0,24},{8,16},{16,8},{24,0},{1,25},{9,17},{17,9},{25,1},{2,26},{10... | collective-permute-start | bytes 221192 | tf_op jit(solution)/shard_map/ppermute | solution.py:17
  37.5 2.4 %collective-permute-done.9.refs_3_ = bf16[144,256]{1,0:T(8,128)(2,1)S(1)} collective-permute-done((bf16[144,256]{1,0:T(8,128)(2,1)S(1)}, bf16[144,256]{1,0:T(8,128)(2,1)S(1)}, u32[]{:S(2)}, u32[]{:S(2)}) %collective-permute-start.9) | collective-permute-done | bytes 73760 | tf_op jit(solution)/shard_map/ppermute | solution.py:17
  40.0 2.7 %collective-permute-done.8.refs_2_ = bf16[144,256]{1,0:T(8,128)(2,1)S(1)} collective-permute-done((bf16[144,256]{1,0:T(8,128)(2,1)S(1)}, bf16[144,256]{1,0:T(8,128)(2,1)S(1)}, u32[]{:S(2)}, u32[]{:S(2)}) %collective-permute-start.8) | collective-permute-done | bytes 73760 | tf_op jit(solution)/shard_map/ppermute | solution.py:17
  42.7 2.0 %project.1 = (f32[256,1792]{1,0:T(8,128)S(1)}, bf16[256,1792]{1,0:T(8,128)(2,1)}) custom-call(bf16[144,256]{1,0:T(8,128)(2,1)S(1)} %attention.1.refs_0_, bf16[144,256]{1,0:T(8,128)(2,1)S(1)} %collective-permute-done.7.refs_1_, bf16[144,256]{1,0:T(8,128)(2,1)S(1)} %collective-permute-done.8.refs_2_, bf16[144,256]{1,0:T(8,128)(2,1)S(1)} %collective-permute-done.9.refs_3_, ...), custom_call_target="tpu_custom_call" | custom-call | tf_op jit(solution)/shard_map/project/pallas_call | solution.py:407
  45.3 2.2 %collective-permute-done.10.got = bf16[256,1792]{1,0:T(8,128)(2,1)S(1)} collective-permute-done((bf16[256,1792]{1,0:T(8,128)(2,1)}, bf16[256,1792]{1,0:T(8,128)(2,1)S(1)}, u32[]{:S(2)}, u32[]{:S(2)}) %collective-permute-start.10) | collective-permute-done | bytes 917536 | tf_op jit(solution)/shard_map/ppermute | solution.py:17
  56.2 3.4 %collective-permute-done.15.refs_5_ = bf16[16,1792]{1,0:T(8,128)(2,1)S(1)} collective-permute-done((bf16[16,1792]{1,0:T(8,128)(2,1)S(1)}, bf16[16,1792]{1,0:T(8,128)(2,1)S(1)}, u32[]{:S(2)}, u32[]{:S(2)}) %collective-permute-start.15) | collective-permute-done | bytes 57376 | tf_op jit(solution)/shard_map/ppermute | solution.py:17
  61.0 2.2 %collective-permute-done.12.refs_1_ = bf16[64,1792]{1,0:T(8,128)(2,1)S(1)} collective-permute-done((bf16[64,1792]{1,0:T(8,128)(2,1)S(1)}, bf16[64,1792]{1,0:T(8,128)(2,1)S(1)}, u32[]{:S(2)}, u32[]{:S(2)}) %collective-permute-start.12) | collective-permute-done | bytes 229408 | tf_op jit(solution)/shard_map/ppermute | solution.py:17
  65.5 2.4 %collective-permute-start.17 = (bf16[32,1792]{1,0:T(8,128)(2,1)S(1)}, bf16[32,1792]{1,0:T(8,128)(2,1)S(1)}, u32[]{:S(2)}, u32[]{:S(2)}) collective-permute-start(bf16[32,1792]{1,0:T(8,128)(2,1)S(1)} %get-tuple-element.38.refs_0_), channel_id=1, source_target_pairs={{0,8},{8,0},{16,24},{24,16},{1,9},{9,1},{17,25},{25,17},{2,10},{10... | collective-permute-start | bytes 344072 | tf_op jit(solution)/shard_map/ppermute | solution.py:17
  68.0 4.1 %collective-permute-done.17.refs_1_ = bf16[32,1792]{1,0:T(8,128)(2,1)S(1)} collective-permute-done((bf16[32,1792]{1,0:T(8,128)(2,1)S(1)}, bf16[32,1792]{1,0:T(8,128)(2,1)S(1)}, u32[]{:S(2)}, u32[]{:S(2)}) %collective-permute-start.17) | collective-permute-done | bytes 114720 | tf_op jit(solution)/shard_map/ppermute | solution.py:17
  72.2 3.0 %collective-permute-done.18.refs_2_ = bf16[32,1792]{1,0:T(8,128)(2,1)S(1)} collective-permute-done((bf16[32,1792]{1,0:T(8,128)(2,1)S(1)}, bf16[32,1792]{1,0:T(8,128)(2,1)S(1)}, u32[]{:S(2)}, u32[]{:S(2)}) %collective-permute-start.18) | collective-permute-done | bytes 114720 | tf_op jit(solution)/shard_map/ppermute | solution.py:17
  75.1 2.1 %collective-permute-start.36 = (bf16[32,1792]{1,0:T(8,128)(2,1)S(1)}, bf16[32,1792]{1,0:T(8,128)(2,1)S(1)}, u32[]{:S(2)}, u32[]{:S(2)}) collective-permute-start(bf16[32,1792]{1,0:T(8,128)(2,1)S(1)} %collect.6), channel_id=1, source_target_pairs={{0,24},{8,16},{16,8},{24,0},{1,25},{9,17},{17,9},{25,1},{2,26},{10... | collective-permute-start | bytes 344072 | tf_op jit(solution)/shard_map/ppermute | solution.py:17
  77.3 2.4 %collective-permute-start.34 = (bf16[32,1792]{1,0:T(8,128)(2,1)S(1)}, bf16[32,1792]{1,0:T(8,128)(2,1)S(1)}, u32[]{:S(2)}, u32[]{:S(2)}) collective-permute-start(bf16[32,1792]{1,0:T(8,128)(2,1)S(1)} %collect.5), channel_id=1, source_target_pairs={{0,8},{8,0},{16,24},{24,16},{1,9},{9,1},{17,25},{25,17},{2,10},{10... | collective-permute-start | bytes 344072 | tf_op jit(solution)/shard_map/ppermute | solution.py:17
  84.0 2.2 %collective-permute-done.35.refs_2_ = bf16[32,1792]{1,0:T(8,128)(2,1)S(1)} collective-permute-done((bf16[32,1792]{1,0:T(8,128)(2,1)S(1)}, bf16[32,1792]{1,0:T(8,128)(2,1)S(1)}, u32[]{:S(2)}, u32[]{:S(2)}) %collective-permute-start.35) | collective-permute-done | bytes 114720 | tf_op jit(solution)/shard_map/ppermute | solution.py:17
  92.9 4.2 %collective-permute-done.37 = bf16[1,32,3584]{2,1,0:T(8,128)(2,1)S(1)} collective-permute-done((bf16[1,32,3584]{2,1,0:T(8,128)(2,1)S(1)}, bf16[1,32,3584]{2,1,0:T(8,128)(2,1)S(1)}, u32[]{:S(2)}, u32[]{:S(2)}) %collective-permute-start.37) | collective-permute-done | bytes 229408 | tf_op jit(solution)/shard_map/ppermute | solution.py:17
  99.6 8.9 %collective-permute-done.21 = bf16[2,32,3584]{2,1,0:T(8,128)(2,1)S(1)} collective-permute-done((bf16[2,32,3584]{2,1,0:T(8,128)(2,1)S(1)}, bf16[2,32,3584]{2,1,0:T(8,128)(2,1)S(1)}, u32[]{:S(2)}, u32[]{:S(2)}) %collective-permute-start.21) | collective-permute-done | bytes 458784 | tf_op jit(solution)/shard_map/ppermute | solution.py:17
  109.5 5.3 %collective-permute-done.38 = bf16[2,32,3584]{2,1,0:T(8,128)(2,1)S(1)} collective-permute-done((bf16[2,32,3584]{2,1,0:T(8,128)(2,1)S(1)}, bf16[2,32,3584]{2,1,0:T(8,128)(2,1)S(1)}, u32[]{:S(2)}, u32[]{:S(2)}) %collective-permute-start.38) | collective-permute-done | bytes 458784 | tf_op jit(solution)/shard_map/ppermute | solution.py:17
  134.1 4.1 %collective-permute-done.30.refs_2_ = bf16[2,32,3584]{2,1,0:T(8,128)(2,1)S(1)} collective-permute-done((bf16[2,32,3584]{2,1,0:T(8,128)(2,1)S(1)}, bf16[2,32,3584]{2,1,0:T(8,128)(2,1)S(1)}, u32[]{:S(2)}, u32[]{:S(2)}) %collective-permute-start.30) | collective-permute-done | bytes 458784 | tf_op jit(solution)/shard_map/ppermute | solution.py:17
  145.1 1.9 %collective-permute-done.28 = bf16[1,32,3584]{2,1,0:T(8,128)(2,1)S(1)} collective-permute-done((bf16[1,32,3584]{2,1,0:T(8,128)(2,1)S(1)}, bf16[1,32,3584]{2,1,0:T(8,128)(2,1)S(1)}, u32[]{:S(2)}, u32[]{:S(2)}) %collective-permute-start.28) | collective-permute-done | bytes 229408 | tf_op jit(solution)/shard_map/ppermute | solution.py:17
  147.1 1.9 %collective-permute-start.32 = (bf16[16,7168]{1,0:T(8,128)(2,1)S(1)}, bf16[16,7168]{1,0:T(8,128)(2,1)S(1)}, u32[]{:S(2)}, u32[]{:S(2)}) collective-permute-start(bf16[16,7168]{1,0:T(8,128)(2,1)S(1)} %get-tuple-element.69), channel_id=1, source_target_pairs={{0,24},{8,16},{16,8},{24,0},{1,25},{9,17},{17,9},{25,1},{2,26},{10... | collective-permute-start | bytes 688136 | tf_op jit(solution)/shard_map/ppermute | solution.py:17
  151.9 8.3 %collective-permute-done.47 = bf16[2,32,3584]{2,1,0:T(8,128)(2,1)S(1)} collective-permute-done((bf16[2,32,3584]{2,1,0:T(8,128)(2,1)S(1)}, bf16[2,32,3584]{2,1,0:T(8,128)(2,1)S(1)}, u32[]{:S(2)}, u32[]{:S(2)}) %collective-permute-start.47) | collective-permute-done | bytes 458784 | tf_op jit(solution)/shard_map/ppermute | solution.py:17
  164.0 3.0 %collective-permute-done.48 = bf16[1,32,3584]{2,1,0:T(8,128)(2,1)S(1)} collective-permute-done((bf16[1,32,3584]{2,1,0:T(8,128)(2,1)S(1)}, bf16[1,32,3584]{2,1,0:T(8,128)(2,1)S(1)}, u32[]{:S(2)}, u32[]{:S(2)}) %collective-permute-start.48) | collective-permute-done | bytes 229408 | tf_op jit(solution)/shard_map/ppermute | solution.py:17
  167.1 2.9 %collective-permute-done.45 = bf16[1,32,3584]{2,1,0:T(8,128)(2,1)S(1)} collective-permute-done((bf16[1,32,3584]{2,1,0:T(8,128)(2,1)S(1)}, bf16[1,32,3584]{2,1,0:T(8,128)(2,1)S(1)}, u32[]{:S(2)}, u32[]{:S(2)}) %collective-permute-start.45) | collective-permute-done | bytes 229408 | tf_op jit(solution)/shard_map/ppermute | solution.py:17
  171.3 4.9 %collective-permute-done.49 = bf16[16,7168]{1,0:T(8,128)(2,1)S(1)} collective-permute-done((bf16[16,7168]{1,0:T(8,128)(2,1)S(1)}, bf16[16,7168]{1,0:T(8,128)(2,1)S(1)}, u32[]{:S(2)}, u32[]{:S(2)}) %collective-permute-start.49) | collective-permute-done | bytes 229408 | tf_op jit(solution)/shard_map/ppermute | solution.py:17
  (265 shorter events, 68.4 us)
Async XLA Ops:
  3.3 11.3 %collective-permute-start = (bf16[16,2304]{1,0:T(8,128)(2,1)}, bf16[16,2304]{1,0:T(8,128)(2,1)S(1)}, u32[]{:S(2)}, u32[]{:S(2)}) collective-permute-start(bf16[16,2304]{1,0:T(8,128)(2,1)} %get-tuple-element.25), channel_id=1, source_target_pairs={{0,8},{8,0},{16,24},{24,16},{1,9},{9,1},{17,25},{25,17},{2,10},{10... | collective-permute-start | bytes 221192 | tf_op jit(solution)/shard_map/ppermute | solution.py:17
  6.4 8.2 %collective-permute-start.1 = (bf16[16,2304]{1,0:T(8,128)(2,1)}, bf16[16,2304]{1,0:T(8,128)(2,1)S(1)}, u32[]{:S(2)}, u32[]{:S(2)}) collective-permute-start(bf16[16,2304]{1,0:T(8,128)(2,1)} %get-tuple-element.26), channel_id=1, source_target_pairs={{0,16},{8,24},{16,0},{24,8},{1,17},{9,25},{17,1},{25,9},{2,18},{10... | collective-permute-start | bytes 221192 | tf_op jit(solution)/shard_map/ppermute | solution.py:17
  15.4 9.2 %collective-permute-start.5 = (bf16[48,2304]{1,0:T(8,128)(2,1)S(1)}, bf16[48,2304]{1,0:T(8,128)(2,1)S(1)}, u32[]{:S(2)}, u32[]{:S(2)}) collective-permute-start(bf16[48,2304]{1,0:T(8,128)(2,1)S(1)} %constant_dynamic-update-slice_fusion), channel_id=1, source_target_pairs={{0,6},{1,7},{2,4},{3,5},{4,2},{5,3},{6,0},{7,1},{8,14},{9,15},{10,... | collective-permute-start | bytes 663560 | tf_op jit(solution)/shard_map/ppermute | solution.py:17
  17.9 9.1 %collective-permute-start.4 = (bf16[48,2304]{1,0:T(8,128)(2,1)S(1)}, bf16[48,2304]{1,0:T(8,128)(2,1)S(1)}, u32[]{:S(2)}, u32[]{:S(2)}) collective-permute-start(bf16[48,2304]{1,0:T(8,128)(2,1)S(1)} %constant_dynamic-update-slice_fusion), channel_id=1, source_target_pairs={{0,4},{1,5},{2,6},{3,7},{4,0},{5,1},{6,2},{7,3},{8,12},{9,13},{10,... | collective-permute-start | bytes 663560 | tf_op jit(solution)/shard_map/ppermute | solution.py:17
  18.4 8.7 %collective-permute-start.3 = (bf16[48,2304]{1,0:T(8,128)(2,1)S(1)}, bf16[48,2304]{1,0:T(8,128)(2,1)S(1)}, u32[]{:S(2)}, u32[]{:S(2)}) collective-permute-start(bf16[48,2304]{1,0:T(8,128)(2,1)S(1)} %constant_dynamic-update-slice_fusion), channel_id=1, source_target_pairs={{0,2},{1,3},{2,0},{3,1},{4,6},{5,7},{6,4},{7,5},{8,10},{9,11},{10,... | collective-permute-start | bytes 663560 | tf_op jit(solution)/shard_map/ppermute | solution.py:17
  33.1 6.9 %collective-permute-start.9 = (bf16[144,256]{1,0:T(8,128)(2,1)S(1)}, bf16[144,256]{1,0:T(8,128)(2,1)S(1)}, u32[]{:S(2)}, u32[]{:S(2)}) collective-permute-start(bf16[144,256]{1,0:T(8,128)(2,1)S(1)} %attention.1.refs_0_), channel_id=1, source_target_pairs={{0,24},{8,16},{16,8},{24,0},{1,25},{9,17},{17,9},{25,1},{2,26},{10... | collective-permute-start | bytes 221192 | tf_op jit(solution)/shard_map/ppermute | solution.py:17
  48.2 6.8 %collective-permute-start.14 = (bf16[16,1792]{1,0:T(8,128)(2,1)S(1)}, bf16[16,1792]{1,0:T(8,128)(2,1)S(1)}, u32[]{:S(2)}, u32[]{:S(2)}) collective-permute-start(bf16[16,1792]{1,0:T(8,128)(2,1)S(1)} %get-tuple-element.35), channel_id=1, source_target_pairs={{0,8},{8,0},{16,24},{24,16},{1,9},{9,1},{17,25},{25,17},{2,10},{10... | collective-permute-start | bytes 172040 | tf_op jit(solution)/shard_map/ppermute | solution.py:17
  49.7 11.3 %collective-permute-start.11 = (bf16[64,1792]{1,0:T(8,128)(2,1)S(1)}, bf16[64,1792]{1,0:T(8,128)(2,1)S(1)}, u32[]{:S(2)}, u32[]{:S(2)}) collective-permute-start(bf16[64,1792]{1,0:T(8,128)(2,1)S(1)} %get-tuple-element.31), channel_id=1, source_target_pairs={{0,2},{1,3},{2,0},{3,1},{4,6},{5,7},{6,4},{7,5},{8,10},{9,11},{10,... | collective-permute-start | bytes 688136 | tf_op jit(solution)/shard_map/ppermute | solution.py:17
  51.2 12.0 %collective-permute-start.12 = (bf16[64,1792]{1,0:T(8,128)(2,1)S(1)}, bf16[64,1792]{1,0:T(8,128)(2,1)S(1)}, u32[]{:S(2)}, u32[]{:S(2)}) collective-permute-start(bf16[64,1792]{1,0:T(8,128)(2,1)S(1)} %get-tuple-element.32), channel_id=1, source_target_pairs={{0,4},{1,5},{2,6},{3,7},{4,0},{5,1},{6,2},{7,3},{8,12},{9,13},{10,... | collective-permute-start | bytes 688136 | tf_op jit(solution)/shard_map/ppermute | solution.py:17
  52.0 11.3 %collective-permute-start.13 = (bf16[64,1792]{1,0:T(8,128)(2,1)S(1)}, bf16[64,1792]{1,0:T(8,128)(2,1)S(1)}, u32[]{:S(2)}, u32[]{:S(2)}) collective-permute-start(bf16[64,1792]{1,0:T(8,128)(2,1)S(1)} %get-tuple-element.33), channel_id=1, source_target_pairs={{0,6},{1,7},{2,4},{3,5},{4,2},{5,3},{6,0},{7,1},{8,14},{9,15},{10,... | collective-permute-start | bytes 688136 | tf_op jit(solution)/shard_map/ppermute | solution.py:17
  63.4 8.8 %collective-permute-start.19 = (bf16[32,1792]{1,0:T(8,128)(2,1)S(1)}, bf16[32,1792]{1,0:T(8,128)(2,1)S(1)}, u32[]{:S(2)}, u32[]{:S(2)}) collective-permute-start(bf16[32,1792]{1,0:T(8,128)(2,1)S(1)} %get-tuple-element.39.refs_0_), channel_id=1, source_target_pairs={{0,24},{8,16},{16,8},{24,0},{1,25},{9,17},{17,9},{25,1},{2,26},{10... | collective-permute-start | bytes 344072 | tf_op jit(solution)/shard_map/ppermute | solution.py:17
  65.0 10.1 %collective-permute-start.18 = (bf16[32,1792]{1,0:T(8,128)(2,1)S(1)}, bf16[32,1792]{1,0:T(8,128)(2,1)S(1)}, u32[]{:S(2)}, u32[]{:S(2)}) collective-permute-start(bf16[32,1792]{1,0:T(8,128)(2,1)S(1)} %get-tuple-element.39.refs_0_), channel_id=1, source_target_pairs={{0,16},{8,24},{16,0},{24,8},{1,17},{9,25},{17,1},{25,9},{2,18},{10... | collective-permute-start | bytes 344072 | tf_op jit(solution)/shard_map/ppermute | solution.py:17
  75.1 8.8 %collective-permute-start.36 = (bf16[32,1792]{1,0:T(8,128)(2,1)S(1)}, bf16[32,1792]{1,0:T(8,128)(2,1)S(1)}, u32[]{:S(2)}, u32[]{:S(2)}) collective-permute-start(bf16[32,1792]{1,0:T(8,128)(2,1)S(1)} %collect.6), channel_id=1, source_target_pairs={{0,24},{8,16},{16,8},{24,0},{1,25},{9,17},{17,9},{25,1},{2,26},{10... | collective-permute-start | bytes 344072 | tf_op jit(solution)/shard_map/ppermute | solution.py:17
  77.3 8.9 %collective-permute-start.35 = (bf16[32,1792]{1,0:T(8,128)(2,1)S(1)}, bf16[32,1792]{1,0:T(8,128)(2,1)S(1)}, u32[]{:S(2)}, u32[]{:S(2)}) collective-permute-start(bf16[32,1792]{1,0:T(8,128)(2,1)S(1)} %collect.6), channel_id=1, source_target_pairs={{0,16},{8,24},{16,0},{24,8},{1,17},{9,25},{17,1},{25,9},{2,18},{10... | collective-permute-start | bytes 344072 | tf_op jit(solution)/shard_map/ppermute | solution.py:17
  88.6 8.6 %collective-permute-start.37 = (bf16[1,32,3584]{2,1,0:T(8,128)(2,1)S(1)}, bf16[1,32,3584]{2,1,0:T(8,128)(2,1)S(1)}, u32[]{:S(2)}, u32[]{:S(2)}) collective-permute-start(bf16[1,32,3584]{2,1,0:T(8,128)(2,1)S(1)} %bitcast.159), channel_id=1, source_target_pairs={{0,2},{1,3},{2,0},{3,1},{4,6},{5,7},{6,4},{7,5},{8,10},{9,11},{10,... | collective-permute-start | bytes 688136 | tf_op jit(solution)/shard_map/ppermute | solution.py:17
  90.1 8.6 %collective-permute-start.40 = (bf16[1,32,3584]{2,1,0:T(8,128)(2,1)S(1)}, bf16[1,32,3584]{2,1,0:T(8,128)(2,1)S(1)}, u32[]{:S(2)}, u32[]{:S(2)}) collective-permute-start(bf16[1,32,3584]{2,1,0:T(8,128)(2,1)S(1)} %bitcast.157), channel_id=1, source_target_pairs={{0,4},{1,5},{2,6},{3,7},{4,0},{5,1},{6,2},{7,3},{8,12},{9,13},{10,... | collective-permute-start | bytes 688136 | tf_op jit(solution)/shard_map/ppermute | solution.py:17
  90.9 17.8 %collective-permute-start.24 = (bf16[2,32,3584]{2,1,0:T(8,128)(2,1)S(1)}, bf16[2,32,3584]{2,1,0:T(8,128)(2,1)S(1)}, u32[]{:S(2)}, u32[]{:S(2)}) collective-permute-start(bf16[2,32,3584]{2,1,0:T(8,128)(2,1)S(1)} %pad_maximum_fusion.10), channel_id=1, source_target_pairs={{0,2},{1,3},{2,0},{3,1},{4,6},{5,7},{6,4},{7,5},{8,10},{9,11},{10,... | collective-permute-start | bytes 1376264 | tf_op jit(solution)/shard_map/ppermute | solution.py:17
  92.2 16.2 %collective-permute-start.21 = (bf16[2,32,3584]{2,1,0:T(8,128)(2,1)S(1)}, bf16[2,32,3584]{2,1,0:T(8,128)(2,1)S(1)}, u32[]{:S(2)}, u32[]{:S(2)}) collective-permute-start(bf16[2,32,3584]{2,1,0:T(8,128)(2,1)S(1)} %pad_maximum_fusion.9), channel_id=1, source_target_pairs={{0,4},{1,5},{2,6},{3,7},{4,0},{5,1},{6,2},{7,3},{8,12},{9,13},{10,... | collective-permute-start | bytes 1376264 | tf_op jit(solution)/shard_map/ppermute | solution.py:17
  97.2 17.6 %collective-permute-start.38 = (bf16[2,32,3584]{2,1,0:T(8,128)(2,1)S(1)}, bf16[2,32,3584]{2,1,0:T(8,128)(2,1)S(1)}, u32[]{:S(2)}, u32[]{:S(2)}) collective-permute-start(bf16[2,32,3584]{2,1,0:T(8,128)(2,1)S(1)} %pad_maximum_fusion.13), channel_id=1, source_target_pairs={{0,4},{1,5},{2,6},{3,7},{4,0},{5,1},{6,2},{7,3},{8,12},{9,13},{10,... | collective-permute-start | bytes 1376264 | tf_op jit(solution)/shard_map/ppermute | solution.py:17
  98.8 24.0 %collective-permute-start.41 = (bf16[2,32,3584]{2,1,0:T(8,128)(2,1)S(1)}, bf16[2,32,3584]{2,1,0:T(8,128)(2,1)S(1)}, u32[]{:S(2)}, u32[]{:S(2)}) collective-permute-start(bf16[2,32,3584]{2,1,0:T(8,128)(2,1)S(1)} %pad_maximum_fusion.14), channel_id=1, source_target_pairs={{0,2},{1,3},{2,0},{3,1},{4,6},{5,7},{6,4},{7,5},{8,10},{9,11},{10,... | collective-permute-start | bytes 1376264 | tf_op jit(solution)/shard_map/ppermute | solution.py:17
  108.6 9.3 %collective-permute-start.22 = (bf16[128,3584]{1,0:T(8,128)(2,1)S(1)}, bf16[128,3584]{1,0:T(8,128)(2,1)S(1)}, u32[]{:S(2)}, u32[]{:S(2)}) collective-permute-start(bf16[128,3584]{1,0:T(8,128)(2,1)S(1)} %pad_maximum_fusion.6), channel_id=1, source_target_pairs={{0,1},{1,0},{2,3},{3,2},{4,5},{5,4},{6,7},{7,6},{8,9},{9,8},{10,11... | collective-permute-start | bytes 2752520 | tf_op jit(solution)/shard_map/ppermute | solution.py:17
  124.6 7.0 %collective-permute-start.39 = (bf16[128,3584]{1,0:T(8,128)(2,1)S(1)}, bf16[128,3584]{1,0:T(8,128)(2,1)S(1)}, u32[]{:S(2)}, u32[]{:S(2)}) collective-permute-start(bf16[128,3584]{1,0:T(8,128)(2,1)S(1)} %collect.7), channel_id=1, source_target_pairs={{0,1},{1,0},{2,3},{3,2},{4,5},{5,4},{6,7},{7,6},{8,9},{9,8},{10,11... | collective-permute-start | bytes 2752520 | tf_op jit(solution)/shard_map/ppermute | solution.py:17
  125.7 12.5 %collective-permute-start.30 = (bf16[2,32,3584]{2,1,0:T(8,128)(2,1)S(1)}, bf16[2,32,3584]{2,1,0:T(8,128)(2,1)S(1)}, u32[]{:S(2)}, u32[]{:S(2)}) collective-permute-start(bf16[2,32,3584]{2,1,0:T(8,128)(2,1)S(1)} %pad_maximum_fusion.12), channel_id=1, source_target_pairs={{0,4},{1,5},{2,6},{3,7},{4,0},{5,1},{6,2},{7,3},{8,12},{9,13},{10,... | collective-permute-start | bytes 1376264 | tf_op jit(solution)/shard_map/ppermute | solution.py:17
  127.1 12.8 %collective-permute-start.27 = (bf16[2,32,3584]{2,1,0:T(8,128)(2,1)S(1)}, bf16[2,32,3584]{2,1,0:T(8,128)(2,1)S(1)}, u32[]{:S(2)}, u32[]{:S(2)}) collective-permute-start(bf16[2,32,3584]{2,1,0:T(8,128)(2,1)S(1)} %pad_maximum_fusion.11), channel_id=1, source_target_pairs={{0,2},{1,3},{2,0},{3,1},{4,6},{5,7},{6,4},{7,5},{8,10},{9,11},{10,... | collective-permute-start | bytes 1376264 | tf_op jit(solution)/shard_map/ppermute | solution.py:17
  138.4 6.8 %collective-permute-start.31 = (bf16[1,32,3584]{2,1,0:T(8,128)(2,1)S(1)}, bf16[1,32,3584]{2,1,0:T(8,128)(2,1)S(1)}, u32[]{:S(2)}, u32[]{:S(2)}) collective-permute-start(bf16[1,32,3584]{2,1,0:T(8,128)(2,1)S(1)} %slice.563), channel_id=1, source_target_pairs={{0,2},{1,3},{2,0},{3,1},{4,6},{5,7},{6,4},{7,5},{8,10},{9,11},{10,... | collective-permute-start | bytes 688136 | tf_op jit(solution)/shard_map/ppermute | solution.py:17
  140.0 7.0 %collective-permute-start.28 = (bf16[1,32,3584]{2,1,0:T(8,128)(2,1)S(1)}, bf16[1,32,3584]{2,1,0:T(8,128)(2,1)S(1)}, u32[]{:S(2)}, u32[]{:S(2)}) collective-permute-start(bf16[1,32,3584]{2,1,0:T(8,128)(2,1)S(1)} %slice.564), channel_id=1, source_target_pairs={{0,4},{1,5},{2,6},{3,7},{4,0},{5,1},{6,2},{7,3},{8,12},{9,13},{10,... | collective-permute-start | bytes 688136 | tf_op jit(solution)/shard_map/ppermute | solution.py:17
  143.7 7.5 %collective-permute-start.43 = (bf16[128,3584]{1,0:T(8,128)(2,1)S(1)}, bf16[128,3584]{1,0:T(8,128)(2,1)S(1)}, u32[]{:S(2)}, u32[]{:S(2)}) collective-permute-start(bf16[128,3584]{1,0:T(8,128)(2,1)S(1)} %slice.558), channel_id=1, source_target_pairs={{0,1},{1,0},{2,3},{3,2},{4,5},{5,4},{6,7},{7,6},{8,9},{9,8},{10,11... | collective-permute-start | bytes 2752520 | tf_op jit(solution)/shard_map/ppermute | solution.py:17
  147.1 24.1 %collective-permute-start.32 = (bf16[16,7168]{1,0:T(8,128)(2,1)S(1)}, bf16[16,7168]{1,0:T(8,128)(2,1)S(1)}, u32[]{:S(2)}, u32[]{:S(2)}) collective-permute-start(bf16[16,7168]{1,0:T(8,128)(2,1)S(1)} %get-tuple-element.69), channel_id=1, source_target_pairs={{0,24},{8,16},{16,8},{24,0},{1,25},{9,17},{17,9},{25,1},{2,26},{10... | collective-permute-start | bytes 688136 | tf_op jit(solution)/shard_map/ppermute | solution.py:17
  149.0 22.3 %collective-permute-start.33 = (bf16[16,7168]{1,0:T(8,128)(2,1)S(1)}, bf16[16,7168]{1,0:T(8,128)(2,1)S(1)}, u32[]{:S(2)}, u32[]{:S(2)}) collective-permute-start(bf16[16,7168]{1,0:T(8,128)(2,1)S(1)} %get-tuple-element.70), channel_id=1, source_target_pairs={{0,16},{8,24},{16,0},{24,8},{1,17},{9,25},{17,1},{25,9},{2,18},{10... | collective-permute-start | bytes 688136 | tf_op jit(solution)/shard_map/ppermute | solution.py:17
  149.4 10.8 %collective-permute-start.47 = (bf16[2,32,3584]{2,1,0:T(8,128)(2,1)S(1)}, bf16[2,32,3584]{2,1,0:T(8,128)(2,1)S(1)}, u32[]{:S(2)}, u32[]{:S(2)}) collective-permute-start(bf16[2,32,3584]{2,1,0:T(8,128)(2,1)S(1)} %pad_maximum_fusion.16), channel_id=1, source_target_pairs={{0,4},{1,5},{2,6},{3,7},{4,0},{5,1},{6,2},{7,3},{8,12},{9,13},{10,... | collective-permute-start | bytes 1376264 | tf_op jit(solution)/shard_map/ppermute | solution.py:17
  151.6 12.3 %collective-permute-start.44 = (bf16[2,32,3584]{2,1,0:T(8,128)(2,1)S(1)}, bf16[2,32,3584]{2,1,0:T(8,128)(2,1)S(1)}, u32[]{:S(2)}, u32[]{:S(2)}) collective-permute-start(bf16[2,32,3584]{2,1,0:T(8,128)(2,1)S(1)} %pad_maximum_fusion.15), channel_id=1, source_target_pairs={{0,2},{1,3},{2,0},{3,1},{4,6},{5,7},{6,4},{7,5},{8,10},{9,11},{10,... | collective-permute-start | bytes 1376264 | tf_op jit(solution)/shard_map/ppermute | solution.py:17
  160.3 6.8 %collective-permute-start.48 = (bf16[1,32,3584]{2,1,0:T(8,128)(2,1)S(1)}, bf16[1,32,3584]{2,1,0:T(8,128)(2,1)S(1)}, u32[]{:S(2)}, u32[]{:S(2)}) collective-permute-start(bf16[1,32,3584]{2,1,0:T(8,128)(2,1)S(1)} %slice.561), channel_id=1, source_target_pairs={{0,2},{1,3},{2,0},{3,1},{4,6},{5,7},{6,4},{7,5},{8,10},{9,11},{10,... | collective-permute-start | bytes 688136 | tf_op jit(solution)/shard_map/ppermute | solution.py:17
  (42 other events, 293.3 us)

commit v4 on v3

--- a/solution.py
+++ b/solution.py
@@ -157,6 +157,14 @@
         base += ref.shape[0]
 
 
+def pick_blocks_kernel(picks, count, *refs):
+    out, base = refs[-1], 0
+    for k, n in picks:
+        rows = refs[k].shape[-2]
+        out[base : base + rows, :] = refs[k][n]
+        base += rows
+
+
 def project_kernel(plan, *refs):
     req_count, exp_count, own_rows = plan
     heads, (weight, keep, give, rows, held, sem) = refs[:req_count], refs[req_count:]
@@ -175,19 +183,15 @@
         give[:, cols] = out[half:].astype(jnp.bfloat16)
 
 
-def pair_kernel(keep, got, *outs):
+def pair_kernel(place, keep, got, hidden, *outs):
     rows = outs[0].shape[0]
-    for k, out in enumerate(outs):
+    for k, out in enumerate(outs[:4]):
         at = slice(k * rows, (k + 1) * rows)
         out[...] = (keep[at, :] + got[at, :].astype(jnp.float32)).astype(out.dtype)
-
-
-def hidden_kernel(req_count, place, hidden, other, *outs):
-    del other
     columns = outs[0].shape[1]
-    for j in range(req_count):
+    for j, out in enumerate(outs[4:]):
         start = pl.multiple_of((place[0] ^ j) * columns, 128)
-        outs[j][...] = hidden[:, pl.ds(start, columns)]
+        out[...] = hidden[:, pl.ds(start, columns)]
 
 
 def resid_kernel(own, *refs):
@@ -396,12 +400,13 @@
         return pl.pallas_call(
             pair_kernel,
             out_shape=[jax.ShapeDtypeStruct((rows, columns), jnp.float32)]
-            + [jax.ShapeDtypeStruct((rows, columns), jnp.bfloat16)] * 3,
-            in_specs=[whole, whole],
-            out_specs=[whole] * 4,
+            + [jax.ShapeDtypeStruct((rows, columns), jnp.bfloat16)] * 3
+            + [jax.ShapeDtypeStruct((own_rows, columns), jnp.bfloat16)] * req_count,
+            in_specs=[scalars, whole, whole, whole],
+            out_specs=[whole] * (4 + req_count),
             compiler_params=grant(4),
             name="pair",
-        )(keep, got)
+        )(place, keep, got, hidden_in)
 
     if aligned:
         keep, give = pl.pallas_call(
@@ -421,6 +426,7 @@
             name="project",
         )(*heads, out_weight)
         parts = pair_blocks(keep, swap(give, "exp", 1))
+        parts, hidden = parts[:4], parts[4:]
     else:
         heads_all = jnp.stack(
             [h[:tok_rows].reshape(exp_count, own_rows, head_cols) for h in heads], axis=1
@@ -449,15 +455,18 @@
             name="collect",
         )(*blocks, *others)
 
+    def pick_blocks(blocks, picks, others):
+        rows = sum(blocks[k].shape[-2] for k, n in picks)
+        return pl.pallas_call(
+            functools.partial(pick_blocks_kernel, picks, len(blocks)),
+            out_shape=jax.ShapeDtypeStruct((rows, blocks[0].shape[-1]), blocks[0].dtype),
+            in_specs=[whole] * len(blocks) + [somewhere] * len(others),
+            out_specs=whole,
+            compiler_params=grant(2),
+            name="pick_blocks",
+        )(*blocks, *others)
+
     if aligned and in_chunk == 2:
-        hidden = pl.pallas_call(
-            functools.partial(hidden_kernel, req_count),
-            out_shape=[jax.ShapeDtypeStruct((own_rows, col_width), jnp.bfloat16)] * req_count,
-            in_specs=[scalars, whole, somewhere],
-            out_specs=[whole] * req_count,
-            compiler_params=grant(2),
-            name="hidden",
-        )(place, hidden_in, parts[0])
         hidden = [x if j == 0 else swap(x, "req", j) for j, x in enumerate(hidden)]
         resid = pl.pallas_call(
             resid_kernel,
@@ -517,17 +526,24 @@
         bit *= 2
     orders = (outer_bits, outer_bits[::-1])
 
-    def gather_plane(piece, bits, others):
-        held = piece[None]
-        ids = [0]
-        firsts = []
-        for bit in bits:
-            firsts.append(swap(held, "exp", 2 * bit))
-            held = jnp.concatenate([held, firsts[-1]], axis=0)
+    def gather_plane(piece, bits):
+        held, ids, trips = piece[None], [0], []
+        for n, bit in enumerate(bits):
+            if n:
+                held = jnp.concatenate([held, trips[-1]], axis=0)
+            trips.append(swap(held, "exp", 2 * bit))
             ids = ids + [k ^ bit for k in ids]
-        same = [held[ids.index(k)] for k in range(outer)]
-        same = collect(same, others) if others else jnp.concatenate(same, axis=0)
-        return jnp.concatenate([same, swap(same, "exp", 1)], axis=0), firsts[0]
+        return held, trips[-1], ids, trips[0]
+
+    def finish_plane(held, got, ids, others, direct):
+        if direct:
+            picks = [divmod(ids.index(k), outer // 2) for k in range(outer)]
+            same = pick_blocks([held, got], picks, others)
+        else:
+            held = jnp.concatenate([held, got], axis=0)
+            same = [held[ids.index(k)] for k in range(outer)]
+            same = collect(same, others) if others else jnp.concatenate(same, axis=0)
+        return jnp.concatenate([same, swap(same, "exp", 1)], axis=0)
 
     def scatter_plane(partial, bits):
         cut = outer * chunk_block
@@ -548,39 +564,55 @@
     up_here = up_weight[0]
     down_here = down_weight[0]
     total = 0.0
-    slices, arrived, before_gather, before_down = [], [], [], []
-    for c in reversed(range(chunks)):
-        slices, halves, resid_own = normalise(c, slices[1:], arrived)
-        (left, *arrived), (right, *last) = (
-            gather_plane(halves[n], orders[n], before_gather) for n in range(2)
-        )
-        arrived = arrived + last
+    slices, halves, resid_own = normalise(1, [], [])
+    parts = [gather_plane(halves[n], orders[n]) for n in range(2)]
+    early = [finish_plane(*part[:3], [], False) for part in parts]
+    slices, halves, resid_own = normalise(0, slices[1:], [part[3] for part in parts])
+    late_parts = [gather_plane(halves[n], orders[n]) for n in range(2)]
+
+    def products(rows, c, before_down):
+        left, right = rows
 
         def project(matrix):
             return jnp.dot(
                 left, matrix[:half_width], preferred_element_type=jnp.float32
             ) + jnp.dot(right, matrix[half_width:], preferred_element_type=jnp.float32)
 
-        active = (jax.nn.silu(project(gate_here)) * project(up_here)).astype(jnp.bfloat16)
+        gate_val, up_val = project(gate_here), project(up_here)
+        active = (jax.nn.silu(gate_val) * up_val).astype(jnp.bfloat16)
         if before_down:
             active = collect([active], before_down)
         reqs = range(c * in_chunk, (c + 1) * in_chunk)
         row_weight = weight_all[:, reqs[0] : reqs[-1] + 1].reshape(-1, 1)
-        sides, before_gather, before_down = [], [], []
+        outs = []
         for n in range(2):
             cols = slice(n * half_width, (n + 1) * half_width)
             out = jnp.dot(active, down_here[:, cols], preferred_element_type=jnp.float32)
-            out = out * row_weight
-            before_gather.append(out)
-            side, first = scatter_plane(out, orders[n])
+            outs.append(out * row_weight)
+        return outs
+
+    def spread(outs, c):
+        nonlocal total
+        sides, firsts = [], []
+        for n in range(2):
+            side, first = scatter_plane(outs[n], orders[n])
             sides.append(side)
-            before_down.append(first)
+            firsts.append(first)
         sums = jnp.concatenate(sides, axis=1)
-        for n, j in reversed(list(enumerate(reqs))):
+        for n, j in reversed(list(enumerate(range(c * in_chunk, (c + 1) * in_chunk)))):
             part = sums[n * own_rows : (n + 1) * own_rows]
             if j:
                 part = swap(part, "req", j)
             total = total + part.astype(jnp.float32)
+        return firsts
+
+    early_outs = products(early, 1, [])
+    late = [
+        finish_plane(*part[:3], early_outs, n == 0) for n, part in enumerate(late_parts)
+    ]
+    firsts = spread(early_outs, 1)
+    late_outs = products(late, 0, firsts)
+    spread(late_outs, 0)
     return (total + resid_own.astype(jnp.float32)).astype(jnp.bfloat16)
 
 

time: 177 us -> 174 us (0.983)
  waiting for transfers between devices: 85.2 us -> 80.2 us
    ppermute x50, waiting for transfers between devices: 85.2 us -> 80.2 us  [swap(): return lax.ppermute(x, axis, [(i, i ^ distance) for i in range(size)])]
  transfers between devices with their start and end apart: 50 -> 50, of which waited for: 30 -> 31; matrix products, arithmetic and copies ran while one was open for 11% -> 12% of each run, Pallas kernels for 3% -> 3%
where the time goes in v4:
time: 174 us
  waiting for transfers between devices  80.2 us (46%)
  starting transfers between devices  54.6 us (31%)
  Pallas kernels  14.1 us (8%)
  matrix products  13.7 us (8%)
  local copies, waits for them, and re-layouts  5.84 us (3%)
  other arithmetic  4.15 us (2%)
    ppermute x50, waiting for transfers between devices, swap(): return lax.ppermute(x, axis, [(i, i ^ distance) for i in range(size)])  80.2 us
    ppermute x50, starting transfers between devices, swap(): return lax.ppermute(x, axis, [(i, i ^ distance) for i in range(size)])  54.6 us
    dot_general x4, matrix products, project(): jnp.dot(left, matrix[:half_width], preferred_element_type=jnp.float32)  4.73 us
    dot_general x4, matrix products, products(): jnp.dot(active, down_here[:, cols], preferred_element_type=jnp.float32)  4.54 us
    dot_general x4, matrix products, project(): jnp.dot(right, matrix[half_width:], preferred_element_type=jnp.float32)  4.41 us
  transfers between devices with their start and end apart: 50, of which 31 were waited for; matrix products, arithmetic and copies ran while one was open for 12% of the time, Pallas kernels for 3%

profile of v4, /device:TPU:0, one launch (start us, length us, event | category | flops | bytes accessed | tf_op | source)
XLA Modules:
  0.0 173.6 jit_solution(15922552124934136554)
XLA Ops:
  0.7 2.6 %pick_far.1 = (bf16[16,2304]{1,0:T(8,128)(2,1)}, bf16[16,2304]{1,0:T(8,128)(2,1)}, bf16[16,2304]{1,0:T(8,128)(2,1)}) custom-call(s32[2]{0:T(128)} %pad_add_fusion.1.place, s32[8,16]{1,0:T(8,128)} %lists.3, bf16[32,36864]{1,0:T(8,128)(2,1)} %pool.3), custom_call_target="tpu_custom_call" | custom-call | tf_op jit(solution)/shard_map/pick_far/pallas_call | solution.py:288
  3.3 3.1 %collective-permute-start = (bf16[16,2304]{1,0:T(8,128)(2,1)}, bf16[16,2304]{1,0:T(8,128)(2,1)S(1)}, u32[]{:S(2)}, u32[]{:S(2)}) collective-permute-start(bf16[16,2304]{1,0:T(8,128)(2,1)} %get-tuple-element.25), channel_id=1, source_target_pairs={{0,8},{8,0},{16,24},{24,16},{1,9},{9,1},{17,25},{25,17},{2,10},{10... | collective-permute-start | bytes 221192 | tf_op jit(solution)/shard_map/ppermute | solution.py:17
  6.4 2.6 %collective-permute-start.1 = (bf16[16,2304]{1,0:T(8,128)(2,1)}, bf16[16,2304]{1,0:T(8,128)(2,1)S(1)}, u32[]{:S(2)}, u32[]{:S(2)}) collective-permute-start(bf16[16,2304]{1,0:T(8,128)(2,1)} %get-tuple-element.26), channel_id=1, source_target_pairs={{0,16},{8,24},{16,0},{24,8},{1,17},{9,25},{17,1},{25,9},{2,18},{10... | collective-permute-start | bytes 221192 | tf_op jit(solution)/shard_map/ppermute | solution.py:17
  9.7 3.0 %pick_near.1.near = bf16[16,18432]{1,0:T(8,128)(2,1)} custom-call(s32[2]{0:T(128)} %pad_add_fusion.1.place, s32[8,16]{1,0:T(8,128)} %lists.3, bf16[32,36864]{1,0:T(8,128)(2,1)} %pool.3), custom_call_target="tpu_custom_call" | custom-call | tf_op jit(solution)/shard_map/pick_near/pallas_call | solution.py:299
  15.5 2.4 %collective-permute-start.5 = (bf16[48,2304]{1,0:T(8,128)(2,1)S(1)}, bf16[48,2304]{1,0:T(8,128)(2,1)S(1)}, u32[]{:S(2)}, u32[]{:S(2)}) collective-permute-start(bf16[48,2304]{1,0:T(8,128)(2,1)S(1)} %constant_dynamic-update-slice_fusion), channel_id=1, source_target_pairs={{0,6},{1,7},{2,4},{3,5},{4,2},{5,3},{6,0},{7,1},{8,14},{9,15},{10,... | collective-permute-start | bytes 663560 | tf_op jit(solution)/shard_map/ppermute | solution.py:17
  19.0 5.7 %collective-permute-done.5 = bf16[48,2304]{1,0:T(8,128)(2,1)S(1)} collective-permute-done((bf16[48,2304]{1,0:T(8,128)(2,1)S(1)}, bf16[48,2304]{1,0:T(8,128)(2,1)S(1)}, u32[]{:S(2)}, u32[]{:S(2)}) %collective-permute-start.5) | collective-permute-done | bytes 221216 | tf_op jit(solution)/shard_map/ppermute | solution.py:17
  24.6 2.3 %collective-permute-done.4 = bf16[48,2304]{1,0:T(8,128)(2,1)S(1)} collective-permute-done((bf16[48,2304]{1,0:T(8,128)(2,1)S(1)}, bf16[48,2304]{1,0:T(8,128)(2,1)S(1)}, u32[]{:S(2)}, u32[]{:S(2)}) %collective-permute-start.4) | collective-permute-done | bytes 221216 | tf_op jit(solution)/shard_map/ppermute | solution.py:17
  27.4 2.3 %collective-permute-done.6 = bf16[4,48,2304]{2,1,0:T(8,128)(2,1)S(1)} collective-permute-done((bf16[4,48,2304]{2,1,0:T(8,128)(2,1)S(1)}, bf16[4,48,2304]{2,1,0:T(8,128)(2,1)S(1)}, u32[]{:S(2)}, u32[]{:S(2)}) %collective-permute-start.6) | collective-permute-done | bytes 884768 | tf_op jit(solution)/shard_map/ppermute | solution.py:17
  29.9 3.2 %attention.1.refs_0_ = bf16[144,256]{1,0:T(8,128)(2,1)S(1)} custom-call(s32[2]{0:T(128)S(1)} %copy-done.5, bf16[16,18432]{1,0:T(8,128)(2,1)S(1)} %copy-done, bf16[8,48,2304]{2,1,0:T(8,128)(2,1)S(1)} %constant_dynamic-update-slice_fusion.3.far, bf16[128,640]{1,0:T(8,128)(2,1)S(1)} %pad.16.new, bf16[256,640]{1,0:T(8,128)(2,1)S(1)} %get-tuple-element.78.q_even, ...), custom_call_target="tpu_custom_call" | custom-call | tf_op jit(solution)/shard_map/attention/pallas_call | solution.py:361
  33.1 3.6 %collective-permute-start.9 = (bf16[144,256]{1,0:T(8,128)(2,1)S(1)}, bf16[144,256]{1,0:T(8,128)(2,1)S(1)}, u32[]{:S(2)}, u32[]{:S(2)}) collective-permute-start(bf16[144,256]{1,0:T(8,128)(2,1)S(1)} %attention.1.refs_0_), channel_id=1, source_target_pairs={{0,24},{8,16},{16,8},{24,0},{1,25},{9,17},{17,9},{25,1},{2,26},{10... | collective-permute-start | bytes 221192 | tf_op jit(solution)/shard_map/ppermute | solution.py:17
  37.6 2.4 %collective-permute-done.9.refs_3_ = bf16[144,256]{1,0:T(8,128)(2,1)S(1)} collective-permute-done((bf16[144,256]{1,0:T(8,128)(2,1)S(1)}, bf16[144,256]{1,0:T(8,128)(2,1)S(1)}, u32[]{:S(2)}, u32[]{:S(2)}) %collective-permute-start.9) | collective-permute-done | bytes 73760 | tf_op jit(solution)/shard_map/ppermute | solution.py:17
  40.0 2.7 %collective-permute-done.8.refs_2_ = bf16[144,256]{1,0:T(8,128)(2,1)S(1)} collective-permute-done((bf16[144,256]{1,0:T(8,128)(2,1)S(1)}, bf16[144,256]{1,0:T(8,128)(2,1)S(1)}, u32[]{:S(2)}, u32[]{:S(2)}) %collective-permute-start.8) | collective-permute-done | bytes 73760 | tf_op jit(solution)/shard_map/ppermute | solution.py:17
  42.7 2.0 %project.1 = (f32[256,1792]{1,0:T(8,128)S(1)}, bf16[256,1792]{1,0:T(8,128)(2,1)}) custom-call(bf16[144,256]{1,0:T(8,128)(2,1)S(1)} %attention.1.refs_0_, bf16[144,256]{1,0:T(8,128)(2,1)S(1)} %collective-permute-done.7.refs_1_, bf16[144,256]{1,0:T(8,128)(2,1)S(1)} %collective-permute-done.8.refs_2_, bf16[144,256]{1,0:T(8,128)(2,1)S(1)} %collective-permute-done.9.refs_3_, ...), custom_call_target="tpu_custom_call" | custom-call | tf_op jit(solution)/shard_map/project/pallas_call | solution.py:412
  45.3 2.2 %collective-permute-done.10.got = bf16[256,1792]{1,0:T(8,128)(2,1)S(1)} collective-permute-done((bf16[256,1792]{1,0:T(8,128)(2,1)}, bf16[256,1792]{1,0:T(8,128)(2,1)S(1)}, u32[]{:S(2)}, u32[]{:S(2)}) %collective-permute-start.10) | collective-permute-done | bytes 917536 | tf_op jit(solution)/shard_map/ppermute | solution.py:17
  56.2 3.4 %collective-permute-done.15.refs_5_ = bf16[16,1792]{1,0:T(8,128)(2,1)S(1)} collective-permute-done((bf16[16,1792]{1,0:T(8,128)(2,1)S(1)}, bf16[16,1792]{1,0:T(8,128)(2,1)S(1)}, u32[]{:S(2)}, u32[]{:S(2)}) %collective-permute-start.15) | collective-permute-done | bytes 57376 | tf_op jit(solution)/shard_map/ppermute | solution.py:17
  61.0 2.2 %collective-permute-done.12.refs_1_ = bf16[64,1792]{1,0:T(8,128)(2,1)S(1)} collective-permute-done((bf16[64,1792]{1,0:T(8,128)(2,1)S(1)}, bf16[64,1792]{1,0:T(8,128)(2,1)S(1)}, u32[]{:S(2)}, u32[]{:S(2)}) %collective-permute-start.12) | collective-permute-done | bytes 229408 | tf_op jit(solution)/shard_map/ppermute | solution.py:17
  65.5 2.4 %collective-permute-start.17 = (bf16[32,1792]{1,0:T(8,128)(2,1)S(1)}, bf16[32,1792]{1,0:T(8,128)(2,1)S(1)}, u32[]{:S(2)}, u32[]{:S(2)}) collective-permute-start(bf16[32,1792]{1,0:T(8,128)(2,1)S(1)} %get-tuple-element.38.refs_0_), channel_id=1, source_target_pairs={{0,8},{8,0},{16,24},{24,16},{1,9},{9,1},{17,25},{25,17},{2,10},{10... | collective-permute-start | bytes 344072 | tf_op jit(solution)/shard_map/ppermute | solution.py:17
  68.0 4.1 %collective-permute-done.17.refs_1_ = bf16[32,1792]{1,0:T(8,128)(2,1)S(1)} collective-permute-done((bf16[32,1792]{1,0:T(8,128)(2,1)S(1)}, bf16[32,1792]{1,0:T(8,128)(2,1)S(1)}, u32[]{:S(2)}, u32[]{:S(2)}) %collective-permute-start.17) | collective-permute-done | bytes 114720 | tf_op jit(solution)/shard_map/ppermute | solution.py:17
  72.2 3.0 %collective-permute-done.18.refs_2_ = bf16[32,1792]{1,0:T(8,128)(2,1)S(1)} collective-permute-done((bf16[32,1792]{1,0:T(8,128)(2,1)S(1)}, bf16[32,1792]{1,0:T(8,128)(2,1)S(1)}, u32[]{:S(2)}, u32[]{:S(2)}) %collective-permute-start.18) | collective-permute-done | bytes 114720 | tf_op jit(solution)/shard_map/ppermute | solution.py:17
  75.1 2.1 %collective-permute-start.36 = (bf16[32,1792]{1,0:T(8,128)(2,1)S(1)}, bf16[32,1792]{1,0:T(8,128)(2,1)S(1)}, u32[]{:S(2)}, u32[]{:S(2)}) collective-permute-start(bf16[32,1792]{1,0:T(8,128)(2,1)S(1)} %collect.5), channel_id=1, source_target_pairs={{0,24},{8,16},{16,8},{24,0},{1,25},{9,17},{17,9},{25,1},{2,26},{10... | collective-permute-start | bytes 344072 | tf_op jit(solution)/shard_map/ppermute | solution.py:17
  77.3 2.4 %collective-permute-start.34 = (bf16[32,1792]{1,0:T(8,128)(2,1)S(1)}, bf16[32,1792]{1,0:T(8,128)(2,1)S(1)}, u32[]{:S(2)}, u32[]{:S(2)}) collective-permute-start(bf16[32,1792]{1,0:T(8,128)(2,1)S(1)} %collect.4), channel_id=1, source_target_pairs={{0,8},{8,0},{16,24},{24,16},{1,9},{9,1},{17,25},{25,17},{2,10},{10... | collective-permute-start | bytes 344072 | tf_op jit(solution)/shard_map/ppermute | solution.py:17
  84.0 2.2 %collective-permute-done.35.refs_2_ = bf16[32,1792]{1,0:T(8,128)(2,1)S(1)} collective-permute-done((bf16[32,1792]{1,0:T(8,128)(2,1)S(1)}, bf16[32,1792]{1,0:T(8,128)(2,1)S(1)}, u32[]{:S(2)}, u32[]{:S(2)}) %collective-permute-start.35) | collective-permute-done | bytes 114720 | tf_op jit(solution)/shard_map/ppermute | solution.py:17
  92.9 5.7 %collective-permute-done.40 = bf16[1,32,3584]{2,1,0:T(8,128)(2,1)S(1)} collective-permute-done((bf16[1,32,3584]{2,1,0:T(8,128)(2,1)S(1)}, bf16[1,32,3584]{2,1,0:T(8,128)(2,1)S(1)}, u32[]{:S(2)}, u32[]{:S(2)}) %collective-permute-start.40) | collective-permute-done | bytes 229408 | tf_op jit(solution)/shard_map/ppermute | solution.py:17
  100.9 7.6 %collective-permute-done.21 = bf16[2,32,3584]{2,1,0:T(8,128)(2,1)S(1)} collective-permute-done((bf16[2,32,3584]{2,1,0:T(8,128)(2,1)S(1)}, bf16[2,32,3584]{2,1,0:T(8,128)(2,1)S(1)}, u32[]{:S(2)}, u32[]{:S(2)}) %collective-permute-start.21) | collective-permute-done | bytes 458784 | tf_op jit(solution)/shard_map/ppermute | solution.py:17
  109.5 3.0 %collective-permute-done.25 = bf16[128,3584]{1,0:T(8,128)(2,1)S(1)} collective-permute-done((bf16[128,3584]{1,0:T(8,128)(2,1)S(1)}, bf16[128,3584]{1,0:T(8,128)(2,1)S(1)}, u32[]{:S(2)}, u32[]{:S(2)}) %collective-permute-start.25) | collective-permute-done | bytes 917536 | tf_op jit(solution)/shard_map/ppermute | solution.py:17
  131.7 4.2 %collective-permute-done.30.refs_2_ = bf16[2,32,3584]{2,1,0:T(8,128)(2,1)S(1)} collective-permute-done((bf16[2,32,3584]{2,1,0:T(8,128)(2,1)S(1)}, bf16[2,32,3584]{2,1,0:T(8,128)(2,1)S(1)}, u32[]{:S(2)}, u32[]{:S(2)}) %collective-permute-start.30) | collective-permute-done | bytes 458784 | tf_op jit(solution)/shard_map/ppermute | solution.py:17
  144.9 2.1 %collective-permute-start.32 = (bf16[16,7168]{1,0:T(8,128)(2,1)S(1)}, bf16[16,7168]{1,0:T(8,128)(2,1)S(1)}, u32[]{:S(2)}, u32[]{:S(2)}) collective-permute-start(bf16[16,7168]{1,0:T(8,128)(2,1)S(1)} %get-tuple-element.69), channel_id=1, source_target_pairs={{0,24},{8,16},{16,8},{24,0},{1,25},{9,17},{17,9},{25,1},{2,26},{10... | collective-permute-start | bytes 688136 | tf_op jit(solution)/shard_map/ppermute | solution.py:17
  149.9 8.3 %collective-permute-done.47 = bf16[2,32,3584]{2,1,0:T(8,128)(2,1)S(1)} collective-permute-done((bf16[2,32,3584]{2,1,0:T(8,128)(2,1)S(1)}, bf16[2,32,3584]{2,1,0:T(8,128)(2,1)S(1)}, u32[]{:S(2)}, u32[]{:S(2)}) %collective-permute-start.47) | collective-permute-done | bytes 458784 | tf_op jit(solution)/shard_map/ppermute | solution.py:17
  159.5 2.8 %collective-permute-start.45 = (bf16[1,32,3584]{2,1,0:T(8,128)(2,1)S(1)}, bf16[1,32,3584]{2,1,0:T(8,128)(2,1)S(1)}, u32[]{:S(2)}, u32[]{:S(2)}) collective-permute-start(bf16[1,32,3584]{2,1,0:T(8,128)(2,1)S(1)} %slice.550), channel_id=1, source_target_pairs={{0,4},{1,5},{2,6},{3,7},{4,0},{5,1},{6,2},{7,3},{8,12},{9,13},{10,... | collective-permute-start | bytes 688136 | tf_op jit(solution)/shard_map/ppermute | solution.py:17
  162.3 2.1 %collective-permute-done.48 = bf16[1,32,3584]{2,1,0:T(8,128)(2,1)S(1)} collective-permute-done((bf16[1,32,3584]{2,1,0:T(8,128)(2,1)S(1)}, bf16[1,32,3584]{2,1,0:T(8,128)(2,1)S(1)}, u32[]{:S(2)}, u32[]{:S(2)}) %collective-permute-start.48) | collective-permute-done | bytes 229408 | tf_op jit(solution)/shard_map/ppermute | solution.py:17
  166.4 2.4 %collective-permute-start.49 = (bf16[16,7168]{1,0:T(8,128)(2,1)S(1)}, bf16[16,7168]{1,0:T(8,128)(2,1)S(1)}, u32[]{:S(2)}, u32[]{:S(2)}) collective-permute-start(bf16[16,7168]{1,0:T(8,128)(2,1)S(1)} %fusion.44), channel_id=1, source_target_pairs={{0,8},{8,0},{16,24},{24,16},{1,9},{9,1},{17,25},{25,17},{2,10},{10... | collective-permute-start | bytes 688136 | tf_op jit(solution)/shard_map/ppermute | solution.py:17
  168.8 4.0 %collective-permute-done.49 = bf16[16,7168]{1,0:T(8,128)(2,1)S(1)} collective-permute-done((bf16[16,7168]{1,0:T(8,128)(2,1)S(1)}, bf16[16,7168]{1,0:T(8,128)(2,1)S(1)}, u32[]{:S(2)}, u32[]{:S(2)}) %collective-permute-start.49) | collective-permute-done | bytes 229408 | tf_op jit(solution)/shard_map/ppermute | solution.py:17
  (263 shorter events, 68.2 us)
Async XLA Ops:
  3.3 11.3 %collective-permute-start = (bf16[16,2304]{1,0:T(8,128)(2,1)}, bf16[16,2304]{1,0:T(8,128)(2,1)S(1)}, u32[]{:S(2)}, u32[]{:S(2)}) collective-permute-start(bf16[16,2304]{1,0:T(8,128)(2,1)} %get-tuple-element.25), channel_id=1, source_target_pairs={{0,8},{8,0},{16,24},{24,16},{1,9},{9,1},{17,25},{25,17},{2,10},{10... | collective-permute-start | bytes 221192 | tf_op jit(solution)/shard_map/ppermute | solution.py:17
  6.4 8.2 %collective-permute-start.1 = (bf16[16,2304]{1,0:T(8,128)(2,1)}, bf16[16,2304]{1,0:T(8,128)(2,1)S(1)}, u32[]{:S(2)}, u32[]{:S(2)}) collective-permute-start(bf16[16,2304]{1,0:T(8,128)(2,1)} %get-tuple-element.26), channel_id=1, source_target_pairs={{0,16},{8,24},{16,0},{24,8},{1,17},{9,25},{17,1},{25,9},{2,18},{10... | collective-permute-start | bytes 221192 | tf_op jit(solution)/shard_map/ppermute | solution.py:17
  15.5 9.2 %collective-permute-start.5 = (bf16[48,2304]{1,0:T(8,128)(2,1)S(1)}, bf16[48,2304]{1,0:T(8,128)(2,1)S(1)}, u32[]{:S(2)}, u32[]{:S(2)}) collective-permute-start(bf16[48,2304]{1,0:T(8,128)(2,1)S(1)} %constant_dynamic-update-slice_fusion), channel_id=1, source_target_pairs={{0,6},{1,7},{2,4},{3,5},{4,2},{5,3},{6,0},{7,1},{8,14},{9,15},{10,... | collective-permute-start | bytes 663560 | tf_op jit(solution)/shard_map/ppermute | solution.py:17
  17.9 9.1 %collective-permute-start.4 = (bf16[48,2304]{1,0:T(8,128)(2,1)S(1)}, bf16[48,2304]{1,0:T(8,128)(2,1)S(1)}, u32[]{:S(2)}, u32[]{:S(2)}) collective-permute-start(bf16[48,2304]{1,0:T(8,128)(2,1)S(1)} %constant_dynamic-update-slice_fusion), channel_id=1, source_target_pairs={{0,4},{1,5},{2,6},{3,7},{4,0},{5,1},{6,2},{7,3},{8,12},{9,13},{10,... | collective-permute-start | bytes 663560 | tf_op jit(solution)/shard_map/ppermute | solution.py:17
  18.4 8.7 %collective-permute-start.3 = (bf16[48,2304]{1,0:T(8,128)(2,1)S(1)}, bf16[48,2304]{1,0:T(8,128)(2,1)S(1)}, u32[]{:S(2)}, u32[]{:S(2)}) collective-permute-start(bf16[48,2304]{1,0:T(8,128)(2,1)S(1)} %constant_dynamic-update-slice_fusion), channel_id=1, source_target_pairs={{0,2},{1,3},{2,0},{3,1},{4,6},{5,7},{6,4},{7,5},{8,10},{9,11},{10,... | collective-permute-start | bytes 663560 | tf_op jit(solution)/shard_map/ppermute | solution.py:17
  33.1 6.9 %collective-permute-start.9 = (bf16[144,256]{1,0:T(8,128)(2,1)S(1)}, bf16[144,256]{1,0:T(8,128)(2,1)S(1)}, u32[]{:S(2)}, u32[]{:S(2)}) collective-permute-start(bf16[144,256]{1,0:T(8,128)(2,1)S(1)} %attention.1.refs_0_), channel_id=1, source_target_pairs={{0,24},{8,16},{16,8},{24,0},{1,25},{9,17},{17,9},{25,1},{2,26},{10... | collective-permute-start | bytes 221192 | tf_op jit(solution)/shard_map/ppermute | solution.py:17
  48.2 6.8 %collective-permute-start.14 = (bf16[16,1792]{1,0:T(8,128)(2,1)S(1)}, bf16[16,1792]{1,0:T(8,128)(2,1)S(1)}, u32[]{:S(2)}, u32[]{:S(2)}) collective-permute-start(bf16[16,1792]{1,0:T(8,128)(2,1)S(1)} %get-tuple-element.35), channel_id=1, source_target_pairs={{0,8},{8,0},{16,24},{24,16},{1,9},{9,1},{17,25},{25,17},{2,10},{10... | collective-permute-start | bytes 172040 | tf_op jit(solution)/shard_map/ppermute | solution.py:17
  49.7 11.3 %collective-permute-start.11 = (bf16[64,1792]{1,0:T(8,128)(2,1)S(1)}, bf16[64,1792]{1,0:T(8,128)(2,1)S(1)}, u32[]{:S(2)}, u32[]{:S(2)}) collective-permute-start(bf16[64,1792]{1,0:T(8,128)(2,1)S(1)} %get-tuple-element.31), channel_id=1, source_target_pairs={{0,2},{1,3},{2,0},{3,1},{4,6},{5,7},{6,4},{7,5},{8,10},{9,11},{10,... | collective-permute-start | bytes 688136 | tf_op jit(solution)/shard_map/ppermute | solution.py:17
  51.2 12.0 %collective-permute-start.12 = (bf16[64,1792]{1,0:T(8,128)(2,1)S(1)}, bf16[64,1792]{1,0:T(8,128)(2,1)S(1)}, u32[]{:S(2)}, u32[]{:S(2)}) collective-permute-start(bf16[64,1792]{1,0:T(8,128)(2,1)S(1)} %get-tuple-element.32), channel_id=1, source_target_pairs={{0,4},{1,5},{2,6},{3,7},{4,0},{5,1},{6,2},{7,3},{8,12},{9,13},{10,... | collective-permute-start | bytes 688136 | tf_op jit(solution)/shard_map/ppermute | solution.py:17
  52.0 11.3 %collective-permute-start.13 = (bf16[64,1792]{1,0:T(8,128)(2,1)S(1)}, bf16[64,1792]{1,0:T(8,128)(2,1)S(1)}, u32[]{:S(2)}, u32[]{:S(2)}) collective-permute-start(bf16[64,1792]{1,0:T(8,128)(2,1)S(1)} %get-tuple-element.33), channel_id=1, source_target_pairs={{0,6},{1,7},{2,4},{3,5},{4,2},{5,3},{6,0},{7,1},{8,14},{9,15},{10,... | collective-permute-start | bytes 688136 | tf_op jit(solution)/shard_map/ppermute | solution.py:17
  63.4 8.8 %collective-permute-start.19 = (bf16[32,1792]{1,0:T(8,128)(2,1)S(1)}, bf16[32,1792]{1,0:T(8,128)(2,1)S(1)}, u32[]{:S(2)}, u32[]{:S(2)}) collective-permute-start(bf16[32,1792]{1,0:T(8,128)(2,1)S(1)} %get-tuple-element.39.refs_0_), channel_id=1, source_target_pairs={{0,24},{8,16},{16,8},{24,0},{1,25},{9,17},{17,9},{25,1},{2,26},{10... | collective-permute-start | bytes 344072 | tf_op jit(solution)/shard_map/ppermute | solution.py:17
  65.0 10.1 %collective-permute-start.18 = (bf16[32,1792]{1,0:T(8,128)(2,1)S(1)}, bf16[32,1792]{1,0:T(8,128)(2,1)S(1)}, u32[]{:S(2)}, u32[]{:S(2)}) collective-permute-start(bf16[32,1792]{1,0:T(8,128)(2,1)S(1)} %get-tuple-element.39.refs_0_), channel_id=1, source_target_pairs={{0,16},{8,24},{16,0},{24,8},{1,17},{9,25},{17,1},{25,9},{2,18},{10... | collective-permute-start | bytes 344072 | tf_op jit(solution)/shard_map/ppermute | solution.py:17
  75.1 8.8 %collective-permute-start.36 = (bf16[32,1792]{1,0:T(8,128)(2,1)S(1)}, bf16[32,1792]{1,0:T(8,128)(2,1)S(1)}, u32[]{:S(2)}, u32[]{:S(2)}) collective-permute-start(bf16[32,1792]{1,0:T(8,128)(2,1)S(1)} %collect.5), channel_id=1, source_target_pairs={{0,24},{8,16},{16,8},{24,0},{1,25},{9,17},{17,9},{25,1},{2,26},{10... | collective-permute-start | bytes 344072 | tf_op jit(solution)/shard_map/ppermute | solution.py:17
  77.3 8.9 %collective-permute-start.35 = (bf16[32,1792]{1,0:T(8,128)(2,1)S(1)}, bf16[32,1792]{1,0:T(8,128)(2,1)S(1)}, u32[]{:S(2)}, u32[]{:S(2)}) collective-permute-start(bf16[32,1792]{1,0:T(8,128)(2,1)S(1)} %collect.5), channel_id=1, source_target_pairs={{0,16},{8,24},{16,0},{24,8},{1,17},{9,25},{17,1},{25,9},{2,18},{10... | collective-permute-start | bytes 344072 | tf_op jit(solution)/shard_map/ppermute | solution.py:17
  88.6 10.8 %collective-permute-start.37 = (bf16[1,32,3584]{2,1,0:T(8,128)(2,1)S(1)}, bf16[1,32,3584]{2,1,0:T(8,128)(2,1)S(1)}, u32[]{:S(2)}, u32[]{:S(2)}) collective-permute-start(bf16[1,32,3584]{2,1,0:T(8,128)(2,1)S(1)} %bitcast.157), channel_id=1, source_target_pairs={{0,2},{1,3},{2,0},{3,1},{4,6},{5,7},{6,4},{7,5},{8,10},{9,11},{10,... | collective-permute-start | bytes 688136 | tf_op jit(solution)/shard_map/ppermute | solution.py:17
  90.1 8.5 %collective-permute-start.40 = (bf16[1,32,3584]{2,1,0:T(8,128)(2,1)S(1)}, bf16[1,32,3584]{2,1,0:T(8,128)(2,1)S(1)}, u32[]{:S(2)}, u32[]{:S(2)}) collective-permute-start(bf16[1,32,3584]{2,1,0:T(8,128)(2,1)S(1)} %bitcast.152), channel_id=1, source_target_pairs={{0,4},{1,5},{2,6},{3,7},{4,0},{5,1},{6,2},{7,3},{8,12},{9,13},{10,... | collective-permute-start | bytes 688136 | tf_op jit(solution)/shard_map/ppermute | solution.py:17
  90.9 17.8 %collective-permute-start.24 = (bf16[2,32,3584]{2,1,0:T(8,128)(2,1)S(1)}, bf16[2,32,3584]{2,1,0:T(8,128)(2,1)S(1)}, u32[]{:S(2)}, u32[]{:S(2)}) collective-permute-start(bf16[2,32,3584]{2,1,0:T(8,128)(2,1)S(1)} %pad_maximum_fusion.10), channel_id=1, source_target_pairs={{0,2},{1,3},{2,0},{3,1},{4,6},{5,7},{6,4},{7,5},{8,10},{9,11},{10,... | collective-permute-start | bytes 1376264 | tf_op jit(solution)/shard_map/ppermute | solution.py:17
  92.2 16.2 %collective-permute-start.21 = (bf16[2,32,3584]{2,1,0:T(8,128)(2,1)S(1)}, bf16[2,32,3584]{2,1,0:T(8,128)(2,1)S(1)}, u32[]{:S(2)}, u32[]{:S(2)}) collective-permute-start(bf16[2,32,3584]{2,1,0:T(8,128)(2,1)S(1)} %pad_maximum_fusion.9), channel_id=1, source_target_pairs={{0,4},{1,5},{2,6},{3,7},{4,0},{5,1},{6,2},{7,3},{8,12},{9,13},{10,... | collective-permute-start | bytes 1376264 | tf_op jit(solution)/shard_map/ppermute | solution.py:17
  98.7 21.8 %collective-permute-start.41 = (bf16[2,32,3584]{2,1,0:T(8,128)(2,1)S(1)}, bf16[2,32,3584]{2,1,0:T(8,128)(2,1)S(1)}, u32[]{:S(2)}, u32[]{:S(2)}) collective-permute-start(bf16[2,32,3584]{2,1,0:T(8,128)(2,1)S(1)} %pad_maximum_fusion.14), channel_id=1, source_target_pairs={{0,2},{1,3},{2,0},{3,1},{4,6},{5,7},{6,4},{7,5},{8,10},{9,11},{10,... | collective-permute-start | bytes 1376264 | tf_op jit(solution)/shard_map/ppermute | solution.py:17
  99.4 22.8 %collective-permute-start.38 = (bf16[2,32,3584]{2,1,0:T(8,128)(2,1)S(1)}, bf16[2,32,3584]{2,1,0:T(8,128)(2,1)S(1)}, u32[]{:S(2)}, u32[]{:S(2)}) collective-permute-start(bf16[2,32,3584]{2,1,0:T(8,128)(2,1)S(1)} %pad_maximum_fusion.13.refs_0_), channel_id=1, source_target_pairs={{0,4},{1,5},{2,6},{3,7},{4,0},{5,1},{6,2},{7,3},{8,12},{9,13},{10,... | collective-permute-start | bytes 1376264 | tf_op jit(solution)/shard_map/ppermute | solution.py:17
  108.6 6.9 %collective-permute-start.22 = (bf16[128,3584]{1,0:T(8,128)(2,1)S(1)}, bf16[128,3584]{1,0:T(8,128)(2,1)S(1)}, u32[]{:S(2)}, u32[]{:S(2)}) collective-permute-start(bf16[128,3584]{1,0:T(8,128)(2,1)S(1)} %pad_maximum_fusion.6), channel_id=1, source_target_pairs={{0,1},{1,0},{2,3},{3,2},{4,5},{5,4},{6,7},{7,6},{8,9},{9,8},{10,11... | collective-permute-start | bytes 2752520 | tf_op jit(solution)/shard_map/ppermute | solution.py:17
  122.3 6.9 %collective-permute-start.39 = (bf16[128,3584]{1,0:T(8,128)(2,1)S(1)}, bf16[128,3584]{1,0:T(8,128)(2,1)S(1)}, u32[]{:S(2)}, u32[]{:S(2)}) collective-permute-start(bf16[128,3584]{1,0:T(8,128)(2,1)S(1)} %pick_blocks.1), channel_id=1, source_target_pairs={{0,1},{1,0},{2,3},{3,2},{4,5},{5,4},{6,7},{7,6},{8,9},{9,8},{10,11... | collective-permute-start | bytes 2752520 | tf_op jit(solution)/shard_map/ppermute | solution.py:17
  123.3 12.6 %collective-permute-start.30 = (bf16[2,32,3584]{2,1,0:T(8,128)(2,1)S(1)}, bf16[2,32,3584]{2,1,0:T(8,128)(2,1)S(1)}, u32[]{:S(2)}, u32[]{:S(2)}) collective-permute-start(bf16[2,32,3584]{2,1,0:T(8,128)(2,1)S(1)} %pad_maximum_fusion.12), channel_id=1, source_target_pairs={{0,4},{1,5},{2,6},{3,7},{4,0},{5,1},{6,2},{7,3},{8,12},{9,13},{10,... | collective-permute-start | bytes 1376264 | tf_op jit(solution)/shard_map/ppermute | solution.py:17
  124.7 12.9 %collective-permute-start.27 = (bf16[2,32,3584]{2,1,0:T(8,128)(2,1)S(1)}, bf16[2,32,3584]{2,1,0:T(8,128)(2,1)S(1)}, u32[]{:S(2)}, u32[]{:S(2)}) collective-permute-start(bf16[2,32,3584]{2,1,0:T(8,128)(2,1)S(1)} %pad_maximum_fusion.11), channel_id=1, source_target_pairs={{0,2},{1,3},{2,0},{3,1},{4,6},{5,7},{6,4},{7,5},{8,10},{9,11},{10,... | collective-permute-start | bytes 1376264 | tf_op jit(solution)/shard_map/ppermute | solution.py:17
  136.1 6.9 %collective-permute-start.31 = (bf16[1,32,3584]{2,1,0:T(8,128)(2,1)S(1)}, bf16[1,32,3584]{2,1,0:T(8,128)(2,1)S(1)}, u32[]{:S(2)}, u32[]{:S(2)}) collective-permute-start(bf16[1,32,3584]{2,1,0:T(8,128)(2,1)S(1)} %slice.551), channel_id=1, source_target_pairs={{0,2},{1,3},{2,0},{3,1},{4,6},{5,7},{6,4},{7,5},{8,10},{9,11},{10,... | collective-permute-start | bytes 688136 | tf_op jit(solution)/shard_map/ppermute | solution.py:17
  137.7 7.1 %collective-permute-start.28 = (bf16[1,32,3584]{2,1,0:T(8,128)(2,1)S(1)}, bf16[1,32,3584]{2,1,0:T(8,128)(2,1)S(1)}, u32[]{:S(2)}, u32[]{:S(2)}) collective-permute-start(bf16[1,32,3584]{2,1,0:T(8,128)(2,1)S(1)} %slice.552), channel_id=1, source_target_pairs={{0,4},{1,5},{2,6},{3,7},{4,0},{5,1},{6,2},{7,3},{8,12},{9,13},{10,... | collective-permute-start | bytes 688136 | tf_op jit(solution)/shard_map/ppermute | solution.py:17
  139.7 7.3 %collective-permute-start.46 = (bf16[128,3584]{1,0:T(8,128)(2,1)S(1)}, bf16[128,3584]{1,0:T(8,128)(2,1)S(1)}, u32[]{:S(2)}, u32[]{:S(2)}) collective-permute-start(bf16[128,3584]{1,0:T(8,128)(2,1)S(1)} %slice.545), channel_id=1, source_target_pairs={{0,1},{1,0},{2,3},{3,2},{4,5},{5,4},{6,7},{7,6},{8,9},{9,8},{10,11... | collective-permute-start | bytes 2752520 | tf_op jit(solution)/shard_map/ppermute | solution.py:17
  144.9 23.9 %collective-permute-start.32 = (bf16[16,7168]{1,0:T(8,128)(2,1)S(1)}, bf16[16,7168]{1,0:T(8,128)(2,1)S(1)}, u32[]{:S(2)}, u32[]{:S(2)}) collective-permute-start(bf16[16,7168]{1,0:T(8,128)(2,1)S(1)} %get-tuple-element.69), channel_id=1, source_target_pairs={{0,24},{8,16},{16,8},{24,0},{1,25},{9,17},{17,9},{25,1},{2,26},{10... | collective-permute-start | bytes 688136 | tf_op jit(solution)/shard_map/ppermute | solution.py:17
  147.0 21.8 %collective-permute-start.33 = (bf16[16,7168]{1,0:T(8,128)(2,1)S(1)}, bf16[16,7168]{1,0:T(8,128)(2,1)S(1)}, u32[]{:S(2)}, u32[]{:S(2)}) collective-permute-start(bf16[16,7168]{1,0:T(8,128)(2,1)S(1)} %get-tuple-element.70), channel_id=1, source_target_pairs={{0,16},{8,24},{16,0},{24,8},{1,17},{9,25},{17,1},{25,9},{2,18},{10... | collective-permute-start | bytes 688136 | tf_op jit(solution)/shard_map/ppermute | solution.py:17
  147.4 10.9 %collective-permute-start.47 = (bf16[2,32,3584]{2,1,0:T(8,128)(2,1)S(1)}, bf16[2,32,3584]{2,1,0:T(8,128)(2,1)S(1)}, u32[]{:S(2)}, u32[]{:S(2)}) collective-permute-start(bf16[2,32,3584]{2,1,0:T(8,128)(2,1)S(1)} %pad_maximum_fusion.16), channel_id=1, source_target_pairs={{0,4},{1,5},{2,6},{3,7},{4,0},{5,1},{6,2},{7,3},{8,12},{9,13},{10,... | collective-permute-start | bytes 1376264 | tf_op jit(solution)/shard_map/ppermute | solution.py:17
  148.1 11.3 %collective-permute-start.44 = (bf16[2,32,3584]{2,1,0:T(8,128)(2,1)S(1)}, bf16[2,32,3584]{2,1,0:T(8,128)(2,1)S(1)}, u32[]{:S(2)}, u32[]{:S(2)}) collective-permute-start(bf16[2,32,3584]{2,1,0:T(8,128)(2,1)S(1)} %pad_maximum_fusion.15), channel_id=1, source_target_pairs={{0,2},{1,3},{2,0},{3,1},{4,6},{5,7},{6,4},{7,5},{8,10},{9,11},{10,... | collective-permute-start | bytes 1376264 | tf_op jit(solution)/shard_map/ppermute | solution.py:17
  159.5 6.8 %collective-permute-start.45 = (bf16[1,32,3584]{2,1,0:T(8,128)(2,1)S(1)}, bf16[1,32,3584]{2,1,0:T(8,128)(2,1)S(1)}, u32[]{:S(2)}, u32[]{:S(2)}) collective-permute-start(bf16[1,32,3584]{2,1,0:T(8,128)(2,1)S(1)} %slice.550), channel_id=1, source_target_pairs={{0,4},{1,5},{2,6},{3,7},{4,0},{5,1},{6,2},{7,3},{8,12},{9,13},{10,... | collective-permute-start | bytes 688136 | tf_op jit(solution)/shard_map/ppermute | solution.py:17
  (42 other events, 290.3 us)

commit v5 on v4

--- a/solution.py
+++ b/solution.py
@@ -580,8 +580,6 @@
 
         gate_val, up_val = project(gate_here), project(up_here)
         active = (jax.nn.silu(gate_val) * up_val).astype(jnp.bfloat16)
-        if before_down:
-            active = collect([active], before_down)
         reqs = range(c * in_chunk, (c + 1) * in_chunk)
         row_weight = weight_all[:, reqs[0] : reqs[-1] + 1].reshape(-1, 1)
         outs = []

time: 174 us -> 174 us (level)
  no operation moved by 1% of the time
where the time goes in v5:
time: 174 us
  waiting for transfers between devices  80.2 us (46%)
  starting transfers between devices  54.6 us (31%)
  Pallas kernels  14.1 us (8%)
  matrix products  13.7 us (8%)
  local copies, waits for them, and re-layouts  5.84 us (3%)
  other arithmetic  4.13 us (2%)
    ppermute x50, waiting for transfers between devices, swap(): return lax.ppermute(x, axis, [(i, i ^ distance) for i in range(size)])  80.2 us
    ppermute x50, starting transfers between devices, swap(): return lax.ppermute(x, axis, [(i, i ^ distance) for i in range(size)])  54.6 us
    dot_general x4, matrix products, project(): jnp.dot(left, matrix[:half_width], preferred_element_type=jnp.float32)  4.73 us
    dot_general x4, matrix products, products(): jnp.dot(active, down_here[:, cols], preferred_element_type=jnp.float32)  4.53 us
    dot_general x4, matrix products, project(): jnp.dot(right, matrix[half_width:], preferred_element_type=jnp.float32)  4.41 us
  transfers between devices with their start and end apart: 50, of which 31 were waited for; matrix products, arithmetic and copies ran while one was open for 12% of the time, Pallas kernels for 3%

profile of v5, /device:TPU:0, one launch (start us, length us, event | category | flops | bytes accessed | tf_op | source)
XLA Modules:
  0.0 173.6 jit_solution(7062665911108902954)
XLA Ops:
  0.7 2.6 %pick_far.1 = (bf16[16,2304]{1,0:T(8,128)(2,1)}, bf16[16,2304]{1,0:T(8,128)(2,1)}, bf16[16,2304]{1,0:T(8,128)(2,1)}) custom-call(s32[2]{0:T(128)} %pad_add_fusion.1.place, s32[8,16]{1,0:T(8,128)} %lists.3, bf16[32,36864]{1,0:T(8,128)(2,1)} %pool.3), custom_call_target="tpu_custom_call" | custom-call | tf_op jit(solution)/shard_map/pick_far/pallas_call | solution.py:288
  3.3 3.1 %collective-permute-start = (bf16[16,2304]{1,0:T(8,128)(2,1)}, bf16[16,2304]{1,0:T(8,128)(2,1)S(1)}, u32[]{:S(2)}, u32[]{:S(2)}) collective-permute-start(bf16[16,2304]{1,0:T(8,128)(2,1)} %get-tuple-element.25), channel_id=1, source_target_pairs={{0,8},{8,0},{16,24},{24,16},{1,9},{9,1},{17,25},{25,17},{2,10},{10... | collective-permute-start | bytes 221192 | tf_op jit(solution)/shard_map/ppermute | solution.py:17
  6.4 2.6 %collective-permute-start.1 = (bf16[16,2304]{1,0:T(8,128)(2,1)}, bf16[16,2304]{1,0:T(8,128)(2,1)S(1)}, u32[]{:S(2)}, u32[]{:S(2)}) collective-permute-start(bf16[16,2304]{1,0:T(8,128)(2,1)} %get-tuple-element.26), channel_id=1, source_target_pairs={{0,16},{8,24},{16,0},{24,8},{1,17},{9,25},{17,1},{25,9},{2,18},{10... | collective-permute-start | bytes 221192 | tf_op jit(solution)/shard_map/ppermute | solution.py:17
  9.7 3.0 %pick_near.1.near = bf16[16,18432]{1,0:T(8,128)(2,1)} custom-call(s32[2]{0:T(128)} %pad_add_fusion.1.place, s32[8,16]{1,0:T(8,128)} %lists.3, bf16[32,36864]{1,0:T(8,128)(2,1)} %pool.3), custom_call_target="tpu_custom_call" | custom-call | tf_op jit(solution)/shard_map/pick_near/pallas_call | solution.py:299
  15.5 2.4 %collective-permute-start.5 = (bf16[48,2304]{1,0:T(8,128)(2,1)S(1)}, bf16[48,2304]{1,0:T(8,128)(2,1)S(1)}, u32[]{:S(2)}, u32[]{:S(2)}) collective-permute-start(bf16[48,2304]{1,0:T(8,128)(2,1)S(1)} %constant_dynamic-update-slice_fusion), channel_id=1, source_target_pairs={{0,6},{1,7},{2,4},{3,5},{4,2},{5,3},{6,0},{7,1},{8,14},{9,15},{10,... | collective-permute-start | bytes 663560 | tf_op jit(solution)/shard_map/ppermute | solution.py:17
  19.0 5.7 %collective-permute-done.5 = bf16[48,2304]{1,0:T(8,128)(2,1)S(1)} collective-permute-done((bf16[48,2304]{1,0:T(8,128)(2,1)S(1)}, bf16[48,2304]{1,0:T(8,128)(2,1)S(1)}, u32[]{:S(2)}, u32[]{:S(2)}) %collective-permute-start.5) | collective-permute-done | bytes 221216 | tf_op jit(solution)/shard_map/ppermute | solution.py:17
  24.6 2.3 %collective-permute-done.4 = bf16[48,2304]{1,0:T(8,128)(2,1)S(1)} collective-permute-done((bf16[48,2304]{1,0:T(8,128)(2,1)S(1)}, bf16[48,2304]{1,0:T(8,128)(2,1)S(1)}, u32[]{:S(2)}, u32[]{:S(2)}) %collective-permute-start.4) | collective-permute-done | bytes 221216 | tf_op jit(solution)/shard_map/ppermute | solution.py:17
  27.4 2.3 %collective-permute-done.6 = bf16[4,48,2304]{2,1,0:T(8,128)(2,1)S(1)} collective-permute-done((bf16[4,48,2304]{2,1,0:T(8,128)(2,1)S(1)}, bf16[4,48,2304]{2,1,0:T(8,128)(2,1)S(1)}, u32[]{:S(2)}, u32[]{:S(2)}) %collective-permute-start.6) | collective-permute-done | bytes 884768 | tf_op jit(solution)/shard_map/ppermute | solution.py:17
  29.9 3.2 %attention.1.refs_0_ = bf16[144,256]{1,0:T(8,128)(2,1)S(1)} custom-call(s32[2]{0:T(128)S(1)} %copy-done.5, bf16[16,18432]{1,0:T(8,128)(2,1)S(1)} %copy-done, bf16[8,48,2304]{2,1,0:T(8,128)(2,1)S(1)} %constant_dynamic-update-slice_fusion.3.far, bf16[128,640]{1,0:T(8,128)(2,1)S(1)} %pad.16.new, bf16[256,640]{1,0:T(8,128)(2,1)S(1)} %get-tuple-element.78.q_even, ...), custom_call_target="tpu_custom_call" | custom-call | tf_op jit(solution)/shard_map/attention/pallas_call | solution.py:361
  33.1 3.6 %collective-permute-start.9 = (bf16[144,256]{1,0:T(8,128)(2,1)S(1)}, bf16[144,256]{1,0:T(8,128)(2,1)S(1)}, u32[]{:S(2)}, u32[]{:S(2)}) collective-permute-start(bf16[144,256]{1,0:T(8,128)(2,1)S(1)} %attention.1.refs_0_), channel_id=1, source_target_pairs={{0,24},{8,16},{16,8},{24,0},{1,25},{9,17},{17,9},{25,1},{2,26},{10... | collective-permute-start | bytes 221192 | tf_op jit(solution)/shard_map/ppermute | solution.py:17
  37.6 2.4 %collective-permute-done.9.refs_3_ = bf16[144,256]{1,0:T(8,128)(2,1)S(1)} collective-permute-done((bf16[144,256]{1,0:T(8,128)(2,1)S(1)}, bf16[144,256]{1,0:T(8,128)(2,1)S(1)}, u32[]{:S(2)}, u32[]{:S(2)}) %collective-permute-start.9) | collective-permute-done | bytes 73760 | tf_op jit(solution)/shard_map/ppermute | solution.py:17
  40.0 2.7 %collective-permute-done.8.refs_2_ = bf16[144,256]{1,0:T(8,128)(2,1)S(1)} collective-permute-done((bf16[144,256]{1,0:T(8,128)(2,1)S(1)}, bf16[144,256]{1,0:T(8,128)(2,1)S(1)}, u32[]{:S(2)}, u32[]{:S(2)}) %collective-permute-start.8) | collective-permute-done | bytes 73760 | tf_op jit(solution)/shard_map/ppermute | solution.py:17
  42.7 2.0 %project.1 = (f32[256,1792]{1,0:T(8,128)S(1)}, bf16[256,1792]{1,0:T(8,128)(2,1)}) custom-call(bf16[144,256]{1,0:T(8,128)(2,1)S(1)} %attention.1.refs_0_, bf16[144,256]{1,0:T(8,128)(2,1)S(1)} %collective-permute-done.7.refs_1_, bf16[144,256]{1,0:T(8,128)(2,1)S(1)} %collective-permute-done.8.refs_2_, bf16[144,256]{1,0:T(8,128)(2,1)S(1)} %collective-permute-done.9.refs_3_, ...), custom_call_target="tpu_custom_call" | custom-call | tf_op jit(solution)/shard_map/project/pallas_call | solution.py:412
  45.3 2.2 %collective-permute-done.10.got = bf16[256,1792]{1,0:T(8,128)(2,1)S(1)} collective-permute-done((bf16[256,1792]{1,0:T(8,128)(2,1)}, bf16[256,1792]{1,0:T(8,128)(2,1)S(1)}, u32[]{:S(2)}, u32[]{:S(2)}) %collective-permute-start.10) | collective-permute-done | bytes 917536 | tf_op jit(solution)/shard_map/ppermute | solution.py:17
  56.2 3.4 %collective-permute-done.15.refs_5_ = bf16[16,1792]{1,0:T(8,128)(2,1)S(1)} collective-permute-done((bf16[16,1792]{1,0:T(8,128)(2,1)S(1)}, bf16[16,1792]{1,0:T(8,128)(2,1)S(1)}, u32[]{:S(2)}, u32[]{:S(2)}) %collective-permute-start.15) | collective-permute-done | bytes 57376 | tf_op jit(solution)/shard_map/ppermute | solution.py:17
  61.0 2.2 %collective-permute-done.12.refs_1_ = bf16[64,1792]{1,0:T(8,128)(2,1)S(1)} collective-permute-done((bf16[64,1792]{1,0:T(8,128)(2,1)S(1)}, bf16[64,1792]{1,0:T(8,128)(2,1)S(1)}, u32[]{:S(2)}, u32[]{:S(2)}) %collective-permute-start.12) | collective-permute-done | bytes 229408 | tf_op jit(solution)/shard_map/ppermute | solution.py:17
  65.5 2.4 %collective-permute-start.17 = (bf16[32,1792]{1,0:T(8,128)(2,1)S(1)}, bf16[32,1792]{1,0:T(8,128)(2,1)S(1)}, u32[]{:S(2)}, u32[]{:S(2)}) collective-permute-start(bf16[32,1792]{1,0:T(8,128)(2,1)S(1)} %get-tuple-element.38.refs_0_), channel_id=1, source_target_pairs={{0,8},{8,0},{16,24},{24,16},{1,9},{9,1},{17,25},{25,17},{2,10},{10... | collective-permute-start | bytes 344072 | tf_op jit(solution)/shard_map/ppermute | solution.py:17
  68.0 4.1 %collective-permute-done.17.refs_1_ = bf16[32,1792]{1,0:T(8,128)(2,1)S(1)} collective-permute-done((bf16[32,1792]{1,0:T(8,128)(2,1)S(1)}, bf16[32,1792]{1,0:T(8,128)(2,1)S(1)}, u32[]{:S(2)}, u32[]{:S(2)}) %collective-permute-start.17) | collective-permute-done | bytes 114720 | tf_op jit(solution)/shard_map/ppermute | solution.py:17
  72.2 3.0 %collective-permute-done.18.refs_2_ = bf16[32,1792]{1,0:T(8,128)(2,1)S(1)} collective-permute-done((bf16[32,1792]{1,0:T(8,128)(2,1)S(1)}, bf16[32,1792]{1,0:T(8,128)(2,1)S(1)}, u32[]{:S(2)}, u32[]{:S(2)}) %collective-permute-start.18) | collective-permute-done | bytes 114720 | tf_op jit(solution)/shard_map/ppermute | solution.py:17
  75.1 2.1 %collective-permute-start.36 = (bf16[32,1792]{1,0:T(8,128)(2,1)S(1)}, bf16[32,1792]{1,0:T(8,128)(2,1)S(1)}, u32[]{:S(2)}, u32[]{:S(2)}) collective-permute-start(bf16[32,1792]{1,0:T(8,128)(2,1)S(1)} %collect.4), channel_id=1, source_target_pairs={{0,24},{8,16},{16,8},{24,0},{1,25},{9,17},{17,9},{25,1},{2,26},{10... | collective-permute-start | bytes 344072 | tf_op jit(solution)/shard_map/ppermute | solution.py:17
  77.3 2.4 %collective-permute-start.34 = (bf16[32,1792]{1,0:T(8,128)(2,1)S(1)}, bf16[32,1792]{1,0:T(8,128)(2,1)S(1)}, u32[]{:S(2)}, u32[]{:S(2)}) collective-permute-start(bf16[32,1792]{1,0:T(8,128)(2,1)S(1)} %collect.3), channel_id=1, source_target_pairs={{0,8},{8,0},{16,24},{24,16},{1,9},{9,1},{17,25},{25,17},{2,10},{10... | collective-permute-start | bytes 344072 | tf_op jit(solution)/shard_map/ppermute | solution.py:17
  84.0 2.2 %collective-permute-done.35.refs_2_ = bf16[32,1792]{1,0:T(8,128)(2,1)S(1)} collective-permute-done((bf16[32,1792]{1,0:T(8,128)(2,1)S(1)}, bf16[32,1792]{1,0:T(8,128)(2,1)S(1)}, u32[]{:S(2)}, u32[]{:S(2)}) %collective-permute-start.35) | collective-permute-done | bytes 114720 | tf_op jit(solution)/shard_map/ppermute | solution.py:17
  92.9 5.7 %collective-permute-done.40 = bf16[1,32,3584]{2,1,0:T(8,128)(2,1)S(1)} collective-permute-done((bf16[1,32,3584]{2,1,0:T(8,128)(2,1)S(1)}, bf16[1,32,3584]{2,1,0:T(8,128)(2,1)S(1)}, u32[]{:S(2)}, u32[]{:S(2)}) %collective-permute-start.40) | collective-permute-done | bytes 229408 | tf_op jit(solution)/shard_map/ppermute | solution.py:17
  100.9 7.6 %collective-permute-done.21 = bf16[2,32,3584]{2,1,0:T(8,128)(2,1)S(1)} collective-permute-done((bf16[2,32,3584]{2,1,0:T(8,128)(2,1)S(1)}, bf16[2,32,3584]{2,1,0:T(8,128)(2,1)S(1)}, u32[]{:S(2)}, u32[]{:S(2)}) %collective-permute-start.21) | collective-permute-done | bytes 458784 | tf_op jit(solution)/shard_map/ppermute | solution.py:17
  109.5 3.0 %collective-permute-done.25 = bf16[128,3584]{1,0:T(8,128)(2,1)S(1)} collective-permute-done((bf16[128,3584]{1,0:T(8,128)(2,1)S(1)}, bf16[128,3584]{1,0:T(8,128)(2,1)S(1)}, u32[]{:S(2)}, u32[]{:S(2)}) %collective-permute-start.25) | collective-permute-done | bytes 917536 | tf_op jit(solution)/shard_map/ppermute | solution.py:17
  138.4 4.5 %collective-permute-done.31 = bf16[1,32,3584]{2,1,0:T(8,128)(2,1)S(1)} collective-permute-done((bf16[1,32,3584]{2,1,0:T(8,128)(2,1)S(1)}, bf16[1,32,3584]{2,1,0:T(8,128)(2,1)S(1)}, u32[]{:S(2)}, u32[]{:S(2)}) %collective-permute-start.31) | collective-permute-done | bytes 229408 | tf_op jit(solution)/shard_map/ppermute | solution.py:17
  144.9 2.1 %collective-permute-start.32 = (bf16[16,7168]{1,0:T(8,128)(2,1)S(1)}, bf16[16,7168]{1,0:T(8,128)(2,1)S(1)}, u32[]{:S(2)}, u32[]{:S(2)}) collective-permute-start(bf16[16,7168]{1,0:T(8,128)(2,1)S(1)} %get-tuple-element.69), channel_id=1, source_target_pairs={{0,24},{8,16},{16,8},{24,0},{1,25},{9,17},{17,9},{25,1},{2,26},{10... | collective-permute-start | bytes 688136 | tf_op jit(solution)/shard_map/ppermute | solution.py:17
  149.9 8.3 %collective-permute-done.47 = bf16[2,32,3584]{2,1,0:T(8,128)(2,1)S(1)} collective-permute-done((bf16[2,32,3584]{2,1,0:T(8,128)(2,1)S(1)}, bf16[2,32,3584]{2,1,0:T(8,128)(2,1)S(1)}, u32[]{:S(2)}, u32[]{:S(2)}) %collective-permute-start.47) | collective-permute-done | bytes 458784 | tf_op jit(solution)/shard_map/ppermute | solution.py:17
  159.5 2.8 %collective-permute-start.45 = (bf16[1,32,3584]{2,1,0:T(8,128)(2,1)S(1)}, bf16[1,32,3584]{2,1,0:T(8,128)(2,1)S(1)}, u32[]{:S(2)}, u32[]{:S(2)}) collective-permute-start(bf16[1,32,3584]{2,1,0:T(8,128)(2,1)S(1)} %slice.550), channel_id=1, source_target_pairs={{0,4},{1,5},{2,6},{3,7},{4,0},{5,1},{6,2},{7,3},{8,12},{9,13},{10,... | collective-permute-start | bytes 688136 | tf_op jit(solution)/shard_map/ppermute | solution.py:17
  162.3 2.1 %collective-permute-done.48 = bf16[1,32,3584]{2,1,0:T(8,128)(2,1)S(1)} collective-permute-done((bf16[1,32,3584]{2,1,0:T(8,128)(2,1)S(1)}, bf16[1,32,3584]{2,1,0:T(8,128)(2,1)S(1)}, u32[]{:S(2)}, u32[]{:S(2)}) %collective-permute-start.48) | collective-permute-done | bytes 229408 | tf_op jit(solution)/shard_map/ppermute | solution.py:17
  166.4 2.4 %collective-permute-start.49 = (bf16[16,7168]{1,0:T(8,128)(2,1)S(1)}, bf16[16,7168]{1,0:T(8,128)(2,1)S(1)}, u32[]{:S(2)}, u32[]{:S(2)}) collective-permute-start(bf16[16,7168]{1,0:T(8,128)(2,1)S(1)} %fusion.44), channel_id=1, source_target_pairs={{0,8},{8,0},{16,24},{24,16},{1,9},{9,1},{17,25},{25,17},{2,10},{10... | collective-permute-start | bytes 688136 | tf_op jit(solution)/shard_map/ppermute | solution.py:17
  168.8 4.0 %collective-permute-done.49 = bf16[16,7168]{1,0:T(8,128)(2,1)S(1)} collective-permute-done((bf16[16,7168]{1,0:T(8,128)(2,1)S(1)}, bf16[16,7168]{1,0:T(8,128)(2,1)S(1)}, u32[]{:S(2)}, u32[]{:S(2)}) %collective-permute-start.49) | collective-permute-done | bytes 229408 | tf_op jit(solution)/shard_map/ppermute | solution.py:17
  (262 shorter events, 67.9 us)
Async XLA Ops:
  3.3 11.3 %collective-permute-start = (bf16[16,2304]{1,0:T(8,128)(2,1)}, bf16[16,2304]{1,0:T(8,128)(2,1)S(1)}, u32[]{:S(2)}, u32[]{:S(2)}) collective-permute-start(bf16[16,2304]{1,0:T(8,128)(2,1)} %get-tuple-element.25), channel_id=1, source_target_pairs={{0,8},{8,0},{16,24},{24,16},{1,9},{9,1},{17,25},{25,17},{2,10},{10... | collective-permute-start | bytes 221192 | tf_op jit(solution)/shard_map/ppermute | solution.py:17
  6.4 8.2 %collective-permute-start.1 = (bf16[16,2304]{1,0:T(8,128)(2,1)}, bf16[16,2304]{1,0:T(8,128)(2,1)S(1)}, u32[]{:S(2)}, u32[]{:S(2)}) collective-permute-start(bf16[16,2304]{1,0:T(8,128)(2,1)} %get-tuple-element.26), channel_id=1, source_target_pairs={{0,16},{8,24},{16,0},{24,8},{1,17},{9,25},{17,1},{25,9},{2,18},{10... | collective-permute-start | bytes 221192 | tf_op jit(solution)/shard_map/ppermute | solution.py:17
  15.5 9.2 %collective-permute-start.5 = (bf16[48,2304]{1,0:T(8,128)(2,1)S(1)}, bf16[48,2304]{1,0:T(8,128)(2,1)S(1)}, u32[]{:S(2)}, u32[]{:S(2)}) collective-permute-start(bf16[48,2304]{1,0:T(8,128)(2,1)S(1)} %constant_dynamic-update-slice_fusion), channel_id=1, source_target_pairs={{0,6},{1,7},{2,4},{3,5},{4,2},{5,3},{6,0},{7,1},{8,14},{9,15},{10,... | collective-permute-start | bytes 663560 | tf_op jit(solution)/shard_map/ppermute | solution.py:17
  17.9 9.1 %collective-permute-start.4 = (bf16[48,2304]{1,0:T(8,128)(2,1)S(1)}, bf16[48,2304]{1,0:T(8,128)(2,1)S(1)}, u32[]{:S(2)}, u32[]{:S(2)}) collective-permute-start(bf16[48,2304]{1,0:T(8,128)(2,1)S(1)} %constant_dynamic-update-slice_fusion), channel_id=1, source_target_pairs={{0,4},{1,5},{2,6},{3,7},{4,0},{5,1},{6,2},{7,3},{8,12},{9,13},{10,... | collective-permute-start | bytes 663560 | tf_op jit(solution)/shard_map/ppermute | solution.py:17
  18.4 8.7 %collective-permute-start.3 = (bf16[48,2304]{1,0:T(8,128)(2,1)S(1)}, bf16[48,2304]{1,0:T(8,128)(2,1)S(1)}, u32[]{:S(2)}, u32[]{:S(2)}) collective-permute-start(bf16[48,2304]{1,0:T(8,128)(2,1)S(1)} %constant_dynamic-update-slice_fusion), channel_id=1, source_target_pairs={{0,2},{1,3},{2,0},{3,1},{4,6},{5,7},{6,4},{7,5},{8,10},{9,11},{10,... | collective-permute-start | bytes 663560 | tf_op jit(solution)/shard_map/ppermute | solution.py:17
  33.1 6.9 %collective-permute-start.9 = (bf16[144,256]{1,0:T(8,128)(2,1)S(1)}, bf16[144,256]{1,0:T(8,128)(2,1)S(1)}, u32[]{:S(2)}, u32[]{:S(2)}) collective-permute-start(bf16[144,256]{1,0:T(8,128)(2,1)S(1)} %attention.1.refs_0_), channel_id=1, source_target_pairs={{0,24},{8,16},{16,8},{24,0},{1,25},{9,17},{17,9},{25,1},{2,26},{10... | collective-permute-start | bytes 221192 | tf_op jit(solution)/shard_map/ppermute | solution.py:17
  48.2 6.8 %collective-permute-start.14 = (bf16[16,1792]{1,0:T(8,128)(2,1)S(1)}, bf16[16,1792]{1,0:T(8,128)(2,1)S(1)}, u32[]{:S(2)}, u32[]{:S(2)}) collective-permute-start(bf16[16,1792]{1,0:T(8,128)(2,1)S(1)} %get-tuple-element.35), channel_id=1, source_target_pairs={{0,8},{8,0},{16,24},{24,16},{1,9},{9,1},{17,25},{25,17},{2,10},{10... | collective-permute-start | bytes 172040 | tf_op jit(solution)/shard_map/ppermute | solution.py:17
  49.7 11.3 %collective-permute-start.11 = (bf16[64,1792]{1,0:T(8,128)(2,1)S(1)}, bf16[64,1792]{1,0:T(8,128)(2,1)S(1)}, u32[]{:S(2)}, u32[]{:S(2)}) collective-permute-start(bf16[64,1792]{1,0:T(8,128)(2,1)S(1)} %get-tuple-element.31), channel_id=1, source_target_pairs={{0,2},{1,3},{2,0},{3,1},{4,6},{5,7},{6,4},{7,5},{8,10},{9,11},{10,... | collective-permute-start | bytes 688136 | tf_op jit(solution)/shard_map/ppermute | solution.py:17
  51.2 12.0 %collective-permute-start.12 = (bf16[64,1792]{1,0:T(8,128)(2,1)S(1)}, bf16[64,1792]{1,0:T(8,128)(2,1)S(1)}, u32[]{:S(2)}, u32[]{:S(2)}) collective-permute-start(bf16[64,1792]{1,0:T(8,128)(2,1)S(1)} %get-tuple-element.32), channel_id=1, source_target_pairs={{0,4},{1,5},{2,6},{3,7},{4,0},{5,1},{6,2},{7,3},{8,12},{9,13},{10,... | collective-permute-start | bytes 688136 | tf_op jit(solution)/shard_map/ppermute | solution.py:17
  52.0 11.3 %collective-permute-start.13 = (bf16[64,1792]{1,0:T(8,128)(2,1)S(1)}, bf16[64,1792]{1,0:T(8,128)(2,1)S(1)}, u32[]{:S(2)}, u32[]{:S(2)}) collective-permute-start(bf16[64,1792]{1,0:T(8,128)(2,1)S(1)} %get-tuple-element.33), channel_id=1, source_target_pairs={{0,6},{1,7},{2,4},{3,5},{4,2},{5,3},{6,0},{7,1},{8,14},{9,15},{10,... | collective-permute-start | bytes 688136 | tf_op jit(solution)/shard_map/ppermute | solution.py:17
  63.4 8.8 %collective-permute-start.19 = (bf16[32,1792]{1,0:T(8,128)(2,1)S(1)}, bf16[32,1792]{1,0:T(8,128)(2,1)S(1)}, u32[]{:S(2)}, u32[]{:S(2)}) collective-permute-start(bf16[32,1792]{1,0:T(8,128)(2,1)S(1)} %get-tuple-element.39.refs_0_), channel_id=1, source_target_pairs={{0,24},{8,16},{16,8},{24,0},{1,25},{9,17},{17,9},{25,1},{2,26},{10... | collective-permute-start | bytes 344072 | tf_op jit(solution)/shard_map/ppermute | solution.py:17
  65.0 10.1 %collective-permute-start.18 = (bf16[32,1792]{1,0:T(8,128)(2,1)S(1)}, bf16[32,1792]{1,0:T(8,128)(2,1)S(1)}, u32[]{:S(2)}, u32[]{:S(2)}) collective-permute-start(bf16[32,1792]{1,0:T(8,128)(2,1)S(1)} %get-tuple-element.39.refs_0_), channel_id=1, source_target_pairs={{0,16},{8,24},{16,0},{24,8},{1,17},{9,25},{17,1},{25,9},{2,18},{10... | collective-permute-start | bytes 344072 | tf_op jit(solution)/shard_map/ppermute | solution.py:17
  75.1 8.8 %collective-permute-start.36 = (bf16[32,1792]{1,0:T(8,128)(2,1)S(1)}, bf16[32,1792]{1,0:T(8,128)(2,1)S(1)}, u32[]{:S(2)}, u32[]{:S(2)}) collective-permute-start(bf16[32,1792]{1,0:T(8,128)(2,1)S(1)} %collect.4), channel_id=1, source_target_pairs={{0,24},{8,16},{16,8},{24,0},{1,25},{9,17},{17,9},{25,1},{2,26},{10... | collective-permute-start | bytes 344072 | tf_op jit(solution)/shard_map/ppermute | solution.py:17
  77.3 8.9 %collective-permute-start.35 = (bf16[32,1792]{1,0:T(8,128)(2,1)S(1)}, bf16[32,1792]{1,0:T(8,128)(2,1)S(1)}, u32[]{:S(2)}, u32[]{:S(2)}) collective-permute-start(bf16[32,1792]{1,0:T(8,128)(2,1)S(1)} %collect.4), channel_id=1, source_target_pairs={{0,16},{8,24},{16,0},{24,8},{1,17},{9,25},{17,1},{25,9},{2,18},{10... | collective-permute-start | bytes 344072 | tf_op jit(solution)/shard_map/ppermute | solution.py:17
  88.6 10.8 %collective-permute-start.37 = (bf16[1,32,3584]{2,1,0:T(8,128)(2,1)S(1)}, bf16[1,32,3584]{2,1,0:T(8,128)(2,1)S(1)}, u32[]{:S(2)}, u32[]{:S(2)}) collective-permute-start(bf16[1,32,3584]{2,1,0:T(8,128)(2,1)S(1)} %bitcast.157), channel_id=1, source_target_pairs={{0,2},{1,3},{2,0},{3,1},{4,6},{5,7},{6,4},{7,5},{8,10},{9,11},{10,... | collective-permute-start | bytes 688136 | tf_op jit(solution)/shard_map/ppermute | solution.py:17
  90.1 8.5 %collective-permute-start.40 = (bf16[1,32,3584]{2,1,0:T(8,128)(2,1)S(1)}, bf16[1,32,3584]{2,1,0:T(8,128)(2,1)S(1)}, u32[]{:S(2)}, u32[]{:S(2)}) collective-permute-start(bf16[1,32,3584]{2,1,0:T(8,128)(2,1)S(1)} %bitcast.152), channel_id=1, source_target_pairs={{0,4},{1,5},{2,6},{3,7},{4,0},{5,1},{6,2},{7,3},{8,12},{9,13},{10,... | collective-permute-start | bytes 688136 | tf_op jit(solution)/shard_map/ppermute | solution.py:17
  90.9 17.8 %collective-permute-start.24 = (bf16[2,32,3584]{2,1,0:T(8,128)(2,1)S(1)}, bf16[2,32,3584]{2,1,0:T(8,128)(2,1)S(1)}, u32[]{:S(2)}, u32[]{:S(2)}) collective-permute-start(bf16[2,32,3584]{2,1,0:T(8,128)(2,1)S(1)} %pad_maximum_fusion.10), channel_id=1, source_target_pairs={{0,2},{1,3},{2,0},{3,1},{4,6},{5,7},{6,4},{7,5},{8,10},{9,11},{10,... | collective-permute-start | bytes 1376264 | tf_op jit(solution)/shard_map/ppermute | solution.py:17
  92.2 16.2 %collective-permute-start.21 = (bf16[2,32,3584]{2,1,0:T(8,128)(2,1)S(1)}, bf16[2,32,3584]{2,1,0:T(8,128)(2,1)S(1)}, u32[]{:S(2)}, u32[]{:S(2)}) collective-permute-start(bf16[2,32,3584]{2,1,0:T(8,128)(2,1)S(1)} %pad_maximum_fusion.9), channel_id=1, source_target_pairs={{0,4},{1,5},{2,6},{3,7},{4,0},{5,1},{6,2},{7,3},{8,12},{9,13},{10,... | collective-permute-start | bytes 1376264 | tf_op jit(solution)/shard_map/ppermute | solution.py:17
  98.7 21.8 %collective-permute-start.41 = (bf16[2,32,3584]{2,1,0:T(8,128)(2,1)S(1)}, bf16[2,32,3584]{2,1,0:T(8,128)(2,1)S(1)}, u32[]{:S(2)}, u32[]{:S(2)}) collective-permute-start(bf16[2,32,3584]{2,1,0:T(8,128)(2,1)S(1)} %pad_maximum_fusion.14), channel_id=1, source_target_pairs={{0,2},{1,3},{2,0},{3,1},{4,6},{5,7},{6,4},{7,5},{8,10},{9,11},{10,... | collective-permute-start | bytes 1376264 | tf_op jit(solution)/shard_map/ppermute | solution.py:17
  99.4 22.8 %collective-permute-start.38 = (bf16[2,32,3584]{2,1,0:T(8,128)(2,1)S(1)}, bf16[2,32,3584]{2,1,0:T(8,128)(2,1)S(1)}, u32[]{:S(2)}, u32[]{:S(2)}) collective-permute-start(bf16[2,32,3584]{2,1,0:T(8,128)(2,1)S(1)} %pad_maximum_fusion.13.refs_0_), channel_id=1, source_target_pairs={{0,4},{1,5},{2,6},{3,7},{4,0},{5,1},{6,2},{7,3},{8,12},{9,13},{10,... | collective-permute-start | bytes 1376264 | tf_op jit(solution)/shard_map/ppermute | solution.py:17
  108.6 6.9 %collective-permute-start.22 = (bf16[128,3584]{1,0:T(8,128)(2,1)S(1)}, bf16[128,3584]{1,0:T(8,128)(2,1)S(1)}, u32[]{:S(2)}, u32[]{:S(2)}) collective-permute-start(bf16[128,3584]{1,0:T(8,128)(2,1)S(1)} %pad_maximum_fusion.6), channel_id=1, source_target_pairs={{0,1},{1,0},{2,3},{3,2},{4,5},{5,4},{6,7},{7,6},{8,9},{9,8},{10,11... | collective-permute-start | bytes 2752520 | tf_op jit(solution)/shard_map/ppermute | solution.py:17
  122.3 6.9 %collective-permute-start.39 = (bf16[128,3584]{1,0:T(8,128)(2,1)S(1)}, bf16[128,3584]{1,0:T(8,128)(2,1)S(1)}, u32[]{:S(2)}, u32[]{:S(2)}) collective-permute-start(bf16[128,3584]{1,0:T(8,128)(2,1)S(1)} %pick_blocks.1), channel_id=1, source_target_pairs={{0,1},{1,0},{2,3},{3,2},{4,5},{5,4},{6,7},{7,6},{8,9},{9,8},{10,11... | collective-permute-start | bytes 2752520 | tf_op jit(solution)/shard_map/ppermute | solution.py:17
  123.3 12.6 %collective-permute-start.30 = (bf16[2,32,3584]{2,1,0:T(8,128)(2,1)S(1)}, bf16[2,32,3584]{2,1,0:T(8,128)(2,1)S(1)}, u32[]{:S(2)}, u32[]{:S(2)}) collective-permute-start(bf16[2,32,3584]{2,1,0:T(8,128)(2,1)S(1)} %pad_maximum_fusion.12), channel_id=1, source_target_pairs={{0,4},{1,5},{2,6},{3,7},{4,0},{5,1},{6,2},{7,3},{8,12},{9,13},{10,... | collective-permute-start | bytes 1376264 | tf_op jit(solution)/shard_map/ppermute | solution.py:17
  124.7 12.9 %collective-permute-start.27 = (bf16[2,32,3584]{2,1,0:T(8,128)(2,1)S(1)}, bf16[2,32,3584]{2,1,0:T(8,128)(2,1)S(1)}, u32[]{:S(2)}, u32[]{:S(2)}) collective-permute-start(bf16[2,32,3584]{2,1,0:T(8,128)(2,1)S(1)} %pad_maximum_fusion.11), channel_id=1, source_target_pairs={{0,2},{1,3},{2,0},{3,1},{4,6},{5,7},{6,4},{7,5},{8,10},{9,11},{10,... | collective-permute-start | bytes 1376264 | tf_op jit(solution)/shard_map/ppermute | solution.py:17
  133.0 14.0 %collective-permute-start.46 = (bf16[128,3584]{1,0:T(8,128)(2,1)S(1)}, bf16[128,3584]{1,0:T(8,128)(2,1)S(1)}, u32[]{:S(2)}, u32[]{:S(2)}) collective-permute-start(bf16[128,3584]{1,0:T(8,128)(2,1)S(1)} %slice.545), channel_id=1, source_target_pairs={{0,1},{1,0},{2,3},{3,2},{4,5},{5,4},{6,7},{7,6},{8,9},{9,8},{10,11... | collective-permute-start | bytes 2752520 | tf_op jit(solution)/shard_map/ppermute | solution.py:17
  134.6 13.1 %collective-permute-start.43 = (bf16[128,3584]{1,0:T(8,128)(2,1)S(1)}, bf16[128,3584]{1,0:T(8,128)(2,1)S(1)}, u32[]{:S(2)}, u32[]{:S(2)}) collective-permute-start(bf16[128,3584]{1,0:T(8,128)(2,1)S(1)} %slice.546), channel_id=1, source_target_pairs={{0,1},{1,0},{2,3},{3,2},{4,5},{5,4},{6,7},{7,6},{8,9},{9,8},{10,11... | collective-permute-start | bytes 2752520 | tf_op jit(solution)/shard_map/ppermute | solution.py:17
  136.1 6.9 %collective-permute-start.31 = (bf16[1,32,3584]{2,1,0:T(8,128)(2,1)S(1)}, bf16[1,32,3584]{2,1,0:T(8,128)(2,1)S(1)}, u32[]{:S(2)}, u32[]{:S(2)}) collective-permute-start(bf16[1,32,3584]{2,1,0:T(8,128)(2,1)S(1)} %slice.551), channel_id=1, source_target_pairs={{0,2},{1,3},{2,0},{3,1},{4,6},{5,7},{6,4},{7,5},{8,10},{9,11},{10,... | collective-permute-start | bytes 688136 | tf_op jit(solution)/shard_map/ppermute | solution.py:17
  137.6 7.1 %collective-permute-start.28 = (bf16[1,32,3584]{2,1,0:T(8,128)(2,1)S(1)}, bf16[1,32,3584]{2,1,0:T(8,128)(2,1)S(1)}, u32[]{:S(2)}, u32[]{:S(2)}) collective-permute-start(bf16[1,32,3584]{2,1,0:T(8,128)(2,1)S(1)} %slice.552), channel_id=1, source_target_pairs={{0,4},{1,5},{2,6},{3,7},{4,0},{5,1},{6,2},{7,3},{8,12},{9,13},{10,... | collective-permute-start | bytes 688136 | tf_op jit(solution)/shard_map/ppermute | solution.py:17
  144.9 23.9 %collective-permute-start.32 = (bf16[16,7168]{1,0:T(8,128)(2,1)S(1)}, bf16[16,7168]{1,0:T(8,128)(2,1)S(1)}, u32[]{:S(2)}, u32[]{:S(2)}) collective-permute-start(bf16[16,7168]{1,0:T(8,128)(2,1)S(1)} %get-tuple-element.69), channel_id=1, source_target_pairs={{0,24},{8,16},{16,8},{24,0},{1,25},{9,17},{17,9},{25,1},{2,26},{10... | collective-permute-start | bytes 688136 | tf_op jit(solution)/shard_map/ppermute | solution.py:17
  147.0 21.8 %collective-permute-start.33 = (bf16[16,7168]{1,0:T(8,128)(2,1)S(1)}, bf16[16,7168]{1,0:T(8,128)(2,1)S(1)}, u32[]{:S(2)}, u32[]{:S(2)}) collective-permute-start(bf16[16,7168]{1,0:T(8,128)(2,1)S(1)} %get-tuple-element.70), channel_id=1, source_target_pairs={{0,16},{8,24},{16,0},{24,8},{1,17},{9,25},{17,1},{25,9},{2,18},{10... | collective-permute-start | bytes 688136 | tf_op jit(solution)/shard_map/ppermute | solution.py:17
  147.3 10.9 %collective-permute-start.47 = (bf16[2,32,3584]{2,1,0:T(8,128)(2,1)S(1)}, bf16[2,32,3584]{2,1,0:T(8,128)(2,1)S(1)}, u32[]{:S(2)}, u32[]{:S(2)}) collective-permute-start(bf16[2,32,3584]{2,1,0:T(8,128)(2,1)S(1)} %pad_maximum_fusion.16), channel_id=1, source_target_pairs={{0,4},{1,5},{2,6},{3,7},{4,0},{5,1},{6,2},{7,3},{8,12},{9,13},{10,... | collective-permute-start | bytes 1376264 | tf_op jit(solution)/shard_map/ppermute | solution.py:17
  148.1 11.3 %collective-permute-start.44 = (bf16[2,32,3584]{2,1,0:T(8,128)(2,1)S(1)}, bf16[2,32,3584]{2,1,0:T(8,128)(2,1)S(1)}, u32[]{:S(2)}, u32[]{:S(2)}) collective-permute-start(bf16[2,32,3584]{2,1,0:T(8,128)(2,1)S(1)} %pad_maximum_fusion.15), channel_id=1, source_target_pairs={{0,2},{1,3},{2,0},{3,1},{4,6},{5,7},{6,4},{7,5},{8,10},{9,11},{10,... | collective-permute-start | bytes 1376264 | tf_op jit(solution)/shard_map/ppermute | solution.py:17
  (42 other events, 290.3 us)
